TPU v7x, 128 devices: a whole 4x4x4 slice. The times are simulated.
128 devices in a mesh: replica: 32 (over x, z, y_hi), fsdp: 4 (over y_lo, core).
Axes of the slice: x: 4, y: 4 (y_hi: 2, y_lo: 2; y = y_hi * 2 + y_lo), z: 4, core: 2. Of those that a mesh axis runs over, the one named last changes fastest.
Arguments:
- hidden_act: bfloat16 [131072, 512], P(('replica', 'fsdp')), may hold values from -6 to 6
- out_grad: bfloat16 [131072, 5120], P(('replica', 'fsdp')), may hold values from -6 to 6
- momentum: float32 [32, 512, 5120], P('replica', 'fsdp'), may hold values from -6 to 6
- coef_picks: int32 [32, 8, 80, 32], P('replica', 'fsdp'), may hold values from 0 to 63, as said below
- params: bfloat16 [512, 5120], P('fsdp'), may hold values from -6 to 6
Outputs:
- momentum_left: float32 [32, 512, 5120], P('replica', 'fsdp')
- update: float32 [512, 5120], P('fsdp')
- new_params: bfloat16 [512, 5120], replicated
Inputs may be any that keep to these rules, and one draw needn't show every extreme that they name: `coef_picks`: for every replica and span, the first 16 entries are distinct, and so are the last 16.
All inputs are finite; a program needn't handle non-finite values.
Results may differ from a plain program's by a relative error of at most 0.001.
Values may be sent and summed in bfloat16 or wider, within the bound.
No kernel may reach another device: no remote copies, remote signals or barrier semaphores. Data moves between devices by JAX's collectives and lax.ppermute only.
A program may use at most 256 MiB of HBM per device.

v0:
```python
import math

import jax
import jax.numpy as jnp
from jax import lax
from jax.sharding import PartitionSpec as P

KEEP = 16


momentum_decay = 0.9
step_size = 0.5


def cosine_table():
    freq_index = jnp.arange(64, dtype=jnp.float32)[:, None]
    place_index = jnp.arange(64, dtype=jnp.float32)[None, :]
    row_weight = jnp.where(freq_index == 0, math.sqrt(1.0 / 64), math.sqrt(2.0 / 64))
    return row_weight * jnp.cos(math.pi * (2.0 * place_index + 1.0) * freq_index / 128.0)


def select_hot(chosen):
    return (chosen[..., None] == jnp.arange(64, dtype=jnp.int32)).astype(jnp.float32)


def compress_spans(moment, chosen, table_dct):
    span_rows = moment.shape[0] // 64
    span_cols = moment.shape[1] // 64
    blocks = moment.reshape(span_rows, 64, span_cols, 64)
    row_hot = select_hot(chosen[..., :KEEP])
    col_hot = select_hot(chosen[..., KEEP:])
    row_basis = jnp.einsum("abuk,kj->abuj", row_hot, table_dct, precision=lax.Precision.HIGHEST)
    col_basis = jnp.einsum("abuk,kj->abuj", col_hot, table_dct, precision=lax.Precision.HIGHEST)
    coeffs = jnp.einsum(
        "abui,aibj,abvj->abuv", row_basis, blocks, col_basis, precision=lax.Precision.HIGHEST
    )
    removed = jnp.einsum(
        "abui,abuv,abvj->aibj", row_basis, coeffs, col_basis, precision=lax.Precision.HIGHEST
    )
    return (coeffs, removed.reshape(moment.shape), row_hot, col_hot)


def body(hidden_act, out_grad, momentum, coef_picks, params):
    group_size = lax.axis_size("fsdp")
    local_rows = params.shape[0]
    width = params.shape[1]
    grad_scale = 1.0 / math.sqrt(hidden_act.shape[0] * group_size)
    table_dct = cosine_table()
    gradient = (
        lax.psum_scatter(
            jnp.dot(hidden_act.T, out_grad, preferred_element_type=jnp.float32),
            "fsdp",
            scatter_dimension=0,
            tiled=True,
        )
        * grad_scale
    )
    moment_new = momentum_decay * momentum[0] + gradient
    coeffs, removed, row_hot, col_hot = compress_spans(moment_new, coef_picks[0], table_dct)
    momentum_left = (moment_new - removed)[None]
    values = lax.all_gather(coeffs[None], "replica", axis=0, tiled=True)
    chosen = lax.all_gather(coef_picks, "replica", axis=0, tiled=True)
    rows_hot = select_hot(chosen[..., :KEEP])
    cols_hot = select_hot(chosen[..., KEEP:])
    placed = jnp.einsum(
        "nabui,nabuv,nabvj->abij", rows_hot, values, cols_hot, precision=lax.Precision.HIGHEST
    )
    update = jnp.einsum(
        "pi,abpq,qj->aibj", table_dct, placed, table_dct, precision=lax.Precision.HIGHEST
    ).reshape(local_rows, width)
    shard_params = (params.astype(jnp.float32) - step_size * update).astype(jnp.bfloat16)
    new_params = lax.all_gather(shard_params, "fsdp", axis=0, tiled=True)
    return (momentum_left, update, new_params)


def solution(mesh):
    return jax.shard_map(
        body,
        mesh=mesh,
        in_specs=(
            P(("replica", "fsdp"), None),
            P(("replica", "fsdp"), None),
            P("replica", "fsdp", None),
            P("replica", "fsdp", None, None),
            P("fsdp", None),
        ),
        out_specs=(P("replica", "fsdp", None), P("fsdp", None), P()),
        check_vma=False,
    )
```

profile of v0, /device:TPU:1, one launch (start us, length us, event | category | flops | bytes accessed | tf_op | source)
XLA Modules:
  0.0 487.5 jit_solution(9749685729023967671)
XLA Ops:
  7.2 0.0 copy-start
  7.2 0.0 reduce-scatter.2.cloned.1.call-start
  7.2 1.2 copy-done
  8.4 12.2 %fusion.35 = f32[512,5120]{1,0:T(8,128)} fusion(bf16[1024,512]{1,0:T(8,128)(2,1)S(1)} %copy-done, bf16[1024,5120]{1,0:T(8,128)(2,1)} %param.6), kind=kOutput, calls=%fused_computation.47 | convolution fusion | flops 5368709120 | bytes 22020096 | tf_op jit(solution)/shard_map/dot_general | solution.py:51
  20.6 0.0 reduce-scatter.2.cloned.1.call-update
  20.6 0.6 all-gather.6.cloned.1.call-start
  21.2 0.1 copy-done.6
  21.4 0.8 fusion.9
  22.2 0.6 copy.20
  22.8 0.0 copy-start.2
  22.8 0.8 fusion.10
  23.6 1.6 copy.21
  25.2 95.1 %reduce-scatter.2.cloned.1.call-done = f32[128,5120]{1,0:T(8,128)} async-done(((f32[512,5120]{1,0:T(8,128)}), f32[128,5120]{1,0:T(8,128)}) %reduce-scatter.2.cloned.1.call-update) | async-done | bytes 2621456 | tf_op jit(solution)/shard_map/reduce_scatter | solution.py:50
  120.3 4.4 bitcast_add_fusion
  124.7 5.1 %reshape.37 = f32[2,64,80,64]{3,2,1,0:T(8,128)} reshape(f32[128,5120]{1,0:T(8,128)} %bitcast_add_fusion) | data formatting | bytes 5242880 | tf_op jit(solution)/shard_map/reshape | solution.py:29
  129.8 0.0 copy-done.2
  129.8 8.4 %fusion.6 = f32[2,80,64,16]{2,3,1,0:T(8,128)S(1)} fusion(f32[2,80,16,64]{3,2,1,0:T(8,128)S(1)} %copy.20, f32[2,64,80,64]{3,2,1,0:T(8,128)} %reshape.37), kind=kOutput, calls=%fused_computation.8 | convolution fusion | flops 125829120 | bytes 3932160 | tf_op jit(solution)/shard_map/abui,aibj,abvj->abuv/dot_general | solution.py:34
  138.2 0.0 copy-done.3
  138.2 2.2 fusion.36
  140.4 1.2 copy.26
  141.6 0.0 all-gather.6.cloned.1.call-update
  141.6 0.0 all-gather.4.cloned.1.call-start
  141.7 89.5 %all_gather.10 = s32[32,2,80,32]{2,3,1,0:T(8,128)S(1)} all-gather(s32[1,2,80,32]{2,3,1,0:T(8,128)S(1)} %copy-done.6), channel_id=1, replica_groups=mesh['replica'=32,'fsdp'=4] {'replica'}, dimensions={0}, use_global_device_ids=true | all-gather | bytes 675840 | tf_op jit(solution)/shard_map/all_gather | solution.py:62
  231.1 0.1 fusion.33
  231.3 2.3 copy.28
  233.5 2.6 copy.29
  236.2 19.2 %all-gather.6.cloned.1.call-done = f32[64,80,16,16]{1,3,2,0:T(8,128)} async-done(((f32[2,80,16,16]{1,3,2,0:T(8,128)}), f32[64,80,16,16]{1,3,2,0:T(8,128)}) %all-gather.6.cloned.1.call-update) | async-done | bytes 5242896 | tf_op jit(solution)/shard_map/all_gather | solution.py:61
  255.3 31.9 %copy.37 = f32[32,2,80,16,16]{3,4,1,2,0:T(8,128)} copy(f32[32,2,80,16,16]{2,4,3,1,0:T(8,128)} %bitcast.43) | data formatting | bytes 10485760 | tf_op jit(solution)/shard_map/all_gather | solution.py:61
  287.3 41.7 %fusion.1 = f32[32,2,80,16,64]{4,3,1,2,0:T(8,128)} fusion(f32[32,2,80,16,16]{3,4,1,2,0:T(8,128)} %copy.37, s32[32,2,80,16]{3,2,1,0:T(8,128)} %copy.28), kind=kOutput, calls=%fused_computation.3 | convolution fusion | flops 1011875840 | bytes 26542080 | tf_op jit(solution)/shard_map/nabui,nabuv,nabvj->abij/dot_general | solution.py:65
  329.0 0.0 copy-done.5
  329.0 55.9 %fusion.8 = f32[2,80,64,64]{2,3,0,1:T(8,128)S(1)} fusion(f32[32,2,80,16,64]{4,3,1,2,0:T(8,128)} %fusion.1, s32[32,2,80,16]{3,1,2,0:T(2,128)S(1)} %copy-done.5), kind=kOutput, calls=%fused_computation.14 | convolution fusion | flops 4031774720 | bytes 23920640 | tf_op jit(solution)/shard_map/nabui,nabuv,nabvj->abij/dot_general | solution.py:65
  384.9 6.3 %fusion.4 = f32[2,80,64,64]{3,2,1,0:T(8,128)} fusion(f32[2,80,64,64]{2,3,0,1:T(8,128)S(1)} %fusion.8, f32[64]{0:T(128)S(1)} %get-tuple-element.8, f32[64]{0:T(128)S(1)} %get-tuple-element.7), kind=kOutput, calls=%fused_computation.6 | convolution fusion | flops 503328768 | bytes 5243392 | tf_op jit(solution)/shard_map/pi,abpq,qj->aibj/dot_general | solution.py:68
  391.2 7.2 %copy.33 = f32[2,80,64,64]{1,2,3,0:T(8,128)} copy(f32[2,80,64,64]{3,2,1,0:T(8,128)} %fusion.4) | data formatting | bytes 5242880 | tf_op jit(solution)/shard_map/pi,abpq,qj->aibj/dot_general | solution.py:68
  398.3 8.3 %convolution_bitcast_fusion.1 = f32[2,64,80,64]{2,3,1,0:T(8,128)} fusion(f32[2,80,64,64]{1,2,3,0:T(8,128)} %copy.33, f32[64]{0:T(128)S(1)} %get-tuple-element.8, f32[64]{0:T(128)S(1)} %get-tuple-element.7), kind=kOutput, calls=%fused_computation.15 | convolution fusion | flops 503328768 | bytes 5243392 | tf_op jit(solution)/shard_map/pi,abpq,qj->aibj/dot_general | solution.py:68
  406.7 5.7 %copy.34 = f32[2,64,80,64]{3,2,1,0:T(8,128)} copy(f32[2,64,80,64]{2,3,1,0:T(8,128)} %convolution_bitcast_fusion.1) | data formatting | bytes 5242880 | tf_op jit(solution)/shard_map/pi,abpq,qj->aibj/transpose | solution.py:68
  412.4 5.5 %reshape.39 = f32[128,5120]{1,0:T(8,128)} reshape(f32[2,64,80,64]{3,2,1,0:T(8,128)} %copy.34) | data formatting | bytes 5242880 | tf_op jit(solution)/shard_map/reshape | solution.py:70
  417.9 3.6 subtract_convert_fusion
  421.4 0.0 all-gather.4.cloned.1.call-update
  421.5 0.0 copy-start.4
  421.5 3.6 fusion.37
  425.1 0.0 copy-done.4
  425.1 8.4 %convolution_bitcast_fusion = f32[2,64,80,64]{3,1,2,0:T(8,128)S(1)} fusion(f32[2,80,16,64]{3,2,1,0:T(8,128)S(1)} %fusion.37, f32[2,80,16,64]{3,2,1,0:T(8,128)S(1)} %copy-done.4), kind=kOutput, calls=%fused_computation.13 | convolution fusion | flops 125829120 | bytes 3932160 | tf_op jit(solution)/shard_map/abui,abuv,abvj->aibj/dot_general | solution.py:37
  433.5 5.6 %copy.25 = f32[2,64,80,64]{3,2,1,0:T(8,128)} copy(f32[2,64,80,64]{3,1,2,0:T(8,128)S(1)} %convolution_bitcast_fusion) | data formatting | bytes 5242880 | tf_op jit(solution)/shard_map/abui,abuv,abvj->aibj/transpose | solution.py:37
  439.2 5.4 %reshape.38 = f32[128,5120]{1,0:T(8,128)} reshape(f32[2,64,80,64]{3,2,1,0:T(8,128)} %copy.25) | data formatting | bytes 5242880 | tf_op jit(solution)/shard_map/reshape | solution.py:40
  444.5 4.4 subtract_bitcast_fusion
  449.0 26.4 %all-gather.4.cloned.1.call-done = bf16[512,5120]{1,0:T(8,128)(2,1)} async-done(((bf16[128,5120]{1,0:T(8,128)(2,1)}), bf16[512,5120]{1,0:T(8,128)(2,1)}) %all-gather.4.cloned.1.call-update) | async-done | bytes 5242896 | tf_op jit(solution)/shard_map/all_gather | solution.py:72
  475.4 5.3 %copy.58 = bf16[512,5120]{1,0:T(8,128)(2,1)} copy(bf16[512,5120]{1,0:T(8,128)(2,1)} %all-gather.4.cloned.1.call-done) | data formatting | bytes 10485760
  480.7 0.0 copy-done.1
  (6 shorter events, 0.0 us)
Async XLA Ops:
  7.2 1.2 copy-start
  7.2 113.1 %reduce-scatter.2.cloned.1.call-start = ((), (), s32[]{:S(2)}) async-start(), calls=%async_computation.1 | async-start | bytes 13107200 | tf_op jit(solution)/shard_map/reduce_scatter | solution.py:50
  20.6 0.8 copy-start.6
  20.6 234.7 %all-gather.6.cloned.1.call-start = ((), (), s32[]{:S(2)}) async-start(), calls=%async_computation.3 | async-start | bytes 8650752 | tf_op jit(solution)/shard_map/all_gather | solution.py:61
  22.8 107.0 %copy-start.2 = (f32[2,80,16,64]{3,2,1,0:T(8,128)}, f32[2,80,16,64]{3,2,1,0:T(8,128)S(1)}, u32[]{:S(2)}) copy-start(f32[2,80,16,64]{3,2,1,0:T(8,128)S(1)} %copy.20) | copy-start | bytes 1966084
  129.8 8.4 %copy-start.3 = (f32[2,80,16,64]{3,2,1,0:T(8,128)S(1)}, f32[2,80,16,64]{3,2,1,0:T(8,128)}, u32[]{:S(2)}) copy-start(f32[2,80,16,64]{3,2,1,0:T(8,128)} %copy.21) | copy-start | bytes 1966084
  141.6 333.8 %all-gather.4.cloned.1.call-start = ((), (), s32[]{:S(2)}) async-start(), calls=%async_computation.2 | async-start | bytes 6553600 | tf_op jit(solution)/shard_map/all_gather | solution.py:72
  287.3 41.7 %copy-start.5 = (s32[32,2,80,16]{3,1,2,0:T(2,128)S(1)}, s32[32,2,80,16]{3,1,2,0:T(2,128)}, u32[]{:S(2)}) copy-start(s32[32,2,80,16]{3,1,2,0:T(2,128)} %copy.29) | copy-start | bytes 983044
  421.5 3.7 copy-start.4
  475.4 5.3 %copy-start.1 = (bf16[1024,512]{1,0:T(8,128)(2,1)S(1)}, bf16[1024,512]{1,0:T(8,128)(2,1)}, u32[]{:S(2)}) copy-start(bf16[1024,512]{1,0:T(8,128)(2,1)} %param.5) | copy-start | bytes 3145732
Sparse Core Ops, SparseCore 0:
  20.8 99.4 reduce-scatter.1
  141.7 113.5 all-gather.5
  421.6 53.7 all-gather.3
where the time goes:
time: 492 us; the launch traced here: 487 us
  matrix products  149 us (30%)
  waiting for transfers between devices  141 us (29%)
  blocking collectives  89.5 us (18%)
  local copies, waits for them, and re-layouts  81.5 us (17%)
  between operations  14.1 us (3%)
  other arithmetic  12.4 us (3%)
    dot_general x2, matrix products, body(): jnp.einsum('nabui,nabuv,nabvj->abij', rows_hot, values, cols_hot, precisi...  97.6 us
    reduce_scatter x1, waiting for transfers between devices, body(): lax.psum_scatter(jnp.dot(hidden_act.T, out_grad, preferred_element_type=j...  95.1 us
    all_gather x1, blocking collectives, body(): chosen = lax.all_gather(coef_picks, 'replica', axis=0, tiled=True)  89.5 us
    all_gather x1, local copies, waits for them, and re-layouts, body(): values = lax.all_gather(coeffs[None], 'replica', axis=0, tiled=True)  31.9 us
    all_gather x1, waiting for transfers between devices, body(): new_params = lax.all_gather(shard_params, 'fsdp', axis=0, tiled=True)  26.4 us
    all_gather x1, waiting for transfers between devices, body(): values = lax.all_gather(coeffs[None], 'replica', axis=0, tiled=True)  19.2 us
    dot_general x2, matrix products, body(): jnp.einsum('pi,abpq,qj->aibj', table_dct, placed, table_dct, precision=la...  14.6 us
    dot_general x1, matrix products, body(): jnp.dot(hidden_act.T, out_grad, preferred_element_type=jnp.float32)  12.2 us
  transfers between devices with their start and end apart: 3, of which 3 were waited for; matrix products, arithmetic and copies ran while one was open for 7% of the time, Pallas kernels for 0%

commit v1 on v0

v1 whole, which is shorter than its diff:
```python
import functools
import math

import jax
import jax.numpy as jnp
import numpy as np
from jax import lax
from jax.experimental import pallas as pl
from jax.experimental.pallas import tpu as pltpu
from jax.sharding import Mesh
from jax.sharding import PartitionSpec as P

KEEP = 16
DECAY = 0.9
STEP = 0.5
PARTS = 2
PAIRS = 8
PER = PAIRS // PARTS
GW = 640
QROWS = 656
UROWS = 176
F32 = jnp.float32
BF16 = jnp.bfloat16
I16 = jnp.int16
I32 = jnp.int32
ARB = pltpu.CompilerParams(vmem_limit_bytes=48 * 1024 * 1024)


def cosine():
    k = np.arange(64, dtype=np.float64)[:, None]
    i = np.arange(64, dtype=np.float64)[None, :]
    w = np.where(k == 0, math.sqrt(1.0 / 64), math.sqrt(2.0 / 64))
    return w * np.cos(math.pi * (2.0 * i + 1.0) * k / 128.0)


def halves(m):
    hi = m.astype(np.float32).astype(jnp.bfloat16)
    lo = (m - hi.astype(np.float64)).astype(np.float32).astype(jnp.bfloat16)
    return hi, lo


def diag(m, n):
    return np.kron(np.eye(n), m)


def right_table(m):
    hi, lo = halves(m)
    row = np.concatenate([hi, lo], axis=1)
    return np.concatenate([row, row], axis=0)


def left_table(m):
    return np.concatenate(halves(m), axis=0)


def split(x):
    hi = x.astype(BF16)
    return hi, (x - hi.astype(F32)).astype(BF16)


def mul_right(x, table):
    hi, lo = split(x)
    o = jnp.dot(jnp.concatenate([hi, lo], axis=1), table, preferred_element_type=F32)
    return o[:, :128] + o[:, 128:]


def mul_left(table, x):
    n = table.shape[0] // 2
    hi, lo = split(x)
    o = jnp.dot(table, hi, preferred_element_type=F32)
    return o[:n] + o[n:] + jnp.dot(table[:n], lo, preferred_element_type=F32)


def lanes_of(x, idx):
    return jnp.take_along_axis(x, jnp.broadcast_to(idx, x.shape), axis=1, mode="promise_in_bounds")


def rows_of(x, idx):
    return jnp.take_along_axis(x, idx, axis=0, mode="promise_in_bounds")


def lane(shape):
    return lax.broadcasted_iota(I32, shape, len(shape) - 1)


def sub(shape):
    return lax.broadcasted_iota(I32, shape, 0)


def pow2(e):
    n = e + 100
    r = jnp.full(e.shape, 2.0**-100, F32)
    for bit in range(7):
        r = r * jnp.where((n >> bit) & 1 == 1, 2.0 ** (1 << bit), 1.0)
    r = r * jnp.where((n >> 7) & 1 == 1, 2.0**64, 1.0)
    return r * jnp.where((n >> 7) & 1 == 1, 2.0**64, 1.0)


def exponent(top):
    e = jnp.floor(math.log2(32767.0) - jnp.log(jnp.maximum(top, 1e-35)) * (1 / math.log(2)))
    return jnp.clip(e, -60.0, 99.0).astype(I32)


def coded(x, e):
    v = jnp.floor(x * pow2(e) + 0.5)
    return jnp.clip(v, -32767.0, 32767.0).astype(I32).astype(I16)


def value(q, e):
    return q.astype(I32).astype(F32) * pow2(-e)


def gradient_kernel(me, h_ref, g_ref, own_ref, other_ref, ht):
    @pl.when(pl.program_id(0) == 0)
    def _():
        yl, core = me[0], me[1]
        for i, (y, c) in enumerate(((yl, core), (1 - yl, core), (yl, 1 - core), (1 - yl, 1 - core))):
            at = pl.multiple_of(128 * (2 * y + c), 128)
            ht[128 * i : 128 * i + 128, :] = h_ref[:, pl.ds(at, 128)].T

    other_ref[...] = jnp.dot(ht[256:], g_ref[...], preferred_element_type=F32)
    own_ref[...] = jnp.dot(ht[:256], g_ref[...], preferred_element_type=F32)


def gradient(me, hidden, grad, part):
    cols = 5120 // PARTS
    tile = 512
    n = cols // tile
    spec = pl.BlockSpec((256, tile), lambda i, me: (0, i))
    return pl.pallas_call(
        gradient_kernel,
        grid_spec=pltpu.PrefetchScalarGridSpec(
            num_scalar_prefetch=1,
            grid=(n,),
            in_specs=[
                pl.BlockSpec((1024, 512), lambda i, me: (0, 0)),
                pl.BlockSpec((1024, tile), lambda i, me: (0, part * n + i)),
            ],
            out_specs=[spec, spec],
            scratch_shapes=[pltpu.VMEM((512, 1024), BF16)],
        ),
        out_shape=[jax.ShapeDtypeStruct((256, cols), F32)] * 2,
        compiler_params=ARB,
        cost_estimate=pl.CostEstimate(flops=2 * 512 * 1024 * cols, bytes_accessed=8 * 2**20, transcendentals=0),
        name="gradient",
    )(me, hidden, grad)


def place(group, pos):
    return pos if group == 0 else 5 + (pos + 1) % 5


def pick_tables():
    t = np.zeros((2, 8, 128), np.int32)
    for g in range(2):
        for ln in range(128):
            pos = min(ln // 16, 4) if ln < 80 else (ln - 80 if ln < 85 else 0)
            t[g, 0, ln] = place(g, pos)
            t[g, 1, ln] = 64 * (place(g, pos) % 2) if ln < 80 else 0
            for tile in range(3):
                t[g, 2 + tile, ln] = place(g, min(2 * tile + ln // 64, 4))
    return t


def compress_kernel(part, me, own, got, mom, picks, tab, rt, lt, *refs):
    pm, q, comp = refs[-3:]
    yl = me[0]
    first = 10 * (PER * part + pl.program_id(0))
    ln = lane((1, 128))
    w0 = (own[:128] + got[:128]) * (1.0 / 64) + DECAY * mom[0]
    w1 = (own[128:] + got[128:]) * (1.0 / 64)
    pm[...] = w0
    exps = jnp.zeros((16, 128), I32)
    tiles = []
    for t in range(5):
        x = w1[:, 128 * t : 128 * t + 128]
        e = exponent(jnp.max(jnp.abs(x), axis=0, keepdims=True))
        q[0, 128 * t : 128 * t + 128, :] = coded(x, jnp.broadcast_to(e, (8, 128))[:1])
        exps = jnp.where(sub((16, 128)) == t, jnp.broadcast_to(e, (16, 128)), exps)
        tiles.append(mul_right(jnp.concatenate([w0[:, 128 * t : 128 * t + 128], x], axis=0), rt[...]))
    q[0, 640:656, :] = exps.astype(I16)
    u16 = sub((16, 128))
    ln16 = lane((16, 128))
    short = []
    for g in range(2):
        pieces = []
        span = first + tab[g, 0:1, :]
        for rb in range(4):
            qt = picks[rb // 2, rb % 2, 16:32, :]
            chosen = jnp.where(u16 == (ln16 & 15), lanes_of(qt, span), 0)
            idx = jnp.sum(chosen, axis=0, keepdims=True) + tab[g, 1:2, :]
            rows = slice(64 * rb, 64 * rb + 64)
            a = lanes_of(tiles[3 * g][rows], idx)
            b = lanes_of(tiles[3 * g + 1][rows], idx)
            c = lanes_of(tiles[2][rows], idx)
            pieces.append(jnp.where(ln < 32, a, jnp.where(ln < 64, b, c)))
        short.append(jnp.concatenate(pieces, axis=0))
    z = mul_left(lt[...], jnp.concatenate(short, axis=1))
    for g in range(2):
        span = first + tab[g, 0:1, :]
        for rb in range(4):
            rel, a = rb // 2, rb % 2
            to = yl if rel == 0 else 1 - yl
            pt = picks[rel, a, 0:16, :]
            qt = picks[rel, a, 16:32, :]
            pidx = lanes_of(pt, span)
            for h in range(2):
                pi = pidx[8 * h : 8 * h + 8]
                low, high = pi & 7, pi >> 3
                acc = pi.astype(F32)
                for j in range(8):
                    r = 64 * rb + 8 * j
                    v = rows_of(z[r : r + 8, 128 * g : 128 * g + 128], low)
                    acc = jnp.where((high == j) & (ln < 80), v, acc)
                comp[a, g, to, 8 * h : 8 * h + 8, :] = acc
            back = jnp.full((8, 128), -1, I32)
            for t in range(3):
                qg = lanes_of(qt, first + tab[g, 2 + t : 3 + t, :])
                src = 16 * (2 * t + (ln16 >> 6)) + u16 + 1
                hit = jnp.where(qg == (ln16 & 63), src, 0)
                if t == 2:
                    hit = jnp.where(ln16 < 64, hit, 0)
                inv = jnp.sum(hit, axis=0, keepdims=True) - 1
                back = jnp.where(sub((8, 128)) == t, jnp.broadcast_to(inv, (8, 128)), back)
            comp[a, g, to, 16:24, :] = back.astype(F32)


def compress(part, me, own, got, mom, picks, tab, rt, lt, before):
    n = PER
    full = lambda *s: pl.BlockSpec(s, lambda i, me: (0,) * len(s))
    col = lambda r: pl.BlockSpec((r, GW), lambda i, me: (0, i))
    args = [own, got, mom, picks, tab, rt, lt]
    in_specs = [
        col(256),
        col(256),
        pl.BlockSpec((1, 128, GW), lambda i, me: (0, 0, part * n + i)),
        full(2, 2, 32, 128),
        full(2, 8, 128),
        full(256, 256),
        full(512, 256),
    ]
    alias = {}
    if before is not None:
        args.append(before)
        in_specs.append(pl.BlockSpec(memory_space=pl.ANY))
        alias = {8: 2}
    return pl.pallas_call(
        functools.partial(compress_kernel, part),
        grid_spec=pltpu.PrefetchScalarGridSpec(
            num_scalar_prefetch=1,
            grid=(n,),
            in_specs=in_specs,
            out_specs=[
                col(128),
                pl.BlockSpec((1, QROWS, 128), lambda i, me: (i, 0, 0)),
                pl.BlockSpec((2, 2, 2, 24, 128), lambda i, me: (0, part * n + i, 0, 0, 0)),
            ],
        ),
        out_shape=[
            jax.ShapeDtypeStruct((128, 5120 // PARTS), F32),
            jax.ShapeDtypeStruct((n, QROWS, 128), I16),
            jax.ShapeDtypeStruct((2, 16, 2, 24, 128), F32),
        ],
        input_output_aliases=alias,
        compiler_params=ARB,
        cost_estimate=pl.CostEstimate(flops=2 * 10**9, bytes_accessed=9 * 2**20, transcendentals=0),
        name="compress",
    )(me, *args)


def owner_kernel(got, rt, lt, out, xh, xl, hot):
    ln16 = lane((16, 128))

    def one(n, _):
        at = pl.multiple_of(16 * n, 16)
        x = got[n, 0:16, :]
        for t in range(3):
            idx = got[n, 16 + t : 17 + t, :].astype(I32)
            v = jnp.where(idx >= 0, lanes_of(x, jnp.maximum(idx, 0)), 0.0)
            hi, lo = split(v)
            xh[t, pl.ds(at, 16), :] = hi
            xl[t, pl.ds(at, 16), :] = lo
            p = lanes_of(x, 80 + 2 * t + (ln16 >> 6))
            hot[t, pl.ds(at, 16), :] = jnp.where(p == (ln16 & 63).astype(F32), 1.0, 0.0).astype(BF16)
        return 0

    lax.fori_loop(0, got.shape[0], one, 0, unroll=4)
    same = (sub((128, 128)) >> 6) == (lane((128, 128)) >> 6)
    tiles = []
    for t in range(3):
        dims = (((0,), (0,)), ((), ()))
        d = lax.dot_general(hot[t], xh[t], dims, preferred_element_type=F32)
        d = d + lax.dot_general(hot[t], xl[t], dims, preferred_element_type=F32)
        d = jnp.where(same, d, 0.0)
        u = mul_left(lt[...], mul_right(d, rt[...]))
        tiles.append(u[:64] + u[64:])
    last = tiles[2]
    ln = lane((32, 128))
    tiles[2] = jnp.where(ln < 64, last[:32], jnp.roll(last[32:], 64, axis=1))
    x = jnp.concatenate(tiles, axis=0)
    e = exponent(jnp.max(jnp.abs(x), axis=0, keepdims=True))
    out[0:160, :] = coded(x, e)
    out[160:176, :] = jnp.broadcast_to(e, (16, 128)).astype(I16)


def owner(got, rt, lt):
    return pl.pallas_call(
        owner_kernel,
        out_shape=jax.ShapeDtypeStruct((UROWS, 128), I16),
        scratch_shapes=[pltpu.VMEM((3, 1024, 128), BF16)] * 3,
        compiler_params=ARB,
        name="owner",
    )(got, rt, lt)


def decode(ref, a, y):
    group = []
    for g in range(2):
        e = ref[a, g, y, 160:176, :].astype(I32)[:1]
        group.append(value(ref[a, g, y, 0:160, :], e))
    even, odd = group
    lo = lane((32, 128)) < 64
    e2, o2 = even[128:160], odd[128:160]
    top = jnp.where(lo, e2, jnp.roll(o2, 64, axis=1))
    bottom = jnp.where(lo, jnp.roll(e2, 64, axis=1), o2)
    return [even[:64], even[64:128], jnp.concatenate([top, bottom], axis=0), odd[:64], odd[64:128]]


def finish_kernel(with_update, me, got, mine, theirs, *refs):
    yl = me[0]
    new = refs[-1]
    for rel in range(2):
        y = yl if rel == 0 else 1 - yl
        par = mine if rel == 0 else theirs
        for a in range(2):
            rows = slice(64 * a, 64 * a + 64)
            for t, u in enumerate(decode(got, a, y)):
                cols = slice(128 * t, 128 * t + 128)
                if with_update and rel == 0:
                    refs[-2][rows, cols] = u
                new[y, 0, rows, cols] = (par[rows, cols].astype(F32) - STEP * u).astype(BF16)


def finish(with_update, me, got, mine, theirs, before):
    col = pl.BlockSpec((128, GW), lambda i, me: (0, i))
    which = (lambda me: me[1]) if with_update else (lambda me: 1 - me[1])
    args = [got, mine, theirs]
    in_specs = [pl.BlockSpec((2, 2, 2, UROWS, 128), lambda i, me: (0, i, 0, 0, 0)), col, col]
    out_specs = [pl.BlockSpec((2, 1, 128, GW), lambda i, me: (0, which(me), 0, i))]
    out_shape = [jax.ShapeDtypeStruct((2, 2, 128, 5120), BF16)]
    alias = {}
    if with_update:
        out_specs.insert(0, col)
        out_shape.insert(0, jax.ShapeDtypeStruct((128, 5120), F32))
    else:
        args.append(before)
        in_specs.append(pl.BlockSpec(memory_space=pl.ANY))
        alias = {4: 0}
    return pl.pallas_call(
        functools.partial(finish_kernel, with_update),
        grid_spec=pltpu.PrefetchScalarGridSpec(
            num_scalar_prefetch=1, grid=(PAIRS,), in_specs=in_specs, out_specs=out_specs
        ),
        out_shape=out_shape,
        input_output_aliases=alias,
        compiler_params=ARB,
        name="finish",
    )(me, *args)


def left_kernel(part, q, pm, picks, rt, lt, irt, ilt, *refs):
    out, mask = refs[-2:]
    first = 10 * (PER * part + pl.program_id(0))

    @pl.when(pl.program_id(0) == 0)
    def _():
        for a in range(2):
            k = sub((64, 128))
            hit = jnp.zeros((64, 128), F32)
            for u in range(16):
                hit = jnp.where(picks[0, a, u : u + 1, :] == k, 1.0, hit)
            mask[64 * a : 64 * a + 64, :] = hit

    ln16 = lane((16, 128))
    for t in range(5):
        cols = slice(128 * t, 128 * t + 128)
        e = q[0, 640:656, :].astype(I32)[t : t + 1]
        m = pm[:, cols] + value(q[0, 128 * t : 128 * t + 128, :], e)
        c = mul_left(lt[...], mul_right(m, rt[...]))
        span = first + 2 * t + (lane((1, 128)) >> 6)
        keep = lanes_of(mask[...], span)
        parts = []
        for a in range(2):
            hit = lanes_of(picks[0, a, 16:32, :], span) == (ln16 & 63)
            parts.append(jnp.max(jnp.where(hit, 1.0, 0.0), axis=0, keepdims=True))
        rows = sub((128, 128)) < 64
        keep = keep * jnp.where(rows, parts[0], parts[1])
        r = mul_left(ilt[...], mul_right(c * keep, irt[...]))
        out[0, :, cols] = m - r


def left(part, q, pm, picks, rt, lt, irt, ilt, before):
    n = PER
    full = lambda *s: pl.BlockSpec(s, lambda i: (0,) * len(s))
    args = [q, pm, picks, rt, lt, irt, ilt]
    in_specs = [
        pl.BlockSpec((1, QROWS, 128), lambda i: (i, 0, 0)),
        pl.BlockSpec((128, GW), lambda i: (0, i)),
        full(2, 2, 32, 128),
        full(256, 256),
        full(256, 128),
        full(256, 256),
        full(256, 128),
    ]
    alias = {}
    if before is not None:
        args.append(before)
        in_specs.append(pl.BlockSpec(memory_space=pl.ANY))
        alias = {7: 0}
    return pl.pallas_call(
        functools.partial(left_kernel, part),
        grid=(n,),
        in_specs=in_specs,
        out_specs=pl.BlockSpec((1, 128, GW), lambda i: (0, 0, part * n + i)),
        out_shape=jax.ShapeDtypeStruct((1, 128, 5120), F32),
        scratch_shapes=[pltpu.VMEM((128, 128), F32)],
        input_output_aliases=alias,
        compiler_params=ARB,
        cost_estimate=pl.CostEstimate(flops=2 * 10**9, bytes_accessed=4 * 2**20, transcendentals=0),
        name="left",
    )(*args)


REP = ("x", "z", "yh", "yl")
NEAR = [(2 * h + k, 2 * h + 1 - k) for h in range(2) for k in range(2)]
FAR = [(y, 3 - y) for y in range(4)]
SWAP = [(0, 1), (1, 0)]


def body(hidden, grad, momentum, coef_picks, params):
    c = cosine()
    rt = jnp.asarray(right_table(diag(c.T, 2)))
    irt = jnp.asarray(right_table(diag(c, 2)))
    lt4 = jnp.asarray(left_table(diag(c, 4)))
    lt = jnp.asarray(left_table(diag(c, 2)))
    ilt = jnp.asarray(left_table(diag(c.T, 2)))
    tab = jnp.asarray(pick_tables())
    me = jnp.stack([lax.axis_index("yl"), lax.axis_index("c")]).astype(I32)

    mine = jnp.pad(coef_picks[0].swapaxes(1, 2), ((0, 0), (0, 0), (0, 48)))
    theirs = lax.ppermute(mine, ("yh", "yl"), NEAR)
    picks = jnp.stack([mine, theirs])
    far_params = lax.ppermute(params, ("yh", "yl"), FAR)

    pms, qs, comp = [], [], None
    grads = [gradient(me, hidden, grad, part) for part in range(PARTS)]
    swapped = [lax.ppermute(other, "c", SWAP) for _, other in grads]
    for part in range(PARTS):
        pm, q, comp = compress(part, me, grads[part][0], swapped[part], momentum, picks, tab, rt, lt4, comp)
        pms.append(pm)
        qs.append(lax.ppermute(q, ("yh", "yl"), NEAR))
    got = lax.all_to_all(comp.reshape(64, 24, 128), REP, 0, 0, tiled=True)
    mine16 = owner(got, irt, ilt)
    every = lax.all_to_all(jnp.broadcast_to(mine16, (64, UROWS, 128)), REP, 0, 0, tiled=True)

    momentum_left = None
    for part in range(PARTS):
        momentum_left = left(part, qs[part], pms[part], picks, rt, lt, irt, ilt, momentum_left)

    other_params = lax.ppermute(params, "c", SWAP)
    other_far = lax.ppermute(far_params, "c", SWAP)
    other_every = lax.ppermute(every, "c", SWAP)
    shape = (2, 16, 2, UROWS, 128)
    update, new = finish(True, me, every.reshape(shape), params, far_params, None)
    (new,) = finish(False, me, other_every.reshape(shape), other_params, other_far, new)
    return momentum_left, update, new.reshape(512, 5120)


def solution(mesh):
    fine = Mesh(mesh.devices.reshape(4, 4, 2, 2, 2), ("x", "z", "yh", "yl", "c"))
    rep, fsdp = ("x", "z", "yh"), ("yl", "c")
    return jax.shard_map(
        body,
        mesh=fine,
        in_specs=(
            P(rep + fsdp, None),
            P(rep + fsdp, None),
            P(rep, fsdp, None),
            P(rep, fsdp, None, None),
            P(fsdp, None),
        ),
        out_specs=(P(rep, fsdp, None), P(fsdp, None), P()),
        check_vma=False,
    )
```

time: 492 us -> 198 us (0.40)
  matrix products: 149 us -> 0 us
  waiting for transfers between devices: 141 us -> 51.7 us
  local copies, waits for them, and re-layouts: 81.5 us -> 4.19 us
  Pallas kernels: 0 us -> 65.2 us
  blocking collectives: 89.5 us -> 63.9 us
  between operations: 14.1 us -> 0.72 us
  other arithmetic: 12.4 us -> 0.08 us
  starting transfers between devices: 0.65 us -> 11.3 us
    dot_general x11 -> x0, matrix products: 149 us -> none  [the longest x2 97.6 us: body(): jnp.einsum('nabui,nabuv,nabvj->abij', rows_hot, values, cols_hot, precisi...]
    reduce_scatter x1 -> x0, waiting for transfers between devices: 95.1 us -> none  [body(): lax.psum_scatter(jnp.dot(hidden_act.T, out_grad, preferred_element_type=j...]
    all_gather x1 -> x0, blocking collectives: 89.5 us -> none  [body(): chosen = lax.all_gather(coef_picks, 'replica', axis=0, tiled=True)]
    pallas_call x0 -> x9, Pallas kernels: none -> 65.2 us  [the longest x2 20 us: left(): pl.pallas_call(functools.partial(left_kernel, part), grid=(n,), in_specs=...]
    all_to_all x0 -> x2, blocking collectives: none -> 63.9 us  [the longest x1 39.1 us: body(): lax.all_to_all(jnp.broadcast_to(mine16, (64, UROWS, 128)), REP, 0, 0, til...]
    ppermute x0 -> x9, waiting for transfers between devices: none -> 51.7 us  [the longest x1 30.5 us: body(): far_params = lax.ppermute(params, ('yh', 'yl'), FAR)]
    all_gather x2 -> x0, waiting for transfers between devices: 45.6 us -> none  [the longest x1 26.4 us: body(): new_params = lax.all_gather(shard_params, 'fsdp', axis=0, tiled=True)]
    all_gather x1 -> x0, local copies, waits for them, and re-layouts: 31.9 us -> none  [body(): values = lax.all_gather(coeffs[None], 'replica', axis=0, tiled=True)]
  transfers between devices with their start and end apart: 3 -> 9, of which waited for: 3 -> 4; matrix products, arithmetic and copies ran while one was open for 7% -> 0% of each run, Pallas kernels for 0% -> 20%
where the time goes in v1:
time: 198 us; the launch traced here: 197 us
  Pallas kernels  65.2 us (33%)
  blocking collectives  63.9 us (32%)
  waiting for transfers between devices  51.7 us (26%)
  starting transfers between devices  11.3 us (6%)
  local copies, waits for them, and re-layouts  4.19 us (2%)
    all_to_all x1, blocking collectives, body(): lax.all_to_all(jnp.broadcast_to(mine16, (64, UROWS, 128)), REP, 0, 0, til...  39.1 us
    ppermute x1, waiting for transfers between devices, body(): far_params = lax.ppermute(params, ('yh', 'yl'), FAR)  30.5 us
    all_to_all x1, blocking collectives, body(): got = lax.all_to_all(comp.reshape(64, 24, 128), REP, 0, 0, tiled=True)  24.8 us
    pallas_call x2, Pallas kernels, left(): pl.pallas_call(functools.partial(left_kernel, part), grid=(n,), in_specs=...  20 us
    ppermute x2, waiting for transfers between devices, body(): qs.append(lax.ppermute(q, ('yh', 'yl'), NEAR))  19.9 us
    pallas_call x2, Pallas kernels, gradient(): pl.pallas_call(gradient_kernel, grid_spec=pltpu.PrefetchScalarGridSpec(nu...  16 us
    pallas_call x2, Pallas kernels, compress(): pl.pallas_call(functools.partial(compress_kernel, part), grid_spec=pltpu....  14.2 us
    pallas_call x2, Pallas kernels, finish(): pl.pallas_call(functools.partial(finish_kernel, with_update), grid_spec=p...  10.5 us
  transfers between devices with their start and end apart: 9, of which 4 were waited for; matrix products, arithmetic and copies ran while one was open for 0% of the time, Pallas kernels for 20%

profile of v1, /device:TPU:1, one launch (start us, length us, event | category | flops | bytes accessed | tf_op | source)
XLA Modules:
  0.0 197.2 jit_solution(1811889657888386273)
XLA Ops:
  0.6 0.1 pad_add_fusion.1.me
  0.7 0.0 copy-start
  0.7 1.2 copy-done
  1.9 8.0 %gradient.3 = (f32[256,2560]{1,0:T(8,128)S(1)}, f32[256,2560]{1,0:T(8,128)}) custom-call(s32[2]{0:T(128)S(1)} %pad_add_fusion.1.me, bf16[1024,512]{1,0:T(8,128)(2,1)S(1)} %copy-done, bf16[1024,5120]{1,0:T(8,128)(2,1)} %g_ref.3), custom_call_target="tpu_custom_call" | custom-call | flops 2684354560 | bytes 8388608 | tf_op jit(solution)/shard_map/gradient/pallas_call | solution.py:130
  9.9 1.5 collective-permute-start.2
  11.4 8.0 %gradient.2 = (f32[256,2560]{1,0:T(8,128)S(1)}, f32[256,2560]{1,0:T(8,128)}) custom-call(s32[2]{0:T(128)S(1)} %pad_add_fusion.1.me, bf16[1024,512]{1,0:T(8,128)(2,1)S(1)} %copy-done, bf16[1024,5120]{1,0:T(8,128)(2,1)} %g_ref.3), custom_call_target="tpu_custom_call" | custom-call | flops 2684354560 | bytes 8388608 | tf_op jit(solution)/shard_map/gradient/pallas_call | solution.py:130
  19.4 0.0 collective-permute-start
  19.5 0.0 copy-done.11
  19.5 1.5 collective-permute-start.1
  20.9 1.4 collective-permute-done.1
  22.3 0.0 collective-permute-done.2.got
  22.3 0.0 copy-start.10
  22.3 1.5 copy-done.10
  23.8 0.0 copy-done.2
  23.8 0.0 copy-done.3
  23.8 0.0 copy-done.7
  23.8 7.1 %compress.2 = (f32[128,2560]{1,0:T(8,128)S(1)}, s16[4,656,128]{2,1,0:T(8,128)(2,1)}, f32[2,16,2,24,128]{4,3,2,1,0:T(8,128)S(1)}) custom-call(s32[2]{0:T(128)S(1)} %pad_add_fusion.1.me, f32[256,2560]{1,0:T(8,128)S(1)} %get-tuple-element.17.own, f32[256,2560]{1,0:T(8,128)} %copy-done.10, f32[1,128,5120]{2,1,0:T(8,128)} %mom.3, ...), custom_call_target="tpu_custom_call" | custom-call | flops 2000000000 | bytes 9437184 | tf_op jit(solution)/shard_map/compress/pallas_call | solution.py:247
  30.9 1.1 copy-done.8
  32.0 0.0 collective-permute-done.got
  32.0 7.1 %compress.3 = (f32[128,2560]{1,0:T(8,128)S(1)}, s16[4,656,128]{2,1,0:T(8,128)(2,1)}, f32[2,16,2,24,128]{4,3,2,1,0:T(8,128)S(1)}) custom-call(s32[2]{0:T(128)S(1)} %pad_add_fusion.1.me, f32[256,2560]{1,0:T(8,128)S(1)} %get-tuple-element.15.own, f32[256,2560]{1,0:T(8,128)} %collective-permute-done.got, ...), custom_call_target="tpu_custom_call", output_to_operand_aliasing={{2}: (8, {})} | custom-call | flops 2000000000 | bytes 9437184 | tf_op jit(solution)/shard_map/compress/pallas_call | solution.py:247
  39.1 24.8 %all_to_all.10.got = f32[64,24,128]{2,1,0:T(8,128)S(1)} all-to-all(f32[64,24,128]{2,1,0:T(8,128)S(1)} %bitcast.13), channel_id=1, replica_groups=mesh['x'=4,'z'=4,'yh'=2,'yl'=2,'c'=2] {'x','z','yh','yl'}, dimensions={0} | all-to-all | bytes 1572864 | tf_op jit(solution)/shard_map/all_to_all | solution.py:462
  63.8 0.0 copy-done.4
  63.8 0.0 copy-done.5
  63.8 4.6 %owner.1 = s16[176,128]{1,0:T(8,128)(2,1)S(1)} custom-call(f32[64,24,128]{2,1,0:T(8,128)S(1)} %all_to_all.10.got, bf16[256,256]{1,0:T(8,128)(2,1)S(1)} %copy-done.4, bf16[256,128]{1,0:T(8,128)(2,1)S(1)} %copy-done.5), custom_call_target="tpu_custom_call" | custom-call | tf_op jit(solution)/shard_map/owner/pallas_call | solution.py:307
  68.4 0.4 broadcast_in_dim.3
  68.8 0.0 copy-start.1
  68.8 0.0 copy-start.6
  68.8 0.0 copy-start.9
  68.8 39.1 %all_to_all.11 = s16[64,176,128]{2,1,0:T(8,128)(2,1)S(1)} all-to-all(s16[64,176,128]{2,1,0:T(8,128)(2,1)S(1)} %broadcast_in_dim.3), channel_id=1, replica_groups=mesh['x'=4,'z'=4,'yh'=2,'yl'=2,'c'=2] {'x','z','yh','yl'}, dimensions={0} | all-to-all | bytes 5767168 | tf_op jit(solution)/shard_map/all_to_all | solution.py:464
  108.0 4.9 %collective-permute-start.6 = (s16[64,176,128]{2,1,0:T(8,128)(2,1)S(1)}, s16[64,176,128]{2,1,0:T(8,128)(2,1)S(1)}, u32[]{:S(2)}, u32[]{:S(2)}) collective-permute-start(s16[64,176,128]{2,1,0:T(8,128)(2,1)S(1)} %all_to_all.11), channel_id=1, source_target_pairs={{0,1},{1,0},{2,3},{3,2},{4,5},{5,4},{6,7},{7,6},{8,9},{9,8},{10,11... | collective-permute-start | bytes 8650760 | tf_op jit(solution)/shard_map/ppermute | solution.py:472
  112.9 0.0 copy-done.1
  112.9 0.8 collective-permute-start.5
  113.8 0.3 collective-permute-start.7
  114.0 30.5 %collective-permute-done.5.theirs = bf16[128,5120]{1,0:T(8,128)(2,1)S(1)} collective-permute-done((bf16[128,5120]{1,0:T(8,128)(2,1)S(1)}, bf16[128,5120]{1,0:T(8,128)(2,1)S(1)}, u32[]{:S(2)}, u32[]{:S(2)}) %collective-permute-start.5) | collective-permute-done | bytes 1310752 | tf_op jit(solution)/shard_map/ppermute | solution.py:453
  144.5 0.8 collective-permute-start.8
  145.3 0.0 collective-permute-start.4
  145.3 1.5 collective-permute-start.3
  146.8 15.5 %collective-permute-done.4.q = s16[4,656,128]{2,1,0:T(8,128)(2,1)S(1)} collective-permute-done((s16[4,656,128]{2,1,0:T(8,128)(2,1)}, s16[4,656,128]{2,1,0:T(8,128)(2,1)S(1)}, u32[]{:S(2)}, u32[]{:S(2)}) %collective-permute-start.4) | collective-permute-done | bytes 671776 | tf_op jit(solution)/shard_map/ppermute | solution.py:461
  162.2 0.0 copy-done.6
  162.3 0.0 copy-done.9
  162.3 10.0 %left.2.refs_0_ = f32[1,128,5120]{2,1,0:T(8,128)} custom-call(s16[4,656,128]{2,1,0:T(8,128)(2,1)S(1)} %collective-permute-done.4.q, f32[128,2560]{1,0:T(8,128)S(1)} %copy-done.9, s32[2,2,32,128]{3,2,1,0:T(8,128)S(1)} %pad_add_fusion.picks, bf16[256,256]{1,0:T(8,128)(2,1)S(1)} %copy-done.2, bf16[256,128]{1,0:T(8,128)(2,1)S(1)} %copy-done.6, ...), custom_call_target="tpu_custom_call" | custom-call | flops 2000000000 | bytes 4194304 | tf_op jit(solution)/shard_map/left/pallas_call | solution.py:420
  172.2 4.4 %collective-permute-done.3.q = s16[4,656,128]{2,1,0:T(8,128)(2,1)S(1)} collective-permute-done((s16[4,656,128]{2,1,0:T(8,128)(2,1)}, s16[4,656,128]{2,1,0:T(8,128)(2,1)S(1)}, u32[]{:S(2)}, u32[]{:S(2)}) %collective-permute-start.3) | collective-permute-done | bytes 671776 | tf_op jit(solution)/shard_map/ppermute | solution.py:461
  176.6 10.0 %left.3 = f32[1,128,5120]{2,1,0:T(8,128)} custom-call(s16[4,656,128]{2,1,0:T(8,128)(2,1)S(1)} %collective-permute-done.3.q, f32[128,2560]{1,0:T(8,128)S(1)} %get-tuple-element.21.pm, s32[2,2,32,128]{3,2,1,0:T(8,128)S(1)} %pad_add_fusion.picks, bf16[256,256]{1,0:T(8,128)(2,1)S(1)} %copy-done.2, ...), custom_call_target="tpu_custom_call", output_to_operand_aliasing={{}: (7, {})} | custom-call | flops 2000000000 | bytes 4194304 | tf_op jit(solution)/shard_map/left/pallas_call | solution.py:420
  186.7 5.3 %finish.2 = (f32[128,5120]{1,0:T(8,128)}, bf16[2,2,128,5120]{3,2,1,0:T(8,128)(2,1)}) custom-call(s32[2]{0:T(128)S(1)} %pad_add_fusion.1.me, s16[2,16,2,176,128]{4,3,2,1,0:T(8,128)(2,1)S(1)} %bitcast.12, bf16[128,5120]{1,0:T(8,128)(2,1)S(1)} %copy-done.1, bf16[128,5120]{1,0:T(8,128)(2,1)S(1)} %collective-permute-done.5.theirs), custom_call_target="tpu_custom_call" | custom-call | tf_op jit(solution)/shard_map/finish/pallas_call | solution.py:359
  192.0 0.0 collective-permute-done.7.mine
  192.0 0.0 collective-permute-done.8.theirs
  192.0 0.0 collective-permute-done.6
  192.0 5.1 %finish.3 = bf16[2,2,128,5120]{3,2,1,0:T(8,128)(2,1)} custom-call(s32[2]{0:T(128)S(1)} %pad_add_fusion.1.me, s16[2,16,2,176,128]{4,3,2,1,0:T(8,128)(2,1)S(1)} %bitcast.14, bf16[128,5120]{1,0:T(8,128)(2,1)S(1)} %collective-permute-done.7.mine, bf16[128,5120]{1,0:T(8,128)(2,1)S(1)} %collective-permute-done.8.theirs, ...), custom_call_target="tpu_custom_call", output_to_operand_aliasing={{}: (4, {})} | custom-call | tf_op jit(solution)/shard_map/finish/pallas_call | solution.py:359
  (9 shorter events, 0.0 us)
Async XLA Ops:
  0.7 1.2 copy-start
  9.9 9.5 %copy-start.11 = (s32[1,2,80,32]{2,3,1,0:T(8,128)S(1)}, s32[1,2,80,32]{2,3,1,0:T(8,128)}, u32[]{:S(2)}) copy-start(s32[1,2,80,32]{2,3,1,0:T(8,128)} %param.14) | copy-start | bytes 61444
  9.9 13.9 %copy-start.2 = (bf16[256,256]{1,0:T(8,128)(2,1)S(1)}, bf16[256,256]{1,0:T(8,128)(2,1)}, u32[]{:S(2)}) copy-start(bf16[256,256]{1,0:T(8,128)(2,1)} %constant.20.clone.rt) | copy-start | bytes 393220
  9.9 13.9 %copy-start.3 = (bf16[512,256]{1,0:T(8,128)(2,1)S(1)}, bf16[512,256]{1,0:T(8,128)(2,1)}, u32[]{:S(2)}) copy-start(bf16[512,256]{1,0:T(8,128)(2,1)} %constant.22.clone.lt) | copy-start | bytes 786436
  9.9 13.9 %copy-start.7 = (s32[2,8,128]{2,1,0:T(8,128)S(1)}, s32[2,8,128]{2,1,0:T(8,128)}, u32[]{:S(2)}) copy-start(s32[2,8,128]{2,1,0:T(8,128)} %constant.25.clone.tab) | copy-start | bytes 24580
  9.9 12.4 %collective-permute-start.2 = (f32[256,2560]{1,0:T(8,128)}, f32[256,2560]{1,0:T(8,128)S(1)}, u32[]{:S(2)}, u32[]{:S(2)}) collective-permute-start(f32[256,2560]{1,0:T(8,128)} %get-tuple-element.18), channel_id=1, source_target_pairs={{0,1},{1,0},{2,3},{3,2},{4,5},{5,4},{6,7},{7,6},{8,9},{9,8},{10,11... | collective-permute-start | bytes 7864328 | tf_op jit(solution)/shard_map/ppermute | solution.py:457
  19.4 12.5 %collective-permute-start = (f32[256,2560]{1,0:T(8,128)}, f32[256,2560]{1,0:T(8,128)}, u32[]{:S(2)}, u32[]{:S(2)}) collective-permute-start(f32[256,2560]{1,0:T(8,128)} %get-tuple-element.16), channel_id=1, source_target_pairs={{0,1},{1,0},{2,3},{3,2},{4,5},{5,4},{6,7},{7,6},{8,9},{9,8},{10,11... | collective-permute-start | bytes 7864328 | tf_op jit(solution)/shard_map/ppermute | solution.py:457
  19.5 2.8 %collective-permute-start.1 = (s32[2,32,128]{2,1,0:T(8,128)S(1)}, s32[2,32,128]{2,1,0:T(8,128)S(1)}, u32[]{:S(2)}, u32[]{:S(2)}) collective-permute-start(s32[2,32,128]{2,1,0:T(8,128)S(1)} %get-tuple-element.28), channel_id=1, source_target_pairs={{0,2},{2,0},{4,6},{6,4},{1,3},{3,1},{5,7},{7,5},{8,10},{10,8},{12,... | collective-permute-start | bytes 98312 | tf_op jit(solution)/shard_map/ppermute | solution.py:451
  22.3 1.5 copy-start.10
  30.9 1.1 copy-start.8
  32.0 31.9 %copy-start.4 = (bf16[256,256]{1,0:T(8,128)(2,1)S(1)}, bf16[256,256]{1,0:T(8,128)(2,1)}, u32[]{:S(2)}) copy-start(bf16[256,256]{1,0:T(8,128)(2,1)} %constant.21.clone.irt.rt) | copy-start | bytes 393220
  32.0 31.9 %copy-start.5 = (bf16[256,128]{1,0:T(8,128)(2,1)S(1)}, bf16[256,128]{1,0:T(8,128)(2,1)}, u32[]{:S(2)}) copy-start(bf16[256,128]{1,0:T(8,128)(2,1)} %constant.24.clone.ilt.lt) | copy-start | bytes 196612
  68.8 44.1 %copy-start.1 = (bf16[128,5120]{1,0:T(8,128)(2,1)S(1)}, bf16[128,5120]{1,0:T(8,128)(2,1)}, u32[]{:S(2)}) copy-start(bf16[128,5120]{1,0:T(8,128)(2,1)} %mine.1) | copy-start | bytes 3932164
  68.8 93.4 %copy-start.6 = (bf16[256,128]{1,0:T(8,128)(2,1)S(1)}, bf16[256,128]{1,0:T(8,128)(2,1)}, u32[]{:S(2)}) copy-start(bf16[256,128]{1,0:T(8,128)(2,1)} %constant.23.clone.lt) | copy-start | bytes 196612
  68.8 93.4 %copy-start.9 = (f32[128,2560]{1,0:T(8,128)S(1)}, f32[128,2560]{1,0:T(8,128)}, u32[]{:S(2)}) copy-start(f32[128,2560]{1,0:T(8,128)} %copy-done.8) | copy-start | bytes 3932164
  108.0 84.0 %collective-permute-start.6 = (s16[64,176,128]{2,1,0:T(8,128)(2,1)S(1)}, s16[64,176,128]{2,1,0:T(8,128)(2,1)S(1)}, u32[]{:S(2)}, u32[]{:S(2)}) collective-permute-start(s16[64,176,128]{2,1,0:T(8,128)(2,1)S(1)} %all_to_all.11), channel_id=1, source_target_pairs={{0,1},{1,0},{2,3},{3,2},{4,5},{5,4},{6,7},{7,6},{8,9},{9,8},{10,11... | collective-permute-start | bytes 8650760 | tf_op jit(solution)/shard_map/ppermute | solution.py:472
  112.9 31.6 %collective-permute-start.5 = (bf16[128,5120]{1,0:T(8,128)(2,1)S(1)}, bf16[128,5120]{1,0:T(8,128)(2,1)S(1)}, u32[]{:S(2)}, u32[]{:S(2)}) collective-permute-start(bf16[128,5120]{1,0:T(8,128)(2,1)S(1)} %copy-done.1), channel_id=1, source_target_pairs={{0,6},{2,4},{4,2},{6,0},{1,7},{3,5},{5,3},{7,1},{8,14},{10,12},{12... | collective-permute-start | bytes 3932168 | tf_op jit(solution)/shard_map/ppermute | solution.py:453
  113.8 78.2 %collective-permute-start.7 = (bf16[128,5120]{1,0:T(8,128)(2,1)S(1)}, bf16[128,5120]{1,0:T(8,128)(2,1)S(1)}, u32[]{:S(2)}, u32[]{:S(2)}) collective-permute-start(bf16[128,5120]{1,0:T(8,128)(2,1)S(1)} %copy-done.1), channel_id=1, source_target_pairs={{0,1},{1,0},{2,3},{3,2},{4,5},{5,4},{6,7},{7,6},{8,9},{9,8},{10,11... | collective-permute-start | bytes 3932168 | tf_op jit(solution)/shard_map/ppermute | solution.py:470
  144.5 47.5 %collective-permute-start.8 = (bf16[128,5120]{1,0:T(8,128)(2,1)S(1)}, bf16[128,5120]{1,0:T(8,128)(2,1)S(1)}, u32[]{:S(2)}, u32[]{:S(2)}) collective-permute-start(bf16[128,5120]{1,0:T(8,128)(2,1)S(1)} %collective-permute-done.5.theirs), channel_id=1, source_target_pairs={{0,1},{1,0},{2,3},{3,2},{4,5},{5,4},{6,7},{7,6},{8,9},{9,8},{10,11... | collective-permute-start | bytes 3932168 | tf_op jit(solution)/shard_map/ppermute | solution.py:471
  145.3 16.9 %collective-permute-start.4 = (s16[4,656,128]{2,1,0:T(8,128)(2,1)}, s16[4,656,128]{2,1,0:T(8,128)(2,1)S(1)}, u32[]{:S(2)}, u32[]{:S(2)}) collective-permute-start(s16[4,656,128]{2,1,0:T(8,128)(2,1)} %get-tuple-element.22), channel_id=1, source_target_pairs={{0,2},{2,0},{4,6},{6,4},{1,3},{3,1},{5,7},{7,5},{8,10},{10,8},{12,... | collective-permute-start | bytes 2015240 | tf_op jit(solution)/shard_map/ppermute | solution.py:461
  145.3 31.3 %collective-permute-start.3 = (s16[4,656,128]{2,1,0:T(8,128)(2,1)}, s16[4,656,128]{2,1,0:T(8,128)(2,1)S(1)}, u32[]{:S(2)}, u32[]{:S(2)}) collective-permute-start(s16[4,656,128]{2,1,0:T(8,128)(2,1)} %get-tuple-element.20), channel_id=1, source_target_pairs={{0,2},{2,0},{4,6},{6,4},{1,3},{3,1},{5,7},{7,5},{8,10},{10,8},{12,... | collective-permute-start | bytes 2015240 | tf_op jit(solution)/shard_map/ppermute | solution.py:461

commit v2 on v1

v2 whole, which is shorter than its diff:
```python
import functools
import math

import jax
import jax.numpy as jnp
import numpy as np
from jax import lax
from jax.experimental import pallas as pl
from jax.experimental.pallas import tpu as pltpu
from jax.sharding import Mesh
from jax.sharding import PartitionSpec as P

KEEP = 16
DECAY = 0.9
STEP = 0.5
PARTS = 2
PAIRS = 8
PER = PAIRS // PARTS
GW = 640
LEFT = 2
QROWS = 656
UROWS = 176
F32 = jnp.float32
BF16 = jnp.bfloat16
I16 = jnp.int16
I32 = jnp.int32
ARB = pltpu.CompilerParams(vmem_limit_bytes=20 * 1024 * 1024)


def cosine():
    k = np.arange(64, dtype=np.float64)[:, None]
    i = np.arange(64, dtype=np.float64)[None, :]
    w = np.where(k == 0, math.sqrt(1.0 / 64), math.sqrt(2.0 / 64))
    return w * np.cos(math.pi * (2.0 * i + 1.0) * k / 128.0)


def halves(m):
    hi = m.astype(np.float32).astype(jnp.bfloat16)
    lo = (m - hi.astype(np.float64)).astype(np.float32).astype(jnp.bfloat16)
    return hi, lo


def diag(m, n):
    return np.kron(np.eye(n), m)


def right_table(m):
    hi, lo = halves(m)
    row = np.concatenate([hi, lo], axis=1)
    return np.concatenate([row, row], axis=0)


def left_table(m):
    return np.concatenate(halves(m), axis=0)


def split(x):
    hi = x.astype(BF16)
    return hi, (x - hi.astype(F32)).astype(BF16)


def mul_right(x, table):
    hi, lo = split(x)
    o = jnp.dot(jnp.concatenate([hi, lo], axis=1), table, preferred_element_type=F32)
    return o[:, :128] + o[:, 128:]


def mul_left(table, x):
    n = table.shape[0] // 2
    hi, lo = split(x)
    o = jnp.dot(table, hi, preferred_element_type=F32)
    return o[:n] + o[n:] + jnp.dot(table[:n], lo, preferred_element_type=F32)


def lanes_of(x, idx):
    return jnp.take_along_axis(x, jnp.broadcast_to(idx, x.shape), axis=1, mode="promise_in_bounds")


def rows_of(x, idx):
    return jnp.take_along_axis(x, idx, axis=0, mode="promise_in_bounds")


def lane(shape):
    return lax.broadcasted_iota(I32, shape, len(shape) - 1)


def sub(shape):
    return lax.broadcasted_iota(I32, shape, 0)


def pow2(e):
    n = e + 100
    r = jnp.full(e.shape, 2.0**-100, F32)
    for bit in range(7):
        r = r * jnp.where((n >> bit) & 1 == 1, 2.0 ** (1 << bit), 1.0)
    r = r * jnp.where((n >> 7) & 1 == 1, 2.0**64, 1.0)
    return r * jnp.where((n >> 7) & 1 == 1, 2.0**64, 1.0)


def exponent(top):
    e = jnp.floor(math.log2(32767.0) - jnp.log(jnp.maximum(top, 1e-35)) * (1 / math.log(2)))
    return jnp.clip(e, -60.0, 99.0).astype(I32)


def coded(x, e):
    v = jnp.floor(x * pow2(e) + 0.5)
    return jnp.clip(v, -32767.0, 32767.0).astype(I32).astype(I16)


def value(q, e):
    return q.astype(I32).astype(F32) * pow2(-e)


def term(hidden, grad, part):
    cols = 5120 // PARTS
    right = lax.slice_in_dim(grad, part * cols, (part + 1) * cols, axis=1)
    return lax.dot_general(hidden, right, (((0,), (0,)), ((), ())), preferred_element_type=F32)


def rows_for(hidden, core):
    yl = lax.axis_index("yl")
    own = lax.dynamic_slice_in_dim(hidden, 128 * (2 * yl + core), 128, axis=1)
    far = lax.dynamic_slice_in_dim(hidden, 128 * (2 * (1 - yl) + core), 128, axis=1)
    return jnp.concatenate([own, far], axis=1)


def place(group, pos):
    return pos if group == 0 else 5 + (pos + 1) % 5


def pick_tables():
    t = np.zeros((2, 8, 128), np.int32)
    for g in range(2):
        for ln in range(128):
            pos = min(ln // 16, 4) if ln < 80 else (ln - 80) % 5
            t[g, 0, ln] = place(g, pos)
            t[g, 1, ln] = 64 * (place(g, pos) % 2) if ln < 80 else 0
    return t


def code_kernel(own, got, q):
    x = (own[...] + got[...]) * (1.0 / 64)
    for p in range(LEFT):
        exps = jnp.zeros((16, 128), I32)
        for t in range(5):
            at = GW * p + 128 * t
            v = x[:, at : at + 128]
            e = exponent(jnp.max(jnp.abs(v), axis=0, keepdims=True))
            q[p, 128 * t : 128 * t + 128, :] = coded(v, e)
            exps = jnp.where(sub((16, 128)) == t, jnp.broadcast_to(e, (16, 128)), exps)
        q[p, 640:656, :] = exps.astype(I16)


def code(own, got):
    spec = pl.BlockSpec((128, LEFT * GW), lambda i: (1, i))
    return pl.pallas_call(
        code_kernel,
        grid=(PER // LEFT,),
        in_specs=[spec, spec],
        out_specs=pl.BlockSpec((LEFT, QROWS, 128), lambda i: (i, 0, 0)),
        out_shape=jax.ShapeDtypeStruct((PER, QROWS, 128), I16),
        compiler_params=ARB,
        cost_estimate=pl.CostEstimate(flops=10**7, bytes_accessed=4 * 2**20, transcendentals=0),
        name="code",
    )(own, got)


def compress_kernel(part, me, own, got, mom, picks, tab, rt, lt, *refs):
    pm, comp = refs[-2:]
    yl = me[0]
    first = 10 * (PER * part + pl.program_id(0))
    ln = lane((1, 128))
    w0 = (own[:128] + got[:128]) * (1.0 / 64) + DECAY * mom[0]
    w1 = (own[128:] + got[128:]) * (1.0 / 64)
    pm[...] = w0
    tiles = []
    for t in range(5):
        tiles += [w0[:, 128 * t : 128 * t + 128], w1[:, 128 * t : 128 * t + 128]]
    o = mul_right(jnp.concatenate(tiles, axis=0), rt[...])
    tiles = [o[256 * t : 256 * t + 256] for t in range(5)]
    u16 = sub((16, 128))
    ln16 = lane((16, 128))
    short = []
    for g in range(2):
        pieces = []
        span = first + tab[g, 0:1, :]
        for rb in range(4):
            qt = picks[rb // 2, rb % 2, 16:32, :]
            chosen = jnp.where(u16 == (ln16 & 15), lanes_of(qt, span), 0)
            idx = jnp.sum(chosen, axis=0, keepdims=True) + tab[g, 1:2, :]
            rows = slice(64 * rb, 64 * rb + 64)
            a = lanes_of(tiles[3 * g][rows], idx)
            b = lanes_of(tiles[3 * g + 1][rows], idx)
            c = lanes_of(tiles[2][rows], idx)
            pieces.append(jnp.where(ln < 32, a, jnp.where(ln < 64, b, c)))
        short.append(jnp.concatenate(pieces, axis=0))
    z = mul_left(lt[...], jnp.concatenate(short, axis=1))
    for g in range(2):
        span = first + tab[g, 0:1, :]
        for rb in range(4):
            rel, a = rb // 2, rb % 2
            to = yl if rel == 0 else 1 - yl
            pt = picks[rel, a, 0:16, :]
            qt = picks[rel, a, 16:32, :]
            pidx, qidx = lanes_of(pt, span), lanes_of(qt, span)
            for h in range(2):
                pi = pidx[8 * h : 8 * h + 8]
                low, high = pi & 7, pi >> 3
                acc = jnp.where(ln < 85, pi, qidx[8 * h : 8 * h + 8]).astype(F32)
                for j in range(8):
                    r = 64 * rb + 8 * j
                    v = rows_of(z[r : r + 8, 128 * g : 128 * g + 128], low)
                    acc = jnp.where((high == j) & (ln < 80), v, acc)
                comp[a, g, to, 8 * h : 8 * h + 8, :] = acc


def compress(part, me, own, got, mom, picks, tab, rt, lt, before):
    n = PER
    full = lambda *s: pl.BlockSpec(s, lambda i, me: (0,) * len(s))
    col = lambda r: pl.BlockSpec((r, GW), lambda i, me: (0, i))
    args = [own, got, mom, picks, tab, rt, lt]
    in_specs = [
        col(256),
        col(256),
        pl.BlockSpec((1, 128, GW), lambda i, me: (0, 0, part * n + i)),
        full(2, 2, 32, 128),
        full(2, 8, 128),
        full(256, 256),
        full(512, 256),
    ]
    alias = {}
    if before is not None:
        args.append(before)
        in_specs.append(pl.BlockSpec(memory_space=pl.ANY))
        alias = {8: 1}
    return pl.pallas_call(
        functools.partial(compress_kernel, part),
        grid_spec=pltpu.PrefetchScalarGridSpec(
            num_scalar_prefetch=1,
            grid=(n,),
            in_specs=in_specs,
            out_specs=[
                col(128),
                pl.BlockSpec((2, 2, 2, 16, 128), lambda i, me: (0, part * n + i, 0, 0, 0)),
            ],
        ),
        out_shape=[
            jax.ShapeDtypeStruct((128, 5120 // PARTS), F32),
            jax.ShapeDtypeStruct((2, 16, 2, 16, 128), F32),
        ],
        input_output_aliases=alias,
        compiler_params=ARB,
        cost_estimate=pl.CostEstimate(flops=2 * 10**9, bytes_accessed=9 * 2**20, transcendentals=0),
        name="compress",
    )(me, *args)


def owner_kernel(got, rt, lt, out, xh, xl, hot):
    ln16 = lane((16, 128))

    here = (ln16 & 63).astype(F32)
    u16 = sub((16, 128))

    def one(n, _):
        at = pl.multiple_of(16 * n, 16)
        x = got[n]
        for t in range(3):
            half = 2 * t + (ln16 >> 6)
            hit = jnp.where(lanes_of(x, 85 + half) == here, 16 * half + u16 + 1, 0)
            if t == 2:
                hit = jnp.where(ln16 < 64, hit, 0)
            idx = jnp.broadcast_to(jnp.sum(hit, axis=0, keepdims=True), (16, 128)) - 1
            v = jnp.where(idx >= 0, lanes_of(x, jnp.maximum(idx, 0)), 0.0)
            hi, lo = split(v)
            xh[t, pl.ds(at, 16), :] = hi
            xl[t, pl.ds(at, 16), :] = lo
            hot[t, pl.ds(at, 16), :] = jnp.where(lanes_of(x, 80 + half) == here, 1.0, 0.0).astype(BF16)
        return 0

    lax.fori_loop(0, got.shape[0], one, 0, unroll=4)
    same = (sub((128, 128)) >> 6) == (lane((128, 128)) >> 6)
    tiles = []
    for t in range(3):
        dims = (((0,), (0,)), ((), ()))
        d = lax.dot_general(hot[t], xh[t], dims, preferred_element_type=F32)
        d = d + lax.dot_general(hot[t], xl[t], dims, preferred_element_type=F32)
        d = jnp.where(same, d, 0.0)
        u = mul_left(lt[...], mul_right(d, rt[...]))
        tiles.append(u[:64] + u[64:])
    last = tiles[2]
    ln = lane((32, 128))
    tiles[2] = jnp.where(ln < 64, last[:32], jnp.roll(last[32:], 64, axis=1))
    x = jnp.concatenate(tiles, axis=0)
    e = exponent(jnp.max(jnp.abs(x), axis=0, keepdims=True))
    out[0:160, :] = coded(x, e)
    out[160:176, :] = jnp.broadcast_to(e, (16, 128)).astype(I16)


def owner(got, rt, lt):
    return pl.pallas_call(
        owner_kernel,
        out_shape=jax.ShapeDtypeStruct((UROWS, 128), I16),
        scratch_shapes=[pltpu.VMEM((3, 1024, 128), BF16)] * 3,
        compiler_params=ARB,
        name="owner",
    )(got, rt, lt)


def decode(ref, pair):
    group = []
    for g in (2 * pair, 2 * pair + 1):
        e = ref[g, 160:176, :].astype(I32)[:1]
        group.append(value(ref[g, 0:160, :], e))
    even, odd = group
    lo = lane((32, 128)) < 64
    e2, o2 = even[128:160], odd[128:160]
    top = jnp.where(lo, e2, jnp.roll(o2, 64, axis=1))
    bottom = jnp.where(lo, jnp.roll(e2, 64, axis=1), o2)
    return [even[:64], even[64:128], jnp.concatenate([top, bottom], axis=0), odd[:64], odd[64:128]]


def finish_kernel(with_update, _, got0, got1, par, *refs):
    for a, got in enumerate((got0, got1)):
        rows = slice(64 * a, 64 * a + 64)
        for pair in range(LEFT):
            for t, u in enumerate(decode(got, pair)):
                cols = slice(GW * pair + 128 * t, GW * pair + 128 * t + 128)
                if with_update:
                    refs[-2][rows, cols] = u
                refs[-1][rows, cols] = (par[rows, cols].astype(F32) - STEP * u).astype(BF16)


def finish(row, got0, got1, par, before):
    with_update = before is None
    col = pl.BlockSpec((128, LEFT * GW), lambda i, row: (0, i))
    blocks = pl.BlockSpec((2 * LEFT, UROWS, 128), lambda i, row: (i, 0, 0))
    args = [got0, got1, par]
    in_specs = [blocks, blocks, col]
    out_specs = [pl.BlockSpec((128, LEFT * GW), lambda i, row: (row[0], i))]
    out_shape = [jax.ShapeDtypeStruct((512, 5120), BF16)]
    alias = {}
    if with_update:
        out_specs.insert(0, col)
        out_shape.insert(0, jax.ShapeDtypeStruct((128, 5120), F32))
    else:
        args.append(before)
        in_specs.append(pl.BlockSpec(memory_space=pl.ANY))
        alias = {4: 0}
    return pl.pallas_call(
        functools.partial(finish_kernel, with_update),
        grid_spec=pltpu.PrefetchScalarGridSpec(
            num_scalar_prefetch=1, grid=(PAIRS // LEFT,), in_specs=in_specs, out_specs=out_specs
        ),
        out_shape=out_shape,
        input_output_aliases=alias,
        compiler_params=ARB,
        cost_estimate=pl.CostEstimate(flops=10**7, bytes_accessed=4 * 2**20, transcendentals=0),
        name="finish",
    )(row, *args)


def left_kernel(part, q, pm, picks, rt, lt, irt, ilt, *refs):
    out, mask = refs[-2:]
    first = 10 * (PER * part + LEFT * pl.program_id(0))

    @pl.when(pl.program_id(0) == 0)
    def _():
        for a in range(2):
            k = sub((64, 128))
            hit = jnp.zeros((64, 128), F32)
            for u in range(16):
                hit = jnp.where(picks[0, a, u : u + 1, :] == k, 1.0, hit)
            mask[64 * a : 64 * a + 64, :] = hit

    ln16 = lane((16, 128))
    rows = sub((128, 128)) < 64
    moment, keep = [], []
    for t in range(5 * LEFT):
        e = q[t // 5, 640:656, :].astype(I32)[t % 5 : t % 5 + 1]
        at = 128 * (t % 5)
        moment.append(pm[:, 128 * t : 128 * t + 128] + value(q[t // 5, at : at + 128, :], e))
        span = first + 2 * t + (lane((1, 128)) >> 6)
        both = []
        for a in range(2):
            hit = lanes_of(picks[0, a, 16:32, :], span) == (ln16 & 63)
            both.append(jnp.max(jnp.where(hit, 1.0, 0.0), axis=0, keepdims=True))
        keep.append(lanes_of(mask[...], span) * jnp.where(rows, both[0], both[1]))
    n = len(moment)
    c = mul_right(jnp.concatenate(moment, axis=0), rt[...])
    c = mul_left(lt[...], jnp.concatenate([c[128 * t : 128 * t + 128] for t in range(n)], axis=1))
    c = mul_left(ilt[...], c * jnp.concatenate(keep, axis=1))
    r = mul_right(jnp.concatenate([c[:, 128 * t : 128 * t + 128] for t in range(n)], axis=0), irt[...])
    for t in range(n):
        out[0, :, 128 * t : 128 * t + 128] = moment[t] - r[128 * t : 128 * t + 128]


def left(part, q, pm, picks, rt, lt, irt, ilt, before):
    n = PER // LEFT
    full = lambda *s: pl.BlockSpec(s, lambda i: (0,) * len(s))
    args = [q, pm, picks, rt, lt, irt, ilt]
    in_specs = [
        pl.BlockSpec((LEFT, QROWS, 128), lambda i: (i, 0, 0)),
        pl.BlockSpec((128, LEFT * GW), lambda i: (0, i)),
        full(2, 2, 32, 128),
        full(256, 256),
        full(256, 128),
        full(256, 256),
        full(256, 128),
    ]
    alias = {}
    if before is not None:
        args.append(before)
        in_specs.append(pl.BlockSpec(memory_space=pl.ANY))
        alias = {7: 0}
    return pl.pallas_call(
        functools.partial(left_kernel, part),
        grid=(n,),
        in_specs=in_specs,
        out_specs=pl.BlockSpec((1, 128, LEFT * GW), lambda i: (0, 0, part * n + i)),
        out_shape=jax.ShapeDtypeStruct((1, 128, 5120), F32),
        scratch_shapes=[pltpu.VMEM((128, 128), F32)],
        input_output_aliases=alias,
        compiler_params=ARB,
        cost_estimate=pl.CostEstimate(flops=2 * 10**9, bytes_accessed=4 * 2**20, transcendentals=0),
        name="left",
    )(*args)


REP = ("x", "z", "yh")
NEAR = [(2 * h + k, 2 * h + 1 - k) for h in range(2) for k in range(2)]
FAR = [(y, 3 - y) for y in range(4)]
SWAP = [(0, 1), (1, 0)]


def body(hidden, grad, momentum, coef_picks, params):
    c = cosine()
    rt = jnp.asarray(right_table(diag(c.T, 2)))
    irt = jnp.asarray(right_table(diag(c, 2)))
    lt4 = jnp.asarray(left_table(diag(c, 4)))
    lt = jnp.asarray(left_table(diag(c, 2)))
    ilt = jnp.asarray(left_table(diag(c.T, 2)))
    tab = jnp.asarray(pick_tables())
    me = jnp.stack([lax.axis_index("yl"), lax.axis_index("c")]).astype(I32)

    mine = jnp.pad(coef_picks[0].swapaxes(1, 2), ((0, 0), (0, 0), (0, 48)))
    theirs = lax.ppermute(mine, ("yh", "yl"), NEAR)
    picks = jnp.stack([mine, theirs])
    far_params = lax.ppermute(params, ("yh", "yl"), FAR)

    core = lax.axis_index("c")
    sent = rows_for(hidden, 1 - core)
    kept = rows_for(hidden, core)
    swapped = [lax.ppermute(term(sent, grad, part), "c", SWAP) for part in range(PARTS)]
    own = [term(kept, grad, part) for part in range(PARTS)]
    qs = [lax.ppermute(code(own[p], swapped[p]), ("yh", "yl"), NEAR) for p in range(PARTS)]
    pms, comp = [], None
    for part in range(PARTS):
        pm, comp = compress(part, me, own[part], swapped[part], momentum, picks, tab, rt, lt4, comp)
        pms.append(pm)
    comp, qs[0] = lax.optimization_barrier((comp, qs[0]))
    got = lax.all_to_all(comp.reshape(64, 16, 128), REP + ("yl",), 0, 0, tiled=True)
    first_left = left(0, qs[0], pms[0], picks, rt, lt, irt, ilt, None)
    got, first_left = lax.optimization_barrier((got, first_left))
    mine16 = owner(got, irt, ilt)
    other_params = lax.ppermute(params, "c", SWAP)
    mine16, qs[1], far_params, other_params = lax.optimization_barrier((mine16, qs[1], far_params, other_params))
    other_far = lax.ppermute(far_params, "c", SWAP)
    every = lax.all_to_all(jnp.broadcast_to(mine16, (32, UROWS, 128)), REP, 0, 0, tiled=True)

    block = [every[:16], every[16:]]
    far = [lax.ppermute(v, ("yh", "yl"), way) for v, way in zip(block, (NEAR, FAR))]
    other = [lax.ppermute(v, "c", SWAP) for v in block]
    momentum_left = left(1, qs[1], pms[1], picks, rt, lt, irt, ilt, first_left)
    row = lambda y, c: (2 * y + c).astype(I32).reshape(1)
    yl = lax.axis_index("yl")
    update, new = finish(row(yl, core), *block, params, None)
    (new,) = finish(row(yl, 1 - core), *other, other_params, new)
    far, new, momentum_left = lax.optimization_barrier((far, new, momentum_left))
    other_distant = [lax.ppermute(v, "c", SWAP) for v in far]
    (new,) = finish(row(1 - yl, core), *far, far_params, new)
    (new,) = finish(row(1 - yl, 1 - core), *other_distant, other_far, new)
    return momentum_left, update, new


def solution(mesh):
    fine = Mesh(mesh.devices.reshape(4, 4, 2, 2, 2), ("x", "z", "yh", "yl", "c"))
    rep, fsdp = ("x", "z", "yh"), ("yl", "c")
    return jax.shard_map(
        body,
        mesh=fine,
        in_specs=(
            P(rep + fsdp, None),
            P(rep + fsdp, None),
            P(rep, fsdp, None),
            P(rep, fsdp, None, None),
            P(fsdp, None),
        ),
        out_specs=(P(rep, fsdp, None), P(fsdp, None), P()),
        check_vma=False,
    )
```

time: 198 us -> 119 us (0.60)
  waiting for transfers between devices: 51.7 us -> 9.53 us
  blocking collectives: 63.9 us -> 26.1 us
  Pallas kernels: 65.2 us -> 40.6 us
  starting transfers between devices: 11.3 us -> 24.9 us
  matrix products: 0 us -> 8.94 us
  local copies, waits for them, and re-layouts: 4.19 us -> 8.01 us
    all_to_all x2 -> x1, blocking collectives: 63.9 us -> 26.1 us  [body(): lax.all_to_all(jnp.broadcast_to(mine16, (32, UROWS, 128)), REP, 0, 0, til...]
    ppermute x1, waiting for transfers between devices: 30.5 us -> 0.01 us  [body(): far_params = lax.ppermute(params, ('yh', 'yl'), FAR)]
    ppermute x5 -> x10, waiting for transfers between devices: 19.9 us -> 5.51 us  [the longest x2 5.03 us: body(): lax.ppermute(v, ('yh', 'yl'), way)]
    pallas_call x2, Pallas kernels: 16 us -> 2.5 us  [code(): pl.pallas_call(code_kernel, grid=(PER // LEFT,), in_specs=[spec, spec], o...]
    all_to_all x0 -> x1, starting transfers between devices: none -> 11 us  [body(): lax.all_to_all(comp.reshape(64, 16, 128), REP + ('yl',), 0, 0, tiled=True)]
    pallas_call x2, Pallas kernels: 20 us -> 9.08 us  [left(): pl.pallas_call(functools.partial(left_kernel, part), grid=(n,), in_specs=...]
    dot_general x0 -> x4, matrix products: none -> 8.94 us  [term(): lax.dot_general(hidden, right, (((0,), (0,)), ((), ())), preferred_elemen...]
    all_to_all x0 -> x1, waiting for transfers between devices: none -> 4.02 us  [body(): lax.all_to_all(comp.reshape(64, 16, 128), REP + ('yl',), 0, 0, tiled=True)]
  transfers between devices with their start and end apart: 9 -> 15, of which waited for: 4 -> 4; matrix products, arithmetic and copies ran while one was open for 0% -> 4% of each run, Pallas kernels for 20% -> 32%
where the time goes in v2:
time: 119 us
  Pallas kernels  40.6 us (34%)
  blocking collectives  26.1 us (22%)
  starting transfers between devices  24.9 us (21%)
  waiting for transfers between devices  9.53 us (8%)
  matrix products  8.94 us (8%)
  local copies, waits for them, and re-layouts  8.01 us (7%)
    all_to_all x1, blocking collectives, body(): lax.all_to_all(jnp.broadcast_to(mine16, (32, UROWS, 128)), REP, 0, 0, til...  26.1 us
    pallas_call x4, Pallas kernels, finish(): pl.pallas_call(functools.partial(finish_kernel, with_update), grid_spec=p...  11.6 us
    pallas_call x2, Pallas kernels, compress(): pl.pallas_call(functools.partial(compress_kernel, part), grid_spec=pltpu....  11.4 us
    all_to_all x1, starting transfers between devices, body(): lax.all_to_all(comp.reshape(64, 16, 128), REP + ('yl',), 0, 0, tiled=True)  11 us
    pallas_call x2, Pallas kernels, left(): pl.pallas_call(functools.partial(left_kernel, part), grid=(n,), in_specs=...  9.08 us
    dot_general x4, matrix products, term(): lax.dot_general(hidden, right, (((0,), (0,)), ((), ())), preferred_elemen...  8.94 us
    unnamed x32, local copies, waits for them, and re-layouts  6.28 us
    pallas_call x1, Pallas kernels, owner(): pl.pallas_call(owner_kernel, out_shape=jax.ShapeDtypeStruct((UROWS, 128),...  6.06 us
  transfers between devices with their start and end apart: 15, of which 4 were waited for; matrix products, arithmetic and copies ran while one was open for 4% of the time, Pallas kernels for 32%

profile of v2, /device:TPU:1, one launch (start us, length us, event | category | flops | bytes accessed | tf_op | source)
XLA Modules:
  0.0 119.0 jit_solution(9608638394072251733)
XLA Ops:
  0.7 1.4 %constant_dynamic-slice_fusion.1 = (bf16[1024,128]{1,0:T(8,128)(2,1)S(1)}, bf16[1024,128]{1,0:T(8,128)(2,1)S(1)}, bf16[1024,128]{1,0:T(8,128)(2,1)S(1)}, bf16[1024,128]{1,0:T(8,128)(2,1)S(1)}) fusion(bf16[1024,512]{1,0:T(8,128)(2,1)} %param.11, s32[]{:T(128)S(6)} %select_n.14, s32[]{:T(128)S(6)} %select_n.13, s32[]{:T(128)S(6)} %select_n.12, s32[]{:T(128)S(6)} %select_n.15), kind=kLoop, calls=%fused_computation.12 | loop fusion | bytes 2097168 | tf_op jit(solution)/shard_map/dynamic_slice | solution.py:122
  2.1 4.3 %fusion = f32[256,2560]{1,0:T(8,128)S(1)} fusion(bf16[1024,5120]{1,0:T(8,128)(2,1)} %param.12, bf16[1024,128]{1,0:T(8,128)(2,1)S(1)} %get-tuple-element.44, bf16[1024,128]{1,0:T(8,128)(2,1)S(1)} %get-tuple-element.41), kind=kOutput, calls=%fused_computation | convolution fusion | flops 1343225856 | bytes 8388608 | tf_op jit(solution)/shard_map/dot_general | solution.py:117
  6.4 1.5 %collective-permute-start.2 = (f32[256,2560]{1,0:T(8,128)S(1)}, f32[256,2560]{1,0:T(8,128)S(1)}, u32[]{:S(2)}, u32[]{:S(2)}) collective-permute-start(f32[256,2560]{1,0:T(8,128)S(1)} %fusion), channel_id=1, source_target_pairs={{0,1},{1,0},{2,3},{3,2},{4,5},{5,4},{6,7},{7,6},{8,9},{9,8},{10,11... | collective-permute-start | bytes 7864328 | tf_op jit(solution)/shard_map/ppermute | solution.py:453
  7.9 1.6 %fusion.4 = f32[256,2560]{1,0:T(8,128)S(1)} fusion(bf16[1024,5120]{1,0:T(8,128)(2,1)S(1)} %copy-done.15, bf16[1024,128]{1,0:T(8,128)(2,1)S(1)} %get-tuple-element.44, bf16[1024,128]{1,0:T(8,128)(2,1)S(1)} %get-tuple-element.41), kind=kOutput, calls=%fused_computation.4 | convolution fusion | flops 1343225856 | bytes 8388608 | tf_op jit(solution)/shard_map/dot_general | solution.py:117
  9.5 0.1 collective-permute-start
  9.6 2.9 %collective-permute-start.5 = (bf16[128,5120]{1,0:T(8,128)(2,1)}, bf16[128,5120]{1,0:T(8,128)(2,1)S(1)}, u32[]{:S(2)}, u32[]{:S(2)}) collective-permute-start(bf16[128,5120]{1,0:T(8,128)(2,1)} %par.1), channel_id=1, source_target_pairs={{0,6},{2,4},{4,2},{6,0},{1,7},{3,5},{5,3},{7,1},{8,14},{10,12},{12... | collective-permute-start | bytes 3932168 | tf_op jit(solution)/shard_map/ppermute | solution.py:448
  12.5 0.7 collective-permute-start.6
  13.2 0.1 collective-permute-start.1
  13.3 1.5 %fusion.2.own = f32[256,2560]{1,0:T(8,128)S(1)} fusion(bf16[1024,5120]{1,0:T(8,128)(2,1)S(1)} %copy-done.15, bf16[1024,128]{1,0:T(8,128)(2,1)S(1)} %get-tuple-element.42, bf16[1024,128]{1,0:T(8,128)(2,1)S(1)} %get-tuple-element.43), kind=kOutput, calls=%fused_computation.2 | convolution fusion | flops 1343225856 | bytes 8388608 | tf_op jit(solution)/shard_map/dot_general | solution.py:117
  14.8 0.9 code.2
  15.7 1.5 %collective-permute-start.3 = (s16[4,656,128]{2,1,0:T(8,128)(2,1)S(1)}, s16[4,656,128]{2,1,0:T(8,128)(2,1)S(1)}, u32[]{:S(2)}, u32[]{:S(2)}) collective-permute-start(s16[4,656,128]{2,1,0:T(8,128)(2,1)S(1)} %code.2), channel_id=1, source_target_pairs={{0,2},{2,0},{4,6},{6,4},{1,3},{3,1},{5,7},{7,5},{8,10},{10,8},{12,... | collective-permute-start | bytes 2015240 | tf_op jit(solution)/shard_map/ppermute | solution.py:455
  17.3 1.5 %fusion.6.own = f32[256,2560]{1,0:T(8,128)S(1)} fusion(bf16[1024,5120]{1,0:T(8,128)(2,1)S(1)} %copy-done.15, bf16[1024,128]{1,0:T(8,128)(2,1)S(1)} %get-tuple-element.42, bf16[1024,128]{1,0:T(8,128)(2,1)S(1)} %get-tuple-element.43), kind=kOutput, calls=%fused_computation.6 | convolution fusion | flops 1343225856 | bytes 8388608 | tf_op jit(solution)/shard_map/dot_general | solution.py:117
  18.8 0.1 pad_add_fusion.1.me
  18.9 0.0 copy-start.4
  18.9 0.0 copy-start.9
  19.0 1.6 %code.3 = s16[4,656,128]{2,1,0:T(8,128)(2,1)} custom-call(f32[256,2560]{1,0:T(8,128)S(1)} %fusion.6.own, f32[256,2560]{1,0:T(8,128)S(1)} %collective-permute-done.got), custom_call_target="tpu_custom_call" | custom-call | flops 10000000 | bytes 4194304 | tf_op jit(solution)/shard_map/code/pallas_call | solution.py:156
  20.6 0.5 collective-permute-start.4
  21.1 5.7 %compress.2 = (f32[128,2560]{1,0:T(8,128)S(1)}, f32[2,16,2,16,128]{4,3,2,1,0:T(8,128)}) custom-call(s32[2]{0:T(128)S(1)} %pad_add_fusion.1.me, f32[256,2560]{1,0:T(8,128)S(1)} %fusion.2.own, f32[256,2560]{1,0:T(8,128)S(1)} %collective-permute-done.2.got, f32[1,128,5120]{2,1,0:T(8,128)S(1)} %copy-done, s32[2,2,32,128]{3,2,1,0:T(8,128)S(1)} %pad_add_fusion.picks, ...), custom_call_target="tpu_custom_call" | custom-call | flops 2000000000 | bytes 9437184 | tf_op jit(solution)/shard_map/compress/pallas_call | solution.py:236
  26.8 1.1 copy-done.10
  27.8 5.7 %compress.3 = (f32[128,2560]{1,0:T(8,128)S(1)}, f32[2,16,2,16,128]{4,3,2,1,0:T(8,128)}) custom-call(s32[2]{0:T(128)S(1)} %pad_add_fusion.1.me, f32[256,2560]{1,0:T(8,128)S(1)} %fusion.6.own, f32[256,2560]{1,0:T(8,128)S(1)} %collective-permute-done.got, f32[1,128,5120]{2,1,0:T(8,128)S(1)} %copy-done, ...), custom_call_target="tpu_custom_call", output_to_operand_aliasing={{1}: (8, {})} | custom-call | flops 2000000000 | bytes 9437184 | tf_op jit(solution)/shard_map/compress/pallas_call | solution.py:236
  33.5 1.1 copy-done.1
  34.6 0.9 copy-done.12
  35.5 11.0 %all-to-all-start = ((f32[64,16,128]{2,1,0:T(8,128)}), f32[64,16,128]{2,1,0:T(8,128)S(1)}, u32[]{:S(2)}, u32[]{:S(2)}) async-start(f32[64,16,128]{2,1,0:T(8,128)} %bitcast.6), calls=%async_computation | async-start | bytes 1048576 | tf_op jit(solution)/shard_map/all_to_all | solution.py:461
  46.5 0.0 copy-start.7
  46.5 0.8 copy-done.7
  47.3 1.3 %copy-done.11 = f32[128,2560]{1,0:T(8,128)S(1)} copy-done((f32[128,2560]{1,0:T(8,128)S(1)}, f32[128,2560]{1,0:T(8,128)}, u32[]{:S(2)}) %copy-start.11) | copy-done | bytes 1310744
  48.7 1.1 copy-done.13
  49.8 4.1 %left.2.refs_0_ = f32[1,128,5120]{2,1,0:T(8,128)} custom-call(s16[4,656,128]{2,1,0:T(8,128)(2,1)S(1)} %copy-done.13, f32[128,2560]{1,0:T(8,128)S(1)} %copy-done.11, s32[2,2,32,128]{3,2,1,0:T(8,128)S(1)} %pad_add_fusion.picks, bf16[256,256]{1,0:T(8,128)(2,1)S(1)} %copy-done.3, bf16[256,128]{1,0:T(8,128)(2,1)S(1)} %copy-done.7, ...), custom_call_target="tpu_custom_call" | custom-call | flops 2000000000 | bytes 4194304 | tf_op jit(solution)/shard_map/left/pallas_call | solution.py:415
  53.9 4.0 %all-to-all-done.got = f32[64,16,128]{2,1,0:T(8,128)S(1)} async-done(((f32[64,16,128]{2,1,0:T(8,128)}), f32[64,16,128]{2,1,0:T(8,128)S(1)}, u32[]{:S(2)}, u32[]{:S(2)}) %all-to-all-start) | async-done | bytes 524320 | tf_op jit(solution)/shard_map/all_to_all | solution.py:461
  57.9 6.1 %owner.1 = s16[176,128]{1,0:T(8,128)(2,1)S(1)} custom-call(f32[64,16,128]{2,1,0:T(8,128)S(1)} %all-to-all-done.got, bf16[256,256]{1,0:T(8,128)(2,1)S(1)} %copy-done.5, bf16[256,128]{1,0:T(8,128)(2,1)S(1)} %copy-done.6), custom_call_target="tpu_custom_call" | custom-call | tf_op jit(solution)/shard_map/owner/pallas_call | solution.py:300
  64.0 0.2 broadcast_in_dim.3
  64.2 0.0 copy-start.8
  64.2 26.1 %all_to_all.10 = s16[32,176,128]{2,1,0:T(8,128)(2,1)S(1)} all-to-all(s16[32,176,128]{2,1,0:T(8,128)(2,1)S(1)} %broadcast_in_dim.3), channel_id=1, replica_groups=mesh['x'=4,'z'=4,'yh'=2,'yl'=2,'c'=2] {'x','z','yh'}, dimensions={0} | all-to-all | bytes 2883584 | tf_op jit(solution)/shard_map/all_to_all | solution.py:468
  90.3 0.1 fusion.12
  90.4 3.2 %collective-permute-start.10 = (s16[16,176,128]{2,1,0:T(8,128)(2,1)S(1)}, s16[16,176,128]{2,1,0:T(8,128)(2,1)S(1)}, u32[]{:S(2)}, u32[]{:S(2)}) collective-permute-start(s16[16,176,128]{2,1,0:T(8,128)(2,1)S(1)} %get-tuple-element.39.got1), channel_id=1, source_target_pairs={{0,1},{1,0},{2,3},{3,2},{4,5},{5,4},{6,7},{7,6},{8,9},{9,8},{10,11... | collective-permute-start | bytes 2162696 | tf_op jit(solution)/shard_map/ppermute | solution.py:472
  93.6 0.1 collective-permute-start.9
  93.7 0.3 collective-permute-start.7
  94.0 0.4 collective-permute-start.8
  94.4 1.0 collective-permute-start.13
  95.4 5.0 %left.3 = f32[1,128,5120]{2,1,0:T(8,128)} custom-call(s16[4,656,128]{2,1,0:T(8,128)(2,1)} %collective-permute-done.4.q, f32[128,2560]{1,0:T(8,128)S(1)} %copy-done.2, s32[2,2,32,128]{3,2,1,0:T(8,128)S(1)} %pad_add_fusion.picks, bf16[256,256]{1,0:T(8,128)(2,1)S(1)} %copy-done.3, bf16[256,128]{1,0:T(8,128)(2,1)S(1)} %copy-done.8, ...), custom_call_target="tpu_custom_call", output_to_operand_aliasing={{}: (7, {})} | custom-call | flops 2000000000 | bytes 4194304 | tf_op jit(solution)/shard_map/left/pallas_call | solution.py:415
  100.4 4.4 %finish.4 = (f32[128,5120]{1,0:T(8,128)}, bf16[512,5120]{1,0:T(8,128)(2,1)}) custom-call(s32[1]{0:T(128)} %bitcast.8._, s16[16,176,128]{2,1,0:T(8,128)(2,1)S(1)} %get-tuple-element.40.got0, s16[16,176,128]{2,1,0:T(8,128)(2,1)S(1)} %get-tuple-element.39.got1, bf16[128,5120]{1,0:T(8,128)(2,1)} %par.1), custom_call_target="tpu_custom_call" | custom-call | flops 10000000 | bytes 4194304 | tf_op jit(solution)/shard_map/finish/pallas_call | solution.py:349
  104.8 2.4 %finish.5.refs_0_ = bf16[512,5120]{1,0:T(8,128)(2,1)} custom-call(s32[1]{0:T(128)} %bitcast.7._, s16[16,176,128]{2,1,0:T(8,128)(2,1)S(1)} %collective-permute-done.9.got0, s16[16,176,128]{2,1,0:T(8,128)(2,1)S(1)} %collective-permute-done.10.got1, bf16[128,5120]{1,0:T(8,128)(2,1)S(1)} %collective-permute-done.6.par, ...), custom_call_target="tpu_custom_call", output_to_operand_aliasing={{}: (4, {})} | custom-call | flops 10000000 | bytes 4194304 | tf_op jit(solution)/shard_map/finish/pallas_call | solution.py:349
  107.2 3.9 %collective-permute-done.7.got0 = s16[16,176,128]{2,1,0:T(8,128)(2,1)S(1)} collective-permute-done((s16[16,176,128]{2,1,0:T(8,128)(2,1)S(1)}, s16[16,176,128]{2,1,0:T(8,128)(2,1)S(1)}, u32[]{:S(2)}, u32[]{:S(2)}) %collective-permute-start.7) | collective-permute-done | bytes 720928 | tf_op jit(solution)/shard_map/ppermute | solution.py:471
  111.0 1.2 collective-permute-done.8.got1
  112.2 1.6 %collective-permute-start.11 = (s16[16,176,128]{2,1,0:T(8,128)(2,1)S(1)}, s16[16,176,128]{2,1,0:T(8,128)(2,1)S(1)}, u32[]{:S(2)}, u32[]{:S(2)}) collective-permute-start(s16[16,176,128]{2,1,0:T(8,128)(2,1)S(1)} %collective-permute-done.7.got0), channel_id=1, source_target_pairs={{0,1},{1,0},{2,3},{3,2},{4,5},{5,4},{6,7},{7,6},{8,9},{9,8},{10,11... | collective-permute-start | bytes 2162696 | tf_op jit(solution)/shard_map/ppermute | solution.py:479
  113.8 2.4 %finish.6.refs_0_ = bf16[512,5120]{1,0:T(8,128)(2,1)} custom-call(s32[1]{0:T(128)} %bitcast.10._, s16[16,176,128]{2,1,0:T(8,128)(2,1)S(1)} %collective-permute-done.7.got0, s16[16,176,128]{2,1,0:T(8,128)(2,1)S(1)} %collective-permute-done.8.got1, bf16[128,5120]{1,0:T(8,128)(2,1)S(1)} %collective-permute-done.5.par, ...), custom_call_target="tpu_custom_call", output_to_operand_aliasing={{}: (4, {})} | custom-call | flops 10000000 | bytes 4194304 | tf_op jit(solution)/shard_map/finish/pallas_call | solution.py:349
  116.2 0.5 collective-permute-done.12.got1
  116.6 2.4 %finish.7 = bf16[512,5120]{1,0:T(8,128)(2,1)} custom-call(s32[1]{0:T(128)} %bitcast.9._, s16[16,176,128]{2,1,0:T(8,128)(2,1)S(1)} %collective-permute-done.11.got0, s16[16,176,128]{2,1,0:T(8,128)(2,1)S(1)} %collective-permute-done.12.got1, bf16[128,5120]{1,0:T(8,128)(2,1)S(1)} %collective-permute-done.13.par, ...), custom_call_target="tpu_custom_call", output_to_operand_aliasing={{}: (4, {})} | custom-call | flops 10000000 | bytes 4194304 | tf_op jit(solution)/shard_map/finish/pallas_call | solution.py:349
  (36 shorter events, 0.1 us)
Async XLA Ops:
  0.6 7.3 %copy-start.15 = (bf16[1024,5120]{1,0:T(8,128)(2,1)S(1)}, bf16[1024,5120]{1,0:T(8,128)(2,1)}, u32[]{:S(2)}) copy-start(bf16[1024,5120]{1,0:T(8,128)(2,1)} %param.12) | copy-start | bytes 31457284
  6.4 6.8 %copy-start.14 = (s32[1,2,80,32]{2,3,1,0:T(8,128)S(1)}, s32[1,2,80,32]{2,3,1,0:T(8,128)}, u32[]{:S(2)}) copy-start(s32[1,2,80,32]{2,3,1,0:T(8,128)} %param.14) | copy-start | bytes 61444
  6.4 8.4 %collective-permute-start.2 = (f32[256,2560]{1,0:T(8,128)S(1)}, f32[256,2560]{1,0:T(8,128)S(1)}, u32[]{:S(2)}, u32[]{:S(2)}) collective-permute-start(f32[256,2560]{1,0:T(8,128)S(1)} %fusion), channel_id=1, source_target_pairs={{0,1},{1,0},{2,3},{3,2},{4,5},{5,4},{6,7},{7,6},{8,9},{9,8},{10,11... | collective-permute-start | bytes 7864328 | tf_op jit(solution)/shard_map/ppermute | solution.py:453
  9.5 9.5 %collective-permute-start = (f32[256,2560]{1,0:T(8,128)S(1)}, f32[256,2560]{1,0:T(8,128)S(1)}, u32[]{:S(2)}, u32[]{:S(2)}) collective-permute-start(f32[256,2560]{1,0:T(8,128)S(1)} %fusion.4), channel_id=1, source_target_pairs={{0,1},{1,0},{2,3},{3,2},{4,5},{5,4},{6,7},{7,6},{8,9},{9,8},{10,11... | collective-permute-start | bytes 7864328 | tf_op jit(solution)/shard_map/ppermute | solution.py:453
  9.6 54.4 %collective-permute-start.5 = (bf16[128,5120]{1,0:T(8,128)(2,1)}, bf16[128,5120]{1,0:T(8,128)(2,1)S(1)}, u32[]{:S(2)}, u32[]{:S(2)}) collective-permute-start(bf16[128,5120]{1,0:T(8,128)(2,1)} %par.1), channel_id=1, source_target_pairs={{0,6},{2,4},{4,2},{6,0},{1,7},{3,5},{5,3},{7,1},{8,14},{10,12},{12... | collective-permute-start | bytes 3932168 | tf_op jit(solution)/shard_map/ppermute | solution.py:448
  12.5 51.5 %collective-permute-start.6 = (bf16[128,5120]{1,0:T(8,128)(2,1)}, bf16[128,5120]{1,0:T(8,128)(2,1)S(1)}, u32[]{:S(2)}, u32[]{:S(2)}) collective-permute-start(bf16[128,5120]{1,0:T(8,128)(2,1)} %par.1), channel_id=1, source_target_pairs={{0,1},{1,0},{2,3},{3,2},{4,5},{5,4},{6,7},{7,6},{8,9},{9,8},{10,11... | collective-permute-start | bytes 3932168 | tf_op jit(solution)/shard_map/ppermute | solution.py:465
  13.2 5.7 %collective-permute-start.1 = (s32[2,32,128]{2,1,0:T(8,128)S(1)}, s32[2,32,128]{2,1,0:T(8,128)S(1)}, u32[]{:S(2)}, u32[]{:S(2)}) collective-permute-start(s32[2,32,128]{2,1,0:T(8,128)S(1)} %get-tuple-element.46), channel_id=1, source_target_pairs={{0,2},{2,0},{4,6},{6,4},{1,3},{3,1},{5,7},{7,5},{8,10},{10,8},{12,... | collective-permute-start | bytes 98312 | tf_op jit(solution)/shard_map/ppermute | solution.py:446
  15.7 18.8 %collective-permute-start.3 = (s16[4,656,128]{2,1,0:T(8,128)(2,1)S(1)}, s16[4,656,128]{2,1,0:T(8,128)(2,1)S(1)}, u32[]{:S(2)}, u32[]{:S(2)}) collective-permute-start(s16[4,656,128]{2,1,0:T(8,128)(2,1)S(1)} %code.2), channel_id=1, source_target_pairs={{0,2},{2,0},{4,6},{6,4},{1,3},{3,1},{5,7},{7,5},{8,10},{10,8},{12,... | collective-permute-start | bytes 2015240 | tf_op jit(solution)/shard_map/ppermute | solution.py:455
  18.9 2.2 %copy-start = (f32[1,128,5120]{2,1,0:T(8,128)S(1)}, f32[1,128,5120]{2,1,0:T(8,128)}, u32[]{:S(2)}) copy-start(f32[1,128,5120]{2,1,0:T(8,128)} %mom.3) | copy-start | bytes 7864324
  18.9 2.1 %copy-start.3 = (bf16[256,256]{1,0:T(8,128)(2,1)S(1)}, bf16[256,256]{1,0:T(8,128)(2,1)}, u32[]{:S(2)}) copy-start(bf16[256,256]{1,0:T(8,128)(2,1)} %constant.28.clone.rt) | copy-start | bytes 393220
  18.9 2.1 %copy-start.4 = (bf16[512,256]{1,0:T(8,128)(2,1)S(1)}, bf16[512,256]{1,0:T(8,128)(2,1)}, u32[]{:S(2)}) copy-start(bf16[512,256]{1,0:T(8,128)(2,1)} %constant.30.clone.lt) | copy-start | bytes 786436
  18.9 2.1 %copy-start.9 = (s32[2,8,128]{2,1,0:T(8,128)S(1)}, s32[2,8,128]{2,1,0:T(8,128)}, u32[]{:S(2)}) copy-start(s32[2,8,128]{2,1,0:T(8,128)} %constant.33.clone.tab) | copy-start | bytes 24580
  20.6 43.4 %collective-permute-start.4 = (s16[4,656,128]{2,1,0:T(8,128)(2,1)}, s16[4,656,128]{2,1,0:T(8,128)(2,1)}, u32[]{:S(2)}, u32[]{:S(2)}) collective-permute-start(s16[4,656,128]{2,1,0:T(8,128)(2,1)} %code.3), channel_id=1, source_target_pairs={{0,2},{2,0},{4,6},{6,4},{1,3},{3,1},{5,7},{7,5},{8,10},{10,8},{12,... | collective-permute-start | bytes 2015240 | tf_op jit(solution)/shard_map/ppermute | solution.py:455
  26.8 1.1 copy-start.10
  27.8 18.7 %copy-start.5 = (bf16[256,256]{1,0:T(8,128)(2,1)S(1)}, bf16[256,256]{1,0:T(8,128)(2,1)}, u32[]{:S(2)}) copy-start(bf16[256,256]{1,0:T(8,128)(2,1)} %constant.29.clone.irt.rt) | copy-start | bytes 393220
  27.8 18.7 %copy-start.6 = (bf16[256,128]{1,0:T(8,128)(2,1)S(1)}, bf16[256,128]{1,0:T(8,128)(2,1)}, u32[]{:S(2)}) copy-start(bf16[256,128]{1,0:T(8,128)(2,1)} %constant.32.clone.ilt.lt) | copy-start | bytes 196612
  33.5 1.1 copy-start.1
  34.6 0.9 copy-start.12
  35.5 22.4 %all-to-all-start = ((f32[64,16,128]{2,1,0:T(8,128)}), f32[64,16,128]{2,1,0:T(8,128)S(1)}, u32[]{:S(2)}, u32[]{:S(2)}) async-start(f32[64,16,128]{2,1,0:T(8,128)} %bitcast.6), calls=%async_computation | async-start | bytes 1048576 | tf_op jit(solution)/shard_map/all_to_all | solution.py:461
  46.5 0.8 copy-start.7
  47.3 1.3 %copy-start.11 = (f32[128,2560]{1,0:T(8,128)S(1)}, f32[128,2560]{1,0:T(8,128)}, u32[]{:S(2)}) copy-start(f32[128,2560]{1,0:T(8,128)} %copy-done.10) | copy-start | bytes 3932164
  48.7 1.1 copy-start.13
  64.2 31.2 %copy-start.2 = (f32[128,2560]{1,0:T(8,128)S(1)}, f32[128,2560]{1,0:T(8,128)}, u32[]{:S(2)}) copy-start(f32[128,2560]{1,0:T(8,128)} %copy-done.1) | copy-start | bytes 3932164
  64.2 31.2 %copy-start.8 = (bf16[256,128]{1,0:T(8,128)(2,1)S(1)}, bf16[256,128]{1,0:T(8,128)(2,1)}, u32[]{:S(2)}) copy-start(bf16[256,128]{1,0:T(8,128)(2,1)} %constant.31.clone.lt) | copy-start | bytes 196612
  90.4 14.4 %collective-permute-start.10 = (s16[16,176,128]{2,1,0:T(8,128)(2,1)S(1)}, s16[16,176,128]{2,1,0:T(8,128)(2,1)S(1)}, u32[]{:S(2)}, u32[]{:S(2)}) collective-permute-start(s16[16,176,128]{2,1,0:T(8,128)(2,1)S(1)} %get-tuple-element.39.got1), channel_id=1, source_target_pairs={{0,1},{1,0},{2,3},{3,2},{4,5},{5,4},{6,7},{7,6},{8,9},{9,8},{10,11... | collective-permute-start | bytes 2162696 | tf_op jit(solution)/shard_map/ppermute | solution.py:472
  93.6 11.1 %collective-permute-start.9 = (s16[16,176,128]{2,1,0:T(8,128)(2,1)S(1)}, s16[16,176,128]{2,1,0:T(8,128)(2,1)S(1)}, u32[]{:S(2)}, u32[]{:S(2)}) collective-permute-start(s16[16,176,128]{2,1,0:T(8,128)(2,1)S(1)} %get-tuple-element.40.got0), channel_id=1, source_target_pairs={{0,1},{1,0},{2,3},{3,2},{4,5},{5,4},{6,7},{7,6},{8,9},{9,8},{10,11... | collective-permute-start | bytes 2162696 | tf_op jit(solution)/shard_map/ppermute | solution.py:472
  93.7 17.3 %collective-permute-start.7 = (s16[16,176,128]{2,1,0:T(8,128)(2,1)S(1)}, s16[16,176,128]{2,1,0:T(8,128)(2,1)S(1)}, u32[]{:S(2)}, u32[]{:S(2)}) collective-permute-start(s16[16,176,128]{2,1,0:T(8,128)(2,1)S(1)} %get-tuple-element.40.got0), channel_id=1, source_target_pairs={{0,2},{2,0},{4,6},{6,4},{1,3},{3,1},{5,7},{7,5},{8,10},{10,8},{12,... | collective-permute-start | bytes 2162696 | tf_op jit(solution)/shard_map/ppermute | solution.py:471
  94.0 18.2 %collective-permute-start.8 = (s16[16,176,128]{2,1,0:T(8,128)(2,1)S(1)}, s16[16,176,128]{2,1,0:T(8,128)(2,1)S(1)}, u32[]{:S(2)}, u32[]{:S(2)}) collective-permute-start(s16[16,176,128]{2,1,0:T(8,128)(2,1)S(1)} %get-tuple-element.39.got1), channel_id=1, source_target_pairs={{0,6},{2,4},{4,2},{6,0},{1,7},{3,5},{5,3},{7,1},{8,14},{10,12},{12... | collective-permute-start | bytes 2162696 | tf_op jit(solution)/shard_map/ppermute | solution.py:471
  94.4 21.8 %collective-permute-start.13 = (bf16[128,5120]{1,0:T(8,128)(2,1)S(1)}, bf16[128,5120]{1,0:T(8,128)(2,1)S(1)}, u32[]{:S(2)}, u32[]{:S(2)}) collective-permute-start(bf16[128,5120]{1,0:T(8,128)(2,1)S(1)} %collective-permute-done.5.par), channel_id=1, source_target_pairs={{0,1},{1,0},{2,3},{3,2},{4,5},{5,4},{6,7},{7,6},{8,9},{9,8},{10,11... | collective-permute-start | bytes 3932168 | tf_op jit(solution)/shard_map/ppermute | solution.py:467
  112.2 4.0 %collective-permute-start.11 = (s16[16,176,128]{2,1,0:T(8,128)(2,1)S(1)}, s16[16,176,128]{2,1,0:T(8,128)(2,1)S(1)}, u32[]{:S(2)}, u32[]{:S(2)}) collective-permute-start(s16[16,176,128]{2,1,0:T(8,128)(2,1)S(1)} %collective-permute-done.7.got0), channel_id=1, source_target_pairs={{0,1},{1,0},{2,3},{3,2},{4,5},{5,4},{6,7},{7,6},{8,9},{9,8},{10,11... | collective-permute-start | bytes 2162696 | tf_op jit(solution)/shard_map/ppermute | solution.py:479
  113.8 2.8 %collective-permute-start.12 = (s16[16,176,128]{2,1,0:T(8,128)(2,1)S(1)}, s16[16,176,128]{2,1,0:T(8,128)(2,1)S(1)}, u32[]{:S(2)}, u32[]{:S(2)}) collective-permute-start(s16[16,176,128]{2,1,0:T(8,128)(2,1)S(1)} %collective-permute-done.8.got1), channel_id=1, source_target_pairs={{0,1},{1,0},{2,3},{3,2},{4,5},{5,4},{6,7},{7,6},{8,9},{9,8},{10,11... | collective-permute-start | bytes 2162696 | tf_op jit(solution)/shard_map/ppermute | solution.py:479

commit v3 on v2

--- a/solution.py
+++ b/solution.py
@@ -27,6 +27,9 @@
 ARB = pltpu.CompilerParams(vmem_limit_bytes=20 * 1024 * 1024)
 
 
+SHORT = pl.CostEstimate(flops=1000, bytes_accessed=1000, transcendentals=0)
+
+
 def cosine():
     k = np.arange(64, dtype=np.float64)[:, None]
     i = np.arange(64, dtype=np.float64)[None, :]
@@ -138,8 +141,7 @@
     return t
 
 
-def code_kernel(own, got, q):
-    x = (own[...] + got[...]) * (1.0 / 64)
+def code(x, q):
     for p in range(LEFT):
         exps = jnp.zeros((16, 128), I32)
         for t in range(5):
@@ -151,7 +153,11 @@
         q[p, 640:656, :] = exps.astype(I16)
 
 
-def code(own, got):
+def code_kernel(own, got, q):
+    code((own[...] + got[...]) * (1.0 / 64), q)
+
+
+def code_alone(own, got):
     spec = pl.BlockSpec((128, LEFT * GW), lambda i: (1, i))
     return pl.pallas_call(
         code_kernel,
@@ -160,43 +166,46 @@
         out_specs=pl.BlockSpec((LEFT, QROWS, 128), lambda i: (i, 0, 0)),
         out_shape=jax.ShapeDtypeStruct((PER, QROWS, 128), I16),
         compiler_params=ARB,
-        cost_estimate=pl.CostEstimate(flops=10**7, bytes_accessed=4 * 2**20, transcendentals=0),
+        cost_estimate=SHORT,
         name="code",
     )(own, got)
 
 
-def compress_kernel(part, me, own, got, mom, picks, tab, rt, lt, *refs):
+def compress_kernel(part, with_code, me, own, got, mom, picks, tab, rt, lt, *refs):
     pm, comp = refs[-2:]
     yl = me[0]
-    first = 10 * (PER * part + pl.program_id(0))
+    first = 10 * (PER * part + LEFT * pl.program_id(0))
     ln = lane((1, 128))
     w0 = (own[:128] + got[:128]) * (1.0 / 64) + DECAY * mom[0]
     w1 = (own[128:] + got[128:]) * (1.0 / 64)
     pm[...] = w0
+    if with_code:
+        code(w1, refs[-3])
     tiles = []
-    for t in range(5):
+    for t in range(5 * LEFT):
         tiles += [w0[:, 128 * t : 128 * t + 128], w1[:, 128 * t : 128 * t + 128]]
     o = mul_right(jnp.concatenate(tiles, axis=0), rt[...])
-    tiles = [o[256 * t : 256 * t + 256] for t in range(5)]
+    tiles = [o[256 * t : 256 * t + 256] for t in range(5 * LEFT)]
     u16 = sub((16, 128))
     ln16 = lane((16, 128))
     short = []
-    for g in range(2):
+    for k in range(2 * LEFT):
+        g, at = k % 2, 5 * (k // 2)
         pieces = []
-        span = first + tab[g, 0:1, :]
+        span = first + 2 * at + tab[g, 0:1, :]
         for rb in range(4):
             qt = picks[rb // 2, rb % 2, 16:32, :]
             chosen = jnp.where(u16 == (ln16 & 15), lanes_of(qt, span), 0)
             idx = jnp.sum(chosen, axis=0, keepdims=True) + tab[g, 1:2, :]
             rows = slice(64 * rb, 64 * rb + 64)
-            a = lanes_of(tiles[3 * g][rows], idx)
-            b = lanes_of(tiles[3 * g + 1][rows], idx)
-            c = lanes_of(tiles[2][rows], idx)
+            a = lanes_of(tiles[at + 3 * g][rows], idx)
+            b = lanes_of(tiles[at + 3 * g + 1][rows], idx)
+            c = lanes_of(tiles[at + 2][rows], idx)
             pieces.append(jnp.where(ln < 32, a, jnp.where(ln < 64, b, c)))
         short.append(jnp.concatenate(pieces, axis=0))
     z = mul_left(lt[...], jnp.concatenate(short, axis=1))
-    for g in range(2):
-        span = first + tab[g, 0:1, :]
+    for k in range(2 * LEFT):
+        span = first + 10 * (k // 2) + tab[k % 2, 0:1, :]
         for rb in range(4):
             rel, a = rb // 2, rb % 2
             to = yl if rel == 0 else 1 - yl
@@ -209,20 +218,20 @@
                 acc = jnp.where(ln < 85, pi, qidx[8 * h : 8 * h + 8]).astype(F32)
                 for j in range(8):
                     r = 64 * rb + 8 * j
-                    v = rows_of(z[r : r + 8, 128 * g : 128 * g + 128], low)
+                    v = rows_of(z[r : r + 8, 128 * k : 128 * k + 128], low)
                     acc = jnp.where((high == j) & (ln < 80), v, acc)
-                comp[a, g, to, 8 * h : 8 * h + 8, :] = acc
-
-
-def compress(part, me, own, got, mom, picks, tab, rt, lt, before):
-    n = PER
+                comp[a, k, to, 8 * h : 8 * h + 8, :] = acc
+
+
+def compress(part, with_code, me, own, got, mom, picks, tab, rt, lt, before):
+    n = PER // LEFT
     full = lambda *s: pl.BlockSpec(s, lambda i, me: (0,) * len(s))
-    col = lambda r: pl.BlockSpec((r, GW), lambda i, me: (0, i))
+    col = lambda r: pl.BlockSpec((r, LEFT * GW), lambda i, me: (0, i))
     args = [own, got, mom, picks, tab, rt, lt]
     in_specs = [
         col(256),
         col(256),
-        pl.BlockSpec((1, 128, GW), lambda i, me: (0, 0, part * n + i)),
+        pl.BlockSpec((1, 128, LEFT * GW), lambda i, me: (0, 0, part * n + i)),
         full(2, 2, 32, 128),
         full(2, 8, 128),
         full(256, 256),
@@ -232,30 +241,29 @@
     if before is not None:
         args.append(before)
         in_specs.append(pl.BlockSpec(memory_space=pl.ANY))
-        alias = {8: 1}
+        alias = {8: 1 + with_code}
     return pl.pallas_call(
-        functools.partial(compress_kernel, part),
+        functools.partial(compress_kernel, part, with_code),
         grid_spec=pltpu.PrefetchScalarGridSpec(
             num_scalar_prefetch=1,
             grid=(n,),
             in_specs=in_specs,
-            out_specs=[
-                col(128),
-                pl.BlockSpec((2, 2, 2, 16, 128), lambda i, me: (0, part * n + i, 0, 0, 0)),
-            ],
+            out_specs=([pl.BlockSpec((LEFT, QROWS, 128), lambda i, me: (i, 0, 0))] if with_code else [])
+            + [col(128), pl.BlockSpec((2, 2 * LEFT, 2, 16, 128), lambda i, me: (0, part * n + i, 0, 0, 0))],
         ),
-        out_shape=[
+        out_shape=([jax.ShapeDtypeStruct((PER, QROWS, 128), I16)] if with_code else [])
+        + [
             jax.ShapeDtypeStruct((128, 5120 // PARTS), F32),
             jax.ShapeDtypeStruct((2, 16, 2, 16, 128), F32),
         ],
         input_output_aliases=alias,
         compiler_params=ARB,
-        cost_estimate=pl.CostEstimate(flops=2 * 10**9, bytes_accessed=9 * 2**20, transcendentals=0),
+        cost_estimate=SHORT,
         name="compress",
     )(me, *args)
 
 
-def owner_kernel(got, rt, lt, out, xh, xl, hot):
+def owner_kernel(got, rt, lt, out, xs, hot):
     ln16 = lane((16, 128))
 
     here = (ln16 & 63).astype(F32)
@@ -263,7 +271,8 @@
 
     def one(n, _):
         at = pl.multiple_of(16 * n, 16)
-        x = got[n]
+        x = got[2 * n]
+        x = jnp.where(ln16 < 80, x + got[2 * n + 1], x)
         for t in range(3):
             half = 2 * t + (ln16 >> 6)
             hit = jnp.where(lanes_of(x, 85 + half) == here, 16 * half + u16 + 1, 0)
@@ -272,21 +281,20 @@
             idx = jnp.broadcast_to(jnp.sum(hit, axis=0, keepdims=True), (16, 128)) - 1
             v = jnp.where(idx >= 0, lanes_of(x, jnp.maximum(idx, 0)), 0.0)
             hi, lo = split(v)
-            xh[t, pl.ds(at, 16), :] = hi
-            xl[t, pl.ds(at, 16), :] = lo
+            xs[t, pl.ds(at, 16), :] = jnp.concatenate([hi, lo], axis=1)
             hot[t, pl.ds(at, 16), :] = jnp.where(lanes_of(x, 80 + half) == here, 1.0, 0.0).astype(BF16)
         return 0
 
-    lax.fori_loop(0, got.shape[0], one, 0, unroll=4)
+    lax.fori_loop(0, got.shape[0] // 2, one, 0, unroll=8)
     same = (sub((128, 128)) >> 6) == (lane((128, 128)) >> 6)
-    tiles = []
+    grids = []
     for t in range(3):
-        dims = (((0,), (0,)), ((), ()))
-        d = lax.dot_general(hot[t], xh[t], dims, preferred_element_type=F32)
-        d = d + lax.dot_general(hot[t], xl[t], dims, preferred_element_type=F32)
-        d = jnp.where(same, d, 0.0)
-        u = mul_left(lt[...], mul_right(d, rt[...]))
-        tiles.append(u[:64] + u[64:])
+        d = lax.dot_general(hot[t], xs[t], (((0,), (0,)), ((), ())), preferred_element_type=F32)
+        grids.append(jnp.where(same, d[:, :128] + d[:, 128:], 0.0))
+    d = mul_right(jnp.concatenate(grids, axis=0), rt[...])
+    u = mul_left(lt[...], jnp.concatenate([d[128 * t : 128 * t + 128] for t in range(3)], axis=1))
+    u = u[:64] + u[64:]
+    tiles = [u[:, 128 * t : 128 * t + 128] for t in range(3)]
     last = tiles[2]
     ln = lane((32, 128))
     tiles[2] = jnp.where(ln < 64, last[:32], jnp.roll(last[32:], 64, axis=1))
@@ -300,7 +308,7 @@
     return pl.pallas_call(
         owner_kernel,
         out_shape=jax.ShapeDtypeStruct((UROWS, 128), I16),
-        scratch_shapes=[pltpu.VMEM((3, 1024, 128), BF16)] * 3,
+        scratch_shapes=[pltpu.VMEM((3, 512, 256), BF16), pltpu.VMEM((3, 512, 128), BF16)],
         compiler_params=ARB,
         name="owner",
     )(got, rt, lt)
@@ -319,44 +327,72 @@
     return [even[:64], even[64:128], jnp.concatenate([top, bottom], axis=0), odd[:64], odd[64:128]]
 
 
-def finish_kernel(with_update, _, got0, got1, par, *refs):
-    for a, got in enumerate((got0, got1)):
-        rows = slice(64 * a, 64 * a + 64)
-        for pair in range(LEFT):
-            for t, u in enumerate(decode(got, pair)):
-                cols = slice(GW * pair + 128 * t, GW * pair + 128 * t + 128)
-                if with_update:
-                    refs[-2][rows, cols] = u
-                refs[-1][rows, cols] = (par[rows, cols].astype(F32) - STEP * u).astype(BF16)
-
-
-def finish(row, got0, got1, par, before):
-    with_update = before is None
-    col = pl.BlockSpec((128, LEFT * GW), lambda i, row: (0, i))
-    blocks = pl.BlockSpec((2 * LEFT, UROWS, 128), lambda i, row: (i, 0, 0))
-    args = [got0, got1, par]
-    in_specs = [blocks, blocks, col]
-    out_specs = [pl.BlockSpec((128, LEFT * GW), lambda i, row: (row[0], i))]
-    out_shape = [jax.ShapeDtypeStruct((512, 5120), BF16)]
+def finish_kernel(got, par, *refs):
+    update, new = refs[-2:]
+    for pair in range(LEFT):
+        for t, u in enumerate(decode(got, pair)):
+            cols = slice(GW * pair + 128 * t, GW * pair + 128 * t + 128)
+            update[:, cols] = u
+            new[:, cols] = (par[:, cols].astype(F32) - STEP * u).astype(BF16)
+
+
+def finish(a, got, par, before):
+    n = PAIRS // LEFT
+    half = pl.BlockSpec((64, LEFT * GW), lambda i: (a, i))
+    args = [got, par]
+    in_specs = [pl.BlockSpec((2 * LEFT, UROWS, 128), lambda i: (n * a + i, 0, 0)), half]
     alias = {}
-    if with_update:
-        out_specs.insert(0, col)
-        out_shape.insert(0, jax.ShapeDtypeStruct((128, 5120), F32))
-    else:
+    if before is not None:
         args.append(before)
         in_specs.append(pl.BlockSpec(memory_space=pl.ANY))
-        alias = {4: 0}
+        alias = {2: 0}
     return pl.pallas_call(
-        functools.partial(finish_kernel, with_update),
-        grid_spec=pltpu.PrefetchScalarGridSpec(
-            num_scalar_prefetch=1, grid=(PAIRS // LEFT,), in_specs=in_specs, out_specs=out_specs
-        ),
-        out_shape=out_shape,
+        finish_kernel,
+        grid=(n,),
+        in_specs=in_specs,
+        out_specs=[half, pl.BlockSpec((64, LEFT * GW), lambda i: (0, i))],
+        out_shape=[jax.ShapeDtypeStruct((128, 5120), F32), jax.ShapeDtypeStruct((64, 5120), BF16)],
         input_output_aliases=alias,
         compiler_params=ARB,
-        cost_estimate=pl.CostEstimate(flops=10**7, bytes_accessed=4 * 2**20, transcendentals=0),
+        cost_estimate=SHORT,
         name="finish",
-    )(row, *args)
+    )(*args)
+
+
+def gather_kernel(n, rows, *refs):
+    sem = refs[-1]
+    out = refs[-2]
+    copies = []
+    for i in range(n):
+        for k in range(4):
+            at = pl.multiple_of(rows[i] + 16 * k, 16)
+            copies.append(
+                pltpu.make_async_copy(refs[i].at[16 * k : 16 * k + 16, :], out.at[pl.ds(at, 16), :], sem.at[4 * i + k])
+            )
+            copies[-1].start()
+    for copy in copies:
+        copy.wait()
+
+
+def gather(rows, parts, before):
+    n = len(parts)
+    anywhere = pl.BlockSpec(memory_space=pl.ANY)
+    args = list(parts) + ([] if before is None else [before])
+    return pl.pallas_call(
+        functools.partial(gather_kernel, n),
+        grid_spec=pltpu.PrefetchScalarGridSpec(
+            num_scalar_prefetch=1,
+            grid=(1,),
+            in_specs=[anywhere] * len(args),
+            out_specs=anywhere,
+            scratch_shapes=[pltpu.SemaphoreType.DMA((4 * n,))],
+        ),
+        out_shape=jax.ShapeDtypeStruct((512, 5120), BF16),
+        input_output_aliases={} if before is None else {n + 1: 0},
+        compiler_params=ARB,
+        cost_estimate=pl.CostEstimate(flops=0, bytes_accessed=4 * 2**20, transcendentals=0),
+        name="gather",
+    )(rows, *args)
 
 
 def left_kernel(part, q, pm, picks, rt, lt, irt, ilt, *refs):
@@ -421,7 +457,7 @@
         scratch_shapes=[pltpu.VMEM((128, 128), F32)],
         input_output_aliases=alias,
         compiler_params=ARB,
-        cost_estimate=pl.CostEstimate(flops=2 * 10**9, bytes_accessed=4 * 2**20, transcendentals=0),
+        cost_estimate=SHORT,
         name="left",
     )(*args)
 
@@ -445,40 +481,41 @@
     mine = jnp.pad(coef_picks[0].swapaxes(1, 2), ((0, 0), (0, 0), (0, 48)))
     theirs = lax.ppermute(mine, ("yh", "yl"), NEAR)
     picks = jnp.stack([mine, theirs])
-    far_params = lax.ppermute(params, ("yh", "yl"), FAR)
 
     core = lax.axis_index("c")
     sent = rows_for(hidden, 1 - core)
     kept = rows_for(hidden, core)
     swapped = [lax.ppermute(term(sent, grad, part), "c", SWAP) for part in range(PARTS)]
     own = [term(kept, grad, part) for part in range(PARTS)]
-    qs = [lax.ppermute(code(own[p], swapped[p]), ("yh", "yl"), NEAR) for p in range(PARTS)]
-    pms, comp = [], None
-    for part in range(PARTS):
-        pm, comp = compress(part, me, own[part], swapped[part], momentum, picks, tab, rt, lt4, comp)
-        pms.append(pm)
-    comp, qs[0] = lax.optimization_barrier((comp, qs[0]))
+    tables = (momentum, picks, tab, rt, lt4)
+    q0 = lax.ppermute(code_alone(own[0], swapped[0]), ("yh", "yl"), NEAR)
+    pm0, comp = compress(0, False, me, own[0], swapped[0], *tables, None)
+    q1, pm1, comp = compress(1, True, me, own[1], swapped[1], *tables, comp)
+    q1 = lax.ppermute(q1, ("yh", "yl"), NEAR)
+    comp, q0 = lax.optimization_barrier((comp, q0))
     got = lax.all_to_all(comp.reshape(64, 16, 128), REP + ("yl",), 0, 0, tiled=True)
-    first_left = left(0, qs[0], pms[0], picks, rt, lt, irt, ilt, None)
-    got, first_left = lax.optimization_barrier((got, first_left))
+    momentum_left = left(0, q0, pm0, picks, rt, lt, irt, ilt, None)
+    got, momentum_left = lax.optimization_barrier((got, momentum_left))
     mine16 = owner(got, irt, ilt)
-    other_params = lax.ppermute(params, "c", SWAP)
-    mine16, qs[1], far_params, other_params = lax.optimization_barrier((mine16, qs[1], far_params, other_params))
-    other_far = lax.ppermute(far_params, "c", SWAP)
+    mine16, q1 = lax.optimization_barrier((mine16, q1))
     every = lax.all_to_all(jnp.broadcast_to(mine16, (32, UROWS, 128)), REP, 0, 0, tiled=True)
-
-    block = [every[:16], every[16:]]
-    far = [lax.ppermute(v, ("yh", "yl"), way) for v, way in zip(block, (NEAR, FAR))]
-    other = [lax.ppermute(v, "c", SWAP) for v in block]
-    momentum_left = left(1, qs[1], pms[1], picks, rt, lt, irt, ilt, first_left)
-    row = lambda y, c: (2 * y + c).astype(I32).reshape(1)
+    every, pm1 = lax.optimization_barrier((every, pm1))
+
     yl = lax.axis_index("yl")
-    update, new = finish(row(yl, core), *block, params, None)
-    (new,) = finish(row(yl, 1 - core), *other, other_params, new)
-    far, new, momentum_left = lax.optimization_barrier((far, new, momentum_left))
-    other_distant = [lax.ppermute(v, "c", SWAP) for v in far]
-    (new,) = finish(row(1 - yl, core), *far, far_params, new)
-    (new,) = finish(row(1 - yl, 1 - core), *other_distant, other_far, new)
+    rows = lambda y, c: (128 * (2 * y + c) + 64 * jnp.arange(2)).astype(I32)
+    update, low = finish(0, every, params, None)
+    far_low = lax.ppermute(low, ("yh", "yl"), NEAR)
+    update, high = finish(1, every, params, update)
+    far_high = lax.ppermute(high, ("yh", "yl"), FAR)
+    momentum_left = left(1, q1, pm1, picks, rt, lt, irt, ilt, momentum_left)
+    other = [lax.ppermute(v, "c", SWAP) for v in (low, high)]
+    where = jnp.concatenate([rows(yl, core), rows(yl, 1 - core)])
+    new = gather(where, [low, high, *other], None)
+    far_low, far_high, new, momentum_left = lax.optimization_barrier((far_low, far_high, new, momentum_left))
+    distant = [lax.ppermute(v, "c", SWAP) for v in (far_low, far_high)]
+    new = gather(rows(1 - yl, core), [far_low, far_high], new)
+    distant, new = lax.optimization_barrier((distant, new))
+    new = gather(rows(1 - yl, 1 - core), distant, new)
     return momentum_left, update, new
 
 

time: 119 us -> 117 us (0.983)
  waiting for transfers between devices: 9.53 us -> 18.9 us
  Pallas kernels: 40.6 us -> 34.1 us
  starting transfers between devices: 24.9 us -> 21 us
  local copies, waits for them, and re-layouts: 8.01 us -> 5.63 us
    ppermute x11 -> x8, waiting for transfers between devices: 5.51 us -> 12 us  [the longest x1 9.34 us: body(): far_high = lax.ppermute(high, ('yh', 'yl'), FAR)]
    ppermute x11 -> x8, starting transfers between devices: 12.1 us -> 6.48 us  [the longest x2 3.16 us: body(): other = [lax.ppermute(v, 'c', SWAP) for v in (low, high)]]
    pallas_call x8, Pallas kernels: 25.5 us -> 20.4 us  [the longest x2 9.94 us: compress(): pl.pallas_call(functools.partial(compress_kernel, part, with_code), grid_...]
    all_to_all x1, waiting for transfers between devices: 4.02 us -> 6.84 us  [body(): lax.all_to_all(comp.reshape(64, 16, 128), REP + ('yl',), 0, 0, tiled=True)]
    unnamed x32 -> x30, local copies, waits for them, and re-layouts: 6.28 us -> 3.99 us
    pallas_call x1, Pallas kernels: 6.06 us -> 4.68 us  [owner(): pl.pallas_call(owner_kernel, out_shape=jax.ShapeDtypeStruct((UROWS, 128),...]
    ppermute x1, starting transfers between devices: 0.09 us -> 1.46 us  [body(): theirs = lax.ppermute(mine, ('yh', 'yl'), NEAR)]
  transfers between devices with their start and end apart: 15 -> 12, of which waited for: 4 -> 4; matrix products, arithmetic and copies ran while one was open for 4% -> 4% of each run, Pallas kernels for 32% -> 24%
where the time goes in v3:
time: 117 us
  Pallas kernels  34.1 us (29%)
  blocking collectives  26.8 us (23%)
  starting transfers between devices  21 us (18%)
  waiting for transfers between devices  18.9 us (16%)
  matrix products  8.98 us (8%)
  local copies, waits for them, and re-layouts  5.63 us (5%)
    all_to_all x1, blocking collectives, body(): lax.all_to_all(jnp.broadcast_to(mine16, (32, UROWS, 128)), REP, 0, 0, til...  26.8 us
    all_to_all x1, starting transfers between devices, body(): lax.all_to_all(comp.reshape(64, 16, 128), REP + ('yl',), 0, 0, tiled=True)  11.5 us
    pallas_call x2, Pallas kernels, compress(): pl.pallas_call(functools.partial(compress_kernel, part, with_code), grid_...  9.94 us
    ppermute x1, waiting for transfers between devices, body(): far_high = lax.ppermute(high, ('yh', 'yl'), FAR)  9.34 us
    pallas_call x2, Pallas kernels, left(): pl.pallas_call(functools.partial(left_kernel, part), grid=(n,), in_specs=...  9.08 us
    dot_general x4, matrix products, term(): lax.dot_general(hidden, right, (((0,), (0,)), ((), ())), preferred_elemen...  8.98 us
    all_to_all x1, waiting for transfers between devices, body(): lax.all_to_all(comp.reshape(64, 16, 128), REP + ('yl',), 0, 0, tiled=True)  6.84 us
    pallas_call x3, Pallas kernels, gather(): pl.pallas_call(functools.partial(gather_kernel, n), grid_spec=pltpu.Prefe...  5.47 us
  transfers between devices with their start and end apart: 12, of which 4 were waited for; matrix products, arithmetic and copies ran while one was open for 4% of the time, Pallas kernels for 24%

profile of v3, /device:TPU:1, one launch (start us, length us, event | category | flops | bytes accessed | tf_op | source)
XLA Modules:
  0.0 116.6 jit_solution(9651092832552406688)
XLA Ops:
  0.6 0.0 copy-start.14
  0.7 1.4 %constant_dynamic-slice_fusion.1 = (bf16[1024,128]{1,0:T(8,128)(2,1)S(1)}, bf16[1024,128]{1,0:T(8,128)(2,1)S(1)}, bf16[1024,128]{1,0:T(8,128)(2,1)S(1)}, bf16[1024,128]{1,0:T(8,128)(2,1)S(1)}) fusion(bf16[1024,512]{1,0:T(8,128)(2,1)} %param.11, s32[]{:T(128)S(6)} %select_n.14, s32[]{:T(128)S(6)} %select_n.13, s32[]{:T(128)S(6)} %select_n.12, s32[]{:T(128)S(6)} %select_n.15), kind=kLoop, calls=%fused_computation.12 | loop fusion | bytes 2097168 | tf_op jit(solution)/shard_map/dynamic_slice | solution.py:125
  2.1 4.3 %fusion = f32[256,2560]{1,0:T(8,128)S(1)} fusion(bf16[1024,5120]{1,0:T(8,128)(2,1)} %param.12, bf16[1024,128]{1,0:T(8,128)(2,1)S(1)} %get-tuple-element.54, bf16[1024,128]{1,0:T(8,128)(2,1)S(1)} %get-tuple-element.51), kind=kOutput, calls=%fused_computation | convolution fusion | flops 1343225856 | bytes 8388608 | tf_op jit(solution)/shard_map/dot_general | solution.py:120
  6.4 0.0 copy-start.13
  6.4 1.5 %collective-permute-start.2 = (f32[256,2560]{1,0:T(8,128)S(1)}, f32[256,2560]{1,0:T(8,128)S(1)}, u32[]{:S(2)}, u32[]{:S(2)}) collective-permute-start(f32[256,2560]{1,0:T(8,128)S(1)} %fusion), channel_id=1, source_target_pairs={{0,1},{1,0},{2,3},{3,2},{4,5},{5,4},{6,7},{7,6},{8,9},{9,8},{10,11... | collective-permute-start | bytes 7864328 | tf_op jit(solution)/shard_map/ppermute | solution.py:488
  7.9 1.6 %fusion.4 = f32[256,2560]{1,0:T(8,128)S(1)} fusion(bf16[1024,5120]{1,0:T(8,128)(2,1)S(1)} %copy-done.14, bf16[1024,128]{1,0:T(8,128)(2,1)S(1)} %get-tuple-element.54, bf16[1024,128]{1,0:T(8,128)(2,1)S(1)} %get-tuple-element.51), kind=kOutput, calls=%fused_computation.4 | convolution fusion | flops 1343225856 | bytes 8388608 | tf_op jit(solution)/shard_map/dot_general | solution.py:120
  9.5 0.1 collective-permute-start
  9.6 1.5 %collective-permute-start.1 = (s32[2,32,128]{2,1,0:T(8,128)S(1)}, s32[2,32,128]{2,1,0:T(8,128)S(1)}, u32[]{:S(2)}, u32[]{:S(2)}) collective-permute-start(s32[2,32,128]{2,1,0:T(8,128)S(1)} %get-tuple-element.56), channel_id=1, source_target_pairs={{0,2},{2,0},{4,6},{6,4},{1,3},{3,1},{5,7},{7,5},{8,10},{10,8},{12,... | collective-permute-start | bytes 98312 | tf_op jit(solution)/shard_map/ppermute | solution.py:482
  11.1 1.6 %fusion.2.own = f32[256,2560]{1,0:T(8,128)S(1)} fusion(bf16[1024,5120]{1,0:T(8,128)(2,1)S(1)} %copy-done.14, bf16[1024,128]{1,0:T(8,128)(2,1)S(1)} %get-tuple-element.52, bf16[1024,128]{1,0:T(8,128)(2,1)S(1)} %get-tuple-element.53), kind=kOutput, calls=%fused_computation.2 | convolution fusion | flops 1343225856 | bytes 8388608 | tf_op jit(solution)/shard_map/dot_general | solution.py:120
  12.7 0.9 code.1
  13.6 0.0 copy-start
  13.6 0.0 copy-start.2
  13.6 0.0 copy-start.6
  13.6 0.0 copy-start.12
  13.6 1.3 %collective-permute-start.3 = (s16[4,656,128]{2,1,0:T(8,128)(2,1)S(1)}, s16[4,656,128]{2,1,0:T(8,128)(2,1)S(1)}, u32[]{:S(2)}, u32[]{:S(2)}) collective-permute-start(s16[4,656,128]{2,1,0:T(8,128)(2,1)S(1)} %code.1), channel_id=1, source_target_pairs={{0,2},{2,0},{4,6},{6,4},{1,3},{3,1},{5,7},{7,5},{8,10},{10,8},{12,... | collective-permute-start | bytes 2015240 | tf_op jit(solution)/shard_map/ppermute | solution.py:491
  14.9 1.6 %fusion.6.own = f32[256,2560]{1,0:T(8,128)S(1)} fusion(bf16[1024,5120]{1,0:T(8,128)(2,1)S(1)} %copy-done.14, bf16[1024,128]{1,0:T(8,128)(2,1)S(1)} %get-tuple-element.52, bf16[1024,128]{1,0:T(8,128)(2,1)S(1)} %get-tuple-element.53), kind=kOutput, calls=%fused_computation.6 | convolution fusion | flops 1343225856 | bytes 8388608 | tf_op jit(solution)/shard_map/dot_general | solution.py:120
  16.4 0.1 pad_add_fusion.1.me
  16.6 4.6 %compress.2 = (f32[128,2560]{1,0:T(8,128)S(1)}, f32[2,16,2,16,128]{4,3,2,1,0:T(8,128)}) custom-call(s32[2]{0:T(128)S(1)} %pad_add_fusion.1.me, f32[256,2560]{1,0:T(8,128)S(1)} %fusion.2.own, f32[256,2560]{1,0:T(8,128)S(1)} %collective-permute-done.2.got, f32[1,128,5120]{2,1,0:T(8,128)S(1)} %copy-done, s32[2,2,32,128]{3,2,1,0:T(8,128)S(1)} %pad_add_fusion.picks, ...), custom_call_target="tpu_custom_call" | custom-call | flops 1000 | bytes 1000 | tf_op jit(solution)/shard_map/compress/pallas_call | solution.py:245
  21.2 5.3 %compress.3 = (s16[4,656,128]{2,1,0:T(8,128)(2,1)}, f32[128,2560]{1,0:T(8,128)S(1)}, f32[2,16,2,16,128]{4,3,2,1,0:T(8,128)}) custom-call(s32[2]{0:T(128)S(1)} %pad_add_fusion.1.me, f32[256,2560]{1,0:T(8,128)S(1)} %fusion.6.own, f32[256,2560]{1,0:T(8,128)S(1)} %collective-permute-done.got, ...), custom_call_target="tpu_custom_call", output_to_operand_aliasing={{2}: (8, {})} | custom-call | flops 1000 | bytes 1000 | tf_op jit(solution)/shard_map/compress/pallas_call | solution.py:245
  26.5 1.1 copy-done.3
  27.6 0.3 collective-permute-start.4
  27.8 1.7 %collective-permute-done.3.q = s16[4,656,128]{2,1,0:T(8,128)(2,1)S(1)} collective-permute-done((s16[4,656,128]{2,1,0:T(8,128)(2,1)S(1)}, s16[4,656,128]{2,1,0:T(8,128)(2,1)S(1)}, u32[]{:S(2)}, u32[]{:S(2)}) %collective-permute-start.3) | collective-permute-done | bytes 671776 | tf_op jit(solution)/shard_map/ppermute | solution.py:491
  29.5 0.8 copy-done.7
  30.4 11.5 %all-to-all-start = ((f32[64,16,128]{2,1,0:T(8,128)}), f32[64,16,128]{2,1,0:T(8,128)S(1)}, u32[]{:S(2)}, u32[]{:S(2)}) async-start(f32[64,16,128]{2,1,0:T(8,128)} %bitcast.6), calls=%async_computation | async-start | bytes 1048576 | tf_op jit(solution)/shard_map/all_to_all | solution.py:496
  41.9 0.0 copy-start.1
  41.9 0.0 copy-start.8
  41.9 1.2 %copy-done.8 = s16[4,656,128]{2,1,0:T(8,128)(2,1)S(1)} copy-done((s16[4,656,128]{2,1,0:T(8,128)(2,1)S(1)}, s16[4,656,128]{2,1,0:T(8,128)(2,1)}, u32[]{:S(2)}) %copy-start.8) | copy-done | bytes 671768
  43.1 0.8 copy-done.10
  43.9 4.1 %left.2.refs_0_ = f32[1,128,5120]{2,1,0:T(8,128)} custom-call(s16[4,656,128]{2,1,0:T(8,128)(2,1)S(1)} %copy-done.8, f32[128,2560]{1,0:T(8,128)S(1)} %get-tuple-element.31.pm, s32[2,2,32,128]{3,2,1,0:T(8,128)S(1)} %pad_add_fusion.picks, bf16[256,256]{1,0:T(8,128)(2,1)S(1)} %copy-done.2, bf16[256,128]{1,0:T(8,128)(2,1)S(1)} %copy-done.10, ...), custom_call_target="tpu_custom_call" | custom-call | flops 1000 | bytes 1000 | tf_op jit(solution)/shard_map/left/pallas_call | solution.py:451
  48.0 6.8 %all-to-all-done.got = f32[64,16,128]{2,1,0:T(8,128)S(1)} async-done(((f32[64,16,128]{2,1,0:T(8,128)}), f32[64,16,128]{2,1,0:T(8,128)S(1)}, u32[]{:S(2)}, u32[]{:S(2)}) %all-to-all-start) | async-done | bytes 524320 | tf_op jit(solution)/shard_map/all_to_all | solution.py:496
  54.9 4.7 %owner.1 = s16[176,128]{1,0:T(8,128)(2,1)S(1)} custom-call(f32[64,16,128]{2,1,0:T(8,128)S(1)} %all-to-all-done.got, bf16[256,256]{1,0:T(8,128)(2,1)S(1)} %copy-done.5, bf16[256,128]{1,0:T(8,128)(2,1)S(1)} %copy-done.9), custom_call_target="tpu_custom_call" | custom-call | tf_op jit(solution)/shard_map/owner/pallas_call | solution.py:308
  59.6 0.2 broadcast_in_dim.3
  59.7 0.0 copy-start.4
  59.8 0.0 copy-start.11
  59.8 26.8 %all_to_all.10.got = s16[32,176,128]{2,1,0:T(8,128)(2,1)S(1)} all-to-all(s16[32,176,128]{2,1,0:T(8,128)(2,1)S(1)} %broadcast_in_dim.3), channel_id=1, replica_groups=mesh['x'=4,'z'=4,'yh'=2,'yl'=2,'c'=2] {'x','z','yh'}, dimensions={0} | all-to-all | bytes 2883584 | tf_op jit(solution)/shard_map/all_to_all | solution.py:501
  86.6 2.0 %finish.2 = (f32[128,5120]{1,0:T(8,128)}, bf16[64,5120]{1,0:T(8,128)(2,1)S(1)}) custom-call(s16[32,176,128]{2,1,0:T(8,128)(2,1)S(1)} %all_to_all.10.got, bf16[128,5120]{1,0:T(8,128)(2,1)S(1)} %copy-done.1), custom_call_target="tpu_custom_call" | custom-call | flops 1000 | bytes 1000 | tf_op jit(solution)/shard_map/finish/pallas_call | solution.py:349
  88.6 2.0 %finish.3 = (f32[128,5120]{1,0:T(8,128)}, bf16[64,5120]{1,0:T(8,128)(2,1)S(1)}) custom-call(s16[32,176,128]{2,1,0:T(8,128)(2,1)S(1)} %all_to_all.10.got, bf16[128,5120]{1,0:T(8,128)(2,1)S(1)} %copy-done.1, f32[128,5120]{1,0:T(8,128)} %get-tuple-element.38.refs_0_), custom_call_target="tpu_custom_call", output_to_operand_aliasing={{0}: (2, {})} | custom-call | flops 1000 | bytes 1000 | tf_op jit(solution)/shard_map/finish/pallas_call | solution.py:349
  90.6 3.2 %collective-permute-start.8 = (bf16[64,5120]{1,0:T(8,128)(2,1)S(1)}, bf16[64,5120]{1,0:T(8,128)(2,1)S(1)}, u32[]{:S(2)}, u32[]{:S(2)}) collective-permute-start(bf16[64,5120]{1,0:T(8,128)(2,1)S(1)} %get-tuple-element.39.refs_1_), channel_id=1, source_target_pairs={{0,1},{1,0},{2,3},{3,2},{4,5},{5,4},{6,7},{7,6},{8,9},{9,8},{10,11... | collective-permute-start | bytes 1966088 | tf_op jit(solution)/shard_map/ppermute | solution.py:511
  93.8 0.4 collective-permute-start.6
  94.2 0.1 pad_add_fusion.2.rows
  94.3 5.0 %left.3 = f32[1,128,5120]{2,1,0:T(8,128)} custom-call(s16[4,656,128]{2,1,0:T(8,128)(2,1)} %collective-permute-done.4.q, f32[128,2560]{1,0:T(8,128)S(1)} %copy-done.4, s32[2,2,32,128]{3,2,1,0:T(8,128)S(1)} %pad_add_fusion.picks, bf16[256,256]{1,0:T(8,128)(2,1)S(1)} %copy-done.2, bf16[256,128]{1,0:T(8,128)(2,1)S(1)} %copy-done.11, ...), custom_call_target="tpu_custom_call", output_to_operand_aliasing={{}: (7, {})} | custom-call | flops 1000 | bytes 1000 | tf_op jit(solution)/shard_map/left/pallas_call | solution.py:451
  99.3 2.2 %gather.3.refs_2_ = bf16[512,5120]{1,0:T(8,128)(2,1)} custom-call(s32[4]{0:T(128)S(1)} %pad_add_fusion.2.rows, bf16[64,5120]{1,0:T(8,128)(2,1)S(1)} %get-tuple-element.37.refs_0_, bf16[64,5120]{1,0:T(8,128)(2,1)S(1)} %get-tuple-element.39.refs_1_, bf16[64,5120]{1,0:T(8,128)(2,1)S(1)} %collective-permute-done.7.refs_2_, ...), custom_call_target="tpu_custom_call" | custom-call | bytes 4194304 | tf_op jit(solution)/shard_map/gather/pallas_call | solution.py:381
  101.4 9.3 %collective-permute-done.6.refs_1_ = bf16[64,5120]{1,0:T(8,128)(2,1)S(1)} collective-permute-done((bf16[64,5120]{1,0:T(8,128)(2,1)S(1)}, bf16[64,5120]{1,0:T(8,128)(2,1)S(1)}, u32[]{:S(2)}, u32[]{:S(2)}) %collective-permute-start.6) | collective-permute-done | bytes 655392 | tf_op jit(solution)/shard_map/ppermute | solution.py:509
  110.8 1.4 %collective-permute-start.10 = (bf16[64,5120]{1,0:T(8,128)(2,1)S(1)}, bf16[64,5120]{1,0:T(8,128)(2,1)S(1)}, u32[]{:S(2)}, u32[]{:S(2)}) collective-permute-start(bf16[64,5120]{1,0:T(8,128)(2,1)S(1)} %collective-permute-done.6.refs_1_), channel_id=1, source_target_pairs={{0,1},{1,0},{2,3},{3,2},{4,5},{5,4},{6,7},{7,6},{8,9},{9,8},{10,11... | collective-permute-start | bytes 1966088 | tf_op jit(solution)/shard_map/ppermute | solution.py:515
  112.2 1.7 %gather.4.refs_2_ = bf16[512,5120]{1,0:T(8,128)(2,1)} custom-call(s32[2]{0:T(128)S(1)} %fusion.8.rows, bf16[64,5120]{1,0:T(8,128)(2,1)S(1)} %collective-permute-done.5.refs_0_, bf16[64,5120]{1,0:T(8,128)(2,1)S(1)} %collective-permute-done.6.refs_1_, bf16[512,5120]{1,0:T(8,128)(2,1)} %gather.3.refs_2_), custom_call_target="tpu_custom_call", output_to_operand_aliasing={{}: (3, {})} | custom-call | bytes 4194304 | tf_op jit(solution)/shard_map/gather/pallas_call | solution.py:381
  113.8 0.0 collective-permute-done.10.refs_1_
  113.9 0.9 collective-permute-done.9.refs_0_
  114.8 1.7 %gather.5 = bf16[512,5120]{1,0:T(8,128)(2,1)} custom-call(s32[2]{0:T(128)S(1)} %fusion.9.rows, bf16[64,5120]{1,0:T(8,128)(2,1)S(1)} %collective-permute-done.9.refs_0_, bf16[64,5120]{1,0:T(8,128)(2,1)S(1)} %collective-permute-done.10.refs_1_, bf16[512,5120]{1,0:T(8,128)(2,1)} %gather.4.refs_2_), custom_call_target="tpu_custom_call", output_to_operand_aliasing={{}: (3, {})} | custom-call | bytes 4194304 | tf_op jit(solution)/shard_map/gather/pallas_call | solution.py:381
  (31 shorter events, 0.1 us)
Async XLA Ops:
  0.6 7.3 %copy-start.14 = (bf16[1024,5120]{1,0:T(8,128)(2,1)S(1)}, bf16[1024,5120]{1,0:T(8,128)(2,1)}, u32[]{:S(2)}) copy-start(bf16[1024,5120]{1,0:T(8,128)(2,1)} %param.12) | copy-start | bytes 31457284
  6.4 3.2 %copy-start.13 = (s32[1,2,80,32]{2,3,1,0:T(8,128)S(1)}, s32[1,2,80,32]{2,3,1,0:T(8,128)}, u32[]{:S(2)}) copy-start(s32[1,2,80,32]{2,3,1,0:T(8,128)} %param.14) | copy-start | bytes 61444
  6.4 6.2 %collective-permute-start.2 = (f32[256,2560]{1,0:T(8,128)S(1)}, f32[256,2560]{1,0:T(8,128)S(1)}, u32[]{:S(2)}, u32[]{:S(2)}) collective-permute-start(f32[256,2560]{1,0:T(8,128)S(1)} %fusion), channel_id=1, source_target_pairs={{0,1},{1,0},{2,3},{3,2},{4,5},{5,4},{6,7},{7,6},{8,9},{9,8},{10,11... | collective-permute-start | bytes 7864328 | tf_op jit(solution)/shard_map/ppermute | solution.py:488
  9.5 11.7 %collective-permute-start = (f32[256,2560]{1,0:T(8,128)S(1)}, f32[256,2560]{1,0:T(8,128)S(1)}, u32[]{:S(2)}, u32[]{:S(2)}) collective-permute-start(f32[256,2560]{1,0:T(8,128)S(1)} %fusion.4), channel_id=1, source_target_pairs={{0,1},{1,0},{2,3},{3,2},{4,5},{5,4},{6,7},{7,6},{8,9},{9,8},{10,11... | collective-permute-start | bytes 7864328 | tf_op jit(solution)/shard_map/ppermute | solution.py:488
  9.6 6.9 %collective-permute-start.1 = (s32[2,32,128]{2,1,0:T(8,128)S(1)}, s32[2,32,128]{2,1,0:T(8,128)S(1)}, u32[]{:S(2)}, u32[]{:S(2)}) collective-permute-start(s32[2,32,128]{2,1,0:T(8,128)S(1)} %get-tuple-element.56), channel_id=1, source_target_pairs={{0,2},{2,0},{4,6},{6,4},{1,3},{3,1},{5,7},{7,5},{8,10},{10,8},{12,... | collective-permute-start | bytes 98312 | tf_op jit(solution)/shard_map/ppermute | solution.py:482
  13.6 3.0 %copy-start = (f32[1,128,5120]{2,1,0:T(8,128)S(1)}, f32[1,128,5120]{2,1,0:T(8,128)}, u32[]{:S(2)}) copy-start(f32[1,128,5120]{2,1,0:T(8,128)} %mom.3) | copy-start | bytes 7864324
  13.6 3.0 %copy-start.2 = (bf16[256,256]{1,0:T(8,128)(2,1)S(1)}, bf16[256,256]{1,0:T(8,128)(2,1)}, u32[]{:S(2)}) copy-start(bf16[256,256]{1,0:T(8,128)(2,1)} %constant.30.clone.rt) | copy-start | bytes 393220
  13.6 2.9 %copy-start.6 = (bf16[512,256]{1,0:T(8,128)(2,1)S(1)}, bf16[512,256]{1,0:T(8,128)(2,1)}, u32[]{:S(2)}) copy-start(bf16[512,256]{1,0:T(8,128)(2,1)} %constant.32.clone.lt) | copy-start | bytes 786436
  13.6 2.9 %copy-start.12 = (s32[2,8,128]{2,1,0:T(8,128)S(1)}, s32[2,8,128]{2,1,0:T(8,128)}, u32[]{:S(2)}) copy-start(s32[2,8,128]{2,1,0:T(8,128)} %constant.35.clone.tab) | copy-start | bytes 24580
  13.6 15.9 %collective-permute-start.3 = (s16[4,656,128]{2,1,0:T(8,128)(2,1)S(1)}, s16[4,656,128]{2,1,0:T(8,128)(2,1)S(1)}, u32[]{:S(2)}, u32[]{:S(2)}) collective-permute-start(s16[4,656,128]{2,1,0:T(8,128)(2,1)S(1)} %code.1), channel_id=1, source_target_pairs={{0,2},{2,0},{4,6},{6,4},{1,3},{3,1},{5,7},{7,5},{8,10},{10,8},{12,... | collective-permute-start | bytes 2015240 | tf_op jit(solution)/shard_map/ppermute | solution.py:491
  21.2 20.7 %copy-start.5 = (bf16[256,256]{1,0:T(8,128)(2,1)S(1)}, bf16[256,256]{1,0:T(8,128)(2,1)}, u32[]{:S(2)}) copy-start(bf16[256,256]{1,0:T(8,128)(2,1)} %constant.31.clone.irt.rt) | copy-start | bytes 393220
  21.2 20.7 %copy-start.9 = (bf16[256,128]{1,0:T(8,128)(2,1)S(1)}, bf16[256,128]{1,0:T(8,128)(2,1)}, u32[]{:S(2)}) copy-start(bf16[256,128]{1,0:T(8,128)(2,1)} %constant.34.clone.ilt.lt) | copy-start | bytes 196612
  26.5 1.1 copy-start.3
  27.6 32.0 %collective-permute-start.4 = (s16[4,656,128]{2,1,0:T(8,128)(2,1)}, s16[4,656,128]{2,1,0:T(8,128)(2,1)}, u32[]{:S(2)}, u32[]{:S(2)}) collective-permute-start(s16[4,656,128]{2,1,0:T(8,128)(2,1)} %get-tuple-element.33), channel_id=1, source_target_pairs={{0,2},{2,0},{4,6},{6,4},{1,3},{3,1},{5,7},{7,5},{8,10},{10,8},{12,... | collective-permute-start | bytes 2015240 | tf_op jit(solution)/shard_map/ppermute | solution.py:494
  29.5 0.8 copy-start.7
  30.4 24.5 %all-to-all-start = ((f32[64,16,128]{2,1,0:T(8,128)}), f32[64,16,128]{2,1,0:T(8,128)S(1)}, u32[]{:S(2)}, u32[]{:S(2)}) async-start(f32[64,16,128]{2,1,0:T(8,128)} %bitcast.6), calls=%async_computation | async-start | bytes 1048576 | tf_op jit(solution)/shard_map/all_to_all | solution.py:496
  41.9 44.7 %copy-start.1 = (bf16[128,5120]{1,0:T(8,128)(2,1)S(1)}, bf16[128,5120]{1,0:T(8,128)(2,1)}, u32[]{:S(2)}) copy-start(bf16[128,5120]{1,0:T(8,128)(2,1)} %par.3) | copy-start | bytes 3932164
  41.9 1.2 %copy-start.8 = (s16[4,656,128]{2,1,0:T(8,128)(2,1)S(1)}, s16[4,656,128]{2,1,0:T(8,128)(2,1)}, u32[]{:S(2)}) copy-start(s16[4,656,128]{2,1,0:T(8,128)(2,1)} %copy-done.7) | copy-start | bytes 2015236
  43.1 0.8 copy-start.10
  59.7 34.5 %copy-start.4 = (f32[128,2560]{1,0:T(8,128)S(1)}, f32[128,2560]{1,0:T(8,128)}, u32[]{:S(2)}) copy-start(f32[128,2560]{1,0:T(8,128)} %copy-done.3) | copy-start | bytes 3932164
  59.8 34.5 %copy-start.11 = (bf16[256,128]{1,0:T(8,128)(2,1)S(1)}, bf16[256,128]{1,0:T(8,128)(2,1)}, u32[]{:S(2)}) copy-start(bf16[256,128]{1,0:T(8,128)(2,1)} %constant.33.clone.lt) | copy-start | bytes 196612
  90.6 8.6 %collective-permute-start.8 = (bf16[64,5120]{1,0:T(8,128)(2,1)S(1)}, bf16[64,5120]{1,0:T(8,128)(2,1)S(1)}, u32[]{:S(2)}, u32[]{:S(2)}) collective-permute-start(bf16[64,5120]{1,0:T(8,128)(2,1)S(1)} %get-tuple-element.39.refs_1_), channel_id=1, source_target_pairs={{0,1},{1,0},{2,3},{3,2},{4,5},{5,4},{6,7},{7,6},{8,9},{9,8},{10,11... | collective-permute-start | bytes 1966088 | tf_op jit(solution)/shard_map/ppermute | solution.py:511
  93.8 5.5 %collective-permute-start.7 = (bf16[64,5120]{1,0:T(8,128)(2,1)S(1)}, bf16[64,5120]{1,0:T(8,128)(2,1)S(1)}, u32[]{:S(2)}, u32[]{:S(2)}) collective-permute-start(bf16[64,5120]{1,0:T(8,128)(2,1)S(1)} %get-tuple-element.37.refs_0_), channel_id=1, source_target_pairs={{0,1},{1,0},{2,3},{3,2},{4,5},{5,4},{6,7},{7,6},{8,9},{9,8},{10,11... | collective-permute-start | bytes 1966088 | tf_op jit(solution)/shard_map/ppermute | solution.py:511
  93.8 17.0 %collective-permute-start.6 = (bf16[64,5120]{1,0:T(8,128)(2,1)S(1)}, bf16[64,5120]{1,0:T(8,128)(2,1)S(1)}, u32[]{:S(2)}, u32[]{:S(2)}) collective-permute-start(bf16[64,5120]{1,0:T(8,128)(2,1)S(1)} %get-tuple-element.39.refs_1_), channel_id=1, source_target_pairs={{0,6},{2,4},{4,2},{6,0},{1,7},{3,5},{5,3},{7,1},{8,14},{10,12},{12... | collective-permute-start | bytes 1966088 | tf_op jit(solution)/shard_map/ppermute | solution.py:509
  94.2 16.6 %collective-permute-start.5 = (bf16[64,5120]{1,0:T(8,128)(2,1)S(1)}, bf16[64,5120]{1,0:T(8,128)(2,1)S(1)}, u32[]{:S(2)}, u32[]{:S(2)}) collective-permute-start(bf16[64,5120]{1,0:T(8,128)(2,1)S(1)} %get-tuple-element.37.refs_0_), channel_id=1, source_target_pairs={{0,2},{2,0},{4,6},{6,4},{1,3},{3,1},{5,7},{7,5},{8,10},{10,8},{12,... | collective-permute-start | bytes 1966088 | tf_op jit(solution)/shard_map/ppermute | solution.py:507
  110.8 3.1 %collective-permute-start.10 = (bf16[64,5120]{1,0:T(8,128)(2,1)S(1)}, bf16[64,5120]{1,0:T(8,128)(2,1)S(1)}, u32[]{:S(2)}, u32[]{:S(2)}) collective-permute-start(bf16[64,5120]{1,0:T(8,128)(2,1)S(1)} %collective-permute-done.6.refs_1_), channel_id=1, source_target_pairs={{0,1},{1,0},{2,3},{3,2},{4,5},{5,4},{6,7},{7,6},{8,9},{9,8},{10,11... | collective-permute-start | bytes 1966088 | tf_op jit(solution)/shard_map/ppermute | solution.py:515
  112.2 2.7 %collective-permute-start.9 = (bf16[64,5120]{1,0:T(8,128)(2,1)S(1)}, bf16[64,5120]{1,0:T(8,128)(2,1)S(1)}, u32[]{:S(2)}, u32[]{:S(2)}) collective-permute-start(bf16[64,5120]{1,0:T(8,128)(2,1)S(1)} %collective-permute-done.5.refs_0_), channel_id=1, source_target_pairs={{0,1},{1,0},{2,3},{3,2},{4,5},{5,4},{6,7},{7,6},{8,9},{9,8},{10,11... | collective-permute-start | bytes 1966088 | tf_op jit(solution)/shard_map/ppermute | solution.py:515

commit v4 on v3

--- a/solution.py
+++ b/solution.py
@@ -327,36 +327,31 @@
     return [even[:64], even[64:128], jnp.concatenate([top, bottom], axis=0), odd[:64], odd[64:128]]
 
 
-def finish_kernel(got, par, *refs):
-    update, new = refs[-2:]
-    for pair in range(LEFT):
-        for t, u in enumerate(decode(got, pair)):
-            cols = slice(GW * pair + 128 * t, GW * pair + 128 * t + 128)
-            update[:, cols] = u
-            new[:, cols] = (par[:, cols].astype(F32) - STEP * u).astype(BF16)
-
-
-def finish(a, got, par, before):
+def finish_kernel(got0, got1, par, update, low, high):
+    for a, (got, new) in enumerate(((got0, low), (got1, high))):
+        rows = slice(64 * a, 64 * a + 64)
+        for pair in range(LEFT):
+            for t, u in enumerate(decode(got, pair)):
+                cols = slice(GW * pair + 128 * t, GW * pair + 128 * t + 128)
+                update[rows, cols] = u
+                new[:, cols] = (par[rows, cols].astype(F32) - STEP * u).astype(BF16)
+
+
+def finish(got, par):
     n = PAIRS // LEFT
-    half = pl.BlockSpec((64, LEFT * GW), lambda i: (a, i))
-    args = [got, par]
-    in_specs = [pl.BlockSpec((2 * LEFT, UROWS, 128), lambda i: (n * a + i, 0, 0)), half]
-    alias = {}
-    if before is not None:
-        args.append(before)
-        in_specs.append(pl.BlockSpec(memory_space=pl.ANY))
-        alias = {2: 0}
+    col = lambda r: pl.BlockSpec((r, LEFT * GW), lambda i: (0, i))
+    blocks = lambda a: pl.BlockSpec((2 * LEFT, UROWS, 128), lambda i: (n * a + i, 0, 0))
+    half = jax.ShapeDtypeStruct((64, 5120), BF16)
     return pl.pallas_call(
         finish_kernel,
         grid=(n,),
-        in_specs=in_specs,
-        out_specs=[half, pl.BlockSpec((64, LEFT * GW), lambda i: (0, i))],
-        out_shape=[jax.ShapeDtypeStruct((128, 5120), F32), jax.ShapeDtypeStruct((64, 5120), BF16)],
-        input_output_aliases=alias,
+        in_specs=[blocks(0), blocks(1), col(128)],
+        out_specs=[col(128), col(64), col(64)],
+        out_shape=[jax.ShapeDtypeStruct((128, 5120), F32), half, half],
         compiler_params=ARB,
         cost_estimate=SHORT,
         name="finish",
-    )(*args)
+    )(got, got, par)
 
 
 def gather_kernel(n, rows, *refs):
@@ -503,9 +498,8 @@
 
     yl = lax.axis_index("yl")
     rows = lambda y, c: (128 * (2 * y + c) + 64 * jnp.arange(2)).astype(I32)
-    update, low = finish(0, every, params, None)
+    update, low, high = finish(every, params)
     far_low = lax.ppermute(low, ("yh", "yl"), NEAR)
-    update, high = finish(1, every, params, update)
     far_high = lax.ppermute(high, ("yh", "yl"), FAR)
     momentum_left = left(1, q1, pm1, picks, rt, lt, irt, ilt, momentum_left)
     other = [lax.ppermute(v, "c", SWAP) for v in (low, high)]

time: 117 us -> 116 us (level)
  Pallas kernels: 34.1 us -> 32.7 us
    ppermute x1, waiting for transfers between devices: 9.34 us -> 1.18 us  [body(): far_high = lax.ppermute(high, ('yh', 'yl'), FAR)]
    ppermute x1, waiting for transfers between devices: 0.01 us -> 7.57 us  [body(): far_low = lax.ppermute(low, ('yh', 'yl'), NEAR)]
    pallas_call x2 -> x1, Pallas kernels: 4.05 us -> 2.62 us  [finish(): pl.pallas_call(finish_kernel, grid=(n,), in_specs=[blocks(0), blocks(1),...]
  transfers between devices with their start and end apart: 12 -> 12, of which waited for: 4 -> 5; matrix products, arithmetic and copies ran while one was open for 4% -> 4% of each run, Pallas kernels for 24% -> 25%
where the time goes in v4:
time: 116 us; the launch traced here: 115 us
  Pallas kernels  32.7 us (28%)
  blocking collectives  26.7 us (23%)
  starting transfers between devices  21.9 us (19%)
  waiting for transfers between devices  18.3 us (16%)
  matrix products  8.98 us (8%)
  local copies, waits for them, and re-layouts  5.62 us (5%)
    all_to_all x1, blocking collectives, body(): lax.all_to_all(jnp.broadcast_to(mine16, (32, UROWS, 128)), REP, 0, 0, til...  26.7 us
    all_to_all x1, starting transfers between devices, body(): lax.all_to_all(comp.reshape(64, 16, 128), REP + ('yl',), 0, 0, tiled=True)  11.5 us
    pallas_call x2, Pallas kernels, compress(): pl.pallas_call(functools.partial(compress_kernel, part, with_code), grid_...  9.94 us
    pallas_call x2, Pallas kernels, left(): pl.pallas_call(functools.partial(left_kernel, part), grid=(n,), in_specs=...  9.08 us
    dot_general x4, matrix products, term(): lax.dot_general(hidden, right, (((0,), (0,)), ((), ())), preferred_elemen...  8.98 us
    ppermute x1, waiting for transfers between devices, body(): far_low = lax.ppermute(low, ('yh', 'yl'), NEAR)  7.57 us
    all_to_all x1, waiting for transfers between devices, body(): lax.all_to_all(comp.reshape(64, 16, 128), REP + ('yl',), 0, 0, tiled=True)  6.84 us
    pallas_call x3, Pallas kernels, gather(): pl.pallas_call(functools.partial(gather_kernel, n), grid_spec=pltpu.Prefe...  5.47 us
  transfers between devices with their start and end apart: 12, of which 5 were waited for; matrix products, arithmetic and copies ran while one was open for 4% of the time, Pallas kernels for 25%

profile of v4, /device:TPU:1, one launch (start us, length us, event | category | flops | bytes accessed | tf_op | source)
XLA Modules:
  0.0 115.3 jit_solution(17557022152571932915)
XLA Ops:
  0.6 0.0 copy-start.14
  0.7 1.4 %constant_dynamic-slice_fusion.1 = (bf16[1024,128]{1,0:T(8,128)(2,1)S(1)}, bf16[1024,128]{1,0:T(8,128)(2,1)S(1)}, bf16[1024,128]{1,0:T(8,128)(2,1)S(1)}, bf16[1024,128]{1,0:T(8,128)(2,1)S(1)}) fusion(bf16[1024,512]{1,0:T(8,128)(2,1)} %param.11, s32[]{:T(128)S(6)} %select_n.14, s32[]{:T(128)S(6)} %select_n.13, s32[]{:T(128)S(6)} %select_n.12, s32[]{:T(128)S(6)} %select_n.15), kind=kLoop, calls=%fused_computation.12 | loop fusion | bytes 2097168 | tf_op jit(solution)/shard_map/dynamic_slice | solution.py:125
  2.1 4.3 %fusion = f32[256,2560]{1,0:T(8,128)S(1)} fusion(bf16[1024,5120]{1,0:T(8,128)(2,1)} %param.12, bf16[1024,128]{1,0:T(8,128)(2,1)S(1)} %get-tuple-element.52, bf16[1024,128]{1,0:T(8,128)(2,1)S(1)} %get-tuple-element.49), kind=kOutput, calls=%fused_computation | convolution fusion | flops 1343225856 | bytes 8388608 | tf_op jit(solution)/shard_map/dot_general | solution.py:120
  6.4 0.0 copy-start.13
  6.4 1.5 %collective-permute-start.2 = (f32[256,2560]{1,0:T(8,128)S(1)}, f32[256,2560]{1,0:T(8,128)S(1)}, u32[]{:S(2)}, u32[]{:S(2)}) collective-permute-start(f32[256,2560]{1,0:T(8,128)S(1)} %fusion), channel_id=1, source_target_pairs={{0,1},{1,0},{2,3},{3,2},{4,5},{5,4},{6,7},{7,6},{8,9},{9,8},{10,11... | collective-permute-start | bytes 7864328 | tf_op jit(solution)/shard_map/ppermute | solution.py:483
  7.9 1.6 %fusion.4 = f32[256,2560]{1,0:T(8,128)S(1)} fusion(bf16[1024,5120]{1,0:T(8,128)(2,1)S(1)} %copy-done.14, bf16[1024,128]{1,0:T(8,128)(2,1)S(1)} %get-tuple-element.52, bf16[1024,128]{1,0:T(8,128)(2,1)S(1)} %get-tuple-element.49), kind=kOutput, calls=%fused_computation.4 | convolution fusion | flops 1343225856 | bytes 8388608 | tf_op jit(solution)/shard_map/dot_general | solution.py:120
  9.5 0.1 collective-permute-start
  9.6 1.5 %collective-permute-start.1 = (s32[2,32,128]{2,1,0:T(8,128)S(1)}, s32[2,32,128]{2,1,0:T(8,128)S(1)}, u32[]{:S(2)}, u32[]{:S(2)}) collective-permute-start(s32[2,32,128]{2,1,0:T(8,128)S(1)} %get-tuple-element.54), channel_id=1, source_target_pairs={{0,2},{2,0},{4,6},{6,4},{1,3},{3,1},{5,7},{7,5},{8,10},{10,8},{12,... | collective-permute-start | bytes 98312 | tf_op jit(solution)/shard_map/ppermute | solution.py:477
  11.1 1.6 %fusion.2.own = f32[256,2560]{1,0:T(8,128)S(1)} fusion(bf16[1024,5120]{1,0:T(8,128)(2,1)S(1)} %copy-done.14, bf16[1024,128]{1,0:T(8,128)(2,1)S(1)} %get-tuple-element.50, bf16[1024,128]{1,0:T(8,128)(2,1)S(1)} %get-tuple-element.51), kind=kOutput, calls=%fused_computation.2 | convolution fusion | flops 1343225856 | bytes 8388608 | tf_op jit(solution)/shard_map/dot_general | solution.py:120
  12.7 0.9 code.1
  13.6 0.0 copy-start
  13.6 0.0 copy-start.1
  13.6 0.0 copy-start.6
  13.6 0.0 copy-start.12
  13.6 1.3 %collective-permute-start.3 = (s16[4,656,128]{2,1,0:T(8,128)(2,1)S(1)}, s16[4,656,128]{2,1,0:T(8,128)(2,1)S(1)}, u32[]{:S(2)}, u32[]{:S(2)}) collective-permute-start(s16[4,656,128]{2,1,0:T(8,128)(2,1)S(1)} %code.1), channel_id=1, source_target_pairs={{0,2},{2,0},{4,6},{6,4},{1,3},{3,1},{5,7},{7,5},{8,10},{10,8},{12,... | collective-permute-start | bytes 2015240 | tf_op jit(solution)/shard_map/ppermute | solution.py:486
  14.9 1.6 %fusion.6.own = f32[256,2560]{1,0:T(8,128)S(1)} fusion(bf16[1024,5120]{1,0:T(8,128)(2,1)S(1)} %copy-done.14, bf16[1024,128]{1,0:T(8,128)(2,1)S(1)} %get-tuple-element.50, bf16[1024,128]{1,0:T(8,128)(2,1)S(1)} %get-tuple-element.51), kind=kOutput, calls=%fused_computation.6 | convolution fusion | flops 1343225856 | bytes 8388608 | tf_op jit(solution)/shard_map/dot_general | solution.py:120
  16.4 0.1 pad_add_fusion.1.me
  16.6 4.7 %compress.2 = (f32[128,2560]{1,0:T(8,128)S(1)}, f32[2,16,2,16,128]{4,3,2,1,0:T(8,128)}) custom-call(s32[2]{0:T(128)S(1)} %pad_add_fusion.1.me, f32[256,2560]{1,0:T(8,128)S(1)} %fusion.2.own, f32[256,2560]{1,0:T(8,128)S(1)} %collective-permute-done.2.got, f32[1,128,5120]{2,1,0:T(8,128)S(1)} %copy-done, s32[2,2,32,128]{3,2,1,0:T(8,128)S(1)} %pad_add_fusion.picks, ...), custom_call_target="tpu_custom_call" | custom-call | flops 1000 | bytes 1000 | tf_op jit(solution)/shard_map/compress/pallas_call | solution.py:245
  21.2 5.3 %compress.3 = (s16[4,656,128]{2,1,0:T(8,128)(2,1)}, f32[128,2560]{1,0:T(8,128)S(1)}, f32[2,16,2,16,128]{4,3,2,1,0:T(8,128)}) custom-call(s32[2]{0:T(128)S(1)} %pad_add_fusion.1.me, f32[256,2560]{1,0:T(8,128)S(1)} %fusion.6.own, f32[256,2560]{1,0:T(8,128)S(1)} %collective-permute-done.got, ...), custom_call_target="tpu_custom_call", output_to_operand_aliasing={{2}: (8, {})} | custom-call | flops 1000 | bytes 1000 | tf_op jit(solution)/shard_map/compress/pallas_call | solution.py:245
  26.5 1.1 copy-done.3
  27.6 0.3 collective-permute-start.4
  27.8 1.7 %collective-permute-done.3.q = s16[4,656,128]{2,1,0:T(8,128)(2,1)S(1)} collective-permute-done((s16[4,656,128]{2,1,0:T(8,128)(2,1)S(1)}, s16[4,656,128]{2,1,0:T(8,128)(2,1)S(1)}, u32[]{:S(2)}, u32[]{:S(2)}) %collective-permute-start.3) | collective-permute-done | bytes 671776 | tf_op jit(solution)/shard_map/ppermute | solution.py:486
  29.5 0.8 copy-done.7
  30.4 11.5 %all-to-all-start = ((f32[64,16,128]{2,1,0:T(8,128)}), f32[64,16,128]{2,1,0:T(8,128)S(1)}, u32[]{:S(2)}, u32[]{:S(2)}) async-start(f32[64,16,128]{2,1,0:T(8,128)} %bitcast.6), calls=%async_computation | async-start | bytes 1048576 | tf_op jit(solution)/shard_map/all_to_all | solution.py:491
  41.9 0.0 copy-start.2
  41.9 0.0 copy-start.8
  41.9 1.2 %copy-done.8 = s16[4,656,128]{2,1,0:T(8,128)(2,1)S(1)} copy-done((s16[4,656,128]{2,1,0:T(8,128)(2,1)S(1)}, s16[4,656,128]{2,1,0:T(8,128)(2,1)}, u32[]{:S(2)}) %copy-start.8) | copy-done | bytes 671768
  43.1 0.8 copy-done.10
  43.9 4.1 %left.2.refs_0_ = f32[1,128,5120]{2,1,0:T(8,128)} custom-call(s16[4,656,128]{2,1,0:T(8,128)(2,1)S(1)} %copy-done.8, f32[128,2560]{1,0:T(8,128)S(1)} %get-tuple-element.30.pm, s32[2,2,32,128]{3,2,1,0:T(8,128)S(1)} %pad_add_fusion.picks, bf16[256,256]{1,0:T(8,128)(2,1)S(1)} %copy-done.1, bf16[256,128]{1,0:T(8,128)(2,1)S(1)} %copy-done.10, ...), custom_call_target="tpu_custom_call" | custom-call | flops 1000 | bytes 1000 | tf_op jit(solution)/shard_map/left/pallas_call | solution.py:446
  48.0 6.8 %all-to-all-done.got = f32[64,16,128]{2,1,0:T(8,128)S(1)} async-done(((f32[64,16,128]{2,1,0:T(8,128)}), f32[64,16,128]{2,1,0:T(8,128)S(1)}, u32[]{:S(2)}, u32[]{:S(2)}) %all-to-all-start) | async-done | bytes 524320 | tf_op jit(solution)/shard_map/all_to_all | solution.py:491
  54.9 4.7 %owner.1 = s16[176,128]{1,0:T(8,128)(2,1)S(1)} custom-call(f32[64,16,128]{2,1,0:T(8,128)S(1)} %all-to-all-done.got, bf16[256,256]{1,0:T(8,128)(2,1)S(1)} %copy-done.5, bf16[256,128]{1,0:T(8,128)(2,1)S(1)} %copy-done.9), custom_call_target="tpu_custom_call" | custom-call | tf_op jit(solution)/shard_map/owner/pallas_call | solution.py:308
  59.6 0.2 broadcast_in_dim.3
  59.7 26.7 %all_to_all.10.got0.got1 = s16[32,176,128]{2,1,0:T(8,128)(2,1)S(1)} all-to-all(s16[32,176,128]{2,1,0:T(8,128)(2,1)S(1)} %broadcast_in_dim.3), channel_id=1, replica_groups=mesh['x'=4,'z'=4,'yh'=2,'yl'=2,'c'=2] {'x','z','yh'}, dimensions={0} | all-to-all | bytes 2883584 | tf_op jit(solution)/shard_map/all_to_all | solution.py:496
  86.4 2.6 %finish.1 = (f32[128,5120]{1,0:T(8,128)}, bf16[64,5120]{1,0:T(8,128)(2,1)S(1)}, bf16[64,5120]{1,0:T(8,128)(2,1)S(1)}) custom-call(s16[32,176,128]{2,1,0:T(8,128)(2,1)S(1)} %all_to_all.10.got0.got1, s16[32,176,128]{2,1,0:T(8,128)(2,1)S(1)} %all_to_all.10.got0.got1, bf16[128,5120]{1,0:T(8,128)(2,1)S(1)} %copy-done.2), custom_call_target="tpu_custom_call" | custom-call | flops 1000 | bytes 1000 | tf_op jit(solution)/shard_map/finish/pallas_call | solution.py:345
  89.0 3.2 %collective-permute-start.7 = (bf16[64,5120]{1,0:T(8,128)(2,1)S(1)}, bf16[64,5120]{1,0:T(8,128)(2,1)S(1)}, u32[]{:S(2)}, u32[]{:S(2)}) collective-permute-start(bf16[64,5120]{1,0:T(8,128)(2,1)S(1)} %get-tuple-element.36.refs_0_), channel_id=1, source_target_pairs={{0,1},{1,0},{2,3},{3,2},{4,5},{5,4},{6,7},{7,6},{8,9},{9,8},{10,11... | collective-permute-start | bytes 1966088 | tf_op jit(solution)/shard_map/ppermute | solution.py:505
  92.2 0.3 collective-permute-start.5
  92.5 0.7 collective-permute-start.6
  93.2 0.1 pad_add_fusion.2.rows
  93.3 5.0 %left.3 = f32[1,128,5120]{2,1,0:T(8,128)} custom-call(s16[4,656,128]{2,1,0:T(8,128)(2,1)} %collective-permute-done.4.q, f32[128,2560]{1,0:T(8,128)S(1)} %copy-done.4, s32[2,2,32,128]{3,2,1,0:T(8,128)S(1)} %pad_add_fusion.picks, bf16[256,256]{1,0:T(8,128)(2,1)S(1)} %copy-done.1, bf16[256,128]{1,0:T(8,128)(2,1)S(1)} %copy-done.11, ...), custom_call_target="tpu_custom_call", output_to_operand_aliasing={{}: (7, {})} | custom-call | flops 1000 | bytes 1000 | tf_op jit(solution)/shard_map/left/pallas_call | solution.py:446
  98.3 2.2 %gather.3.refs_2_ = bf16[512,5120]{1,0:T(8,128)(2,1)} custom-call(s32[4]{0:T(128)S(1)} %pad_add_fusion.2.rows, bf16[64,5120]{1,0:T(8,128)(2,1)S(1)} %get-tuple-element.36.refs_0_, bf16[64,5120]{1,0:T(8,128)(2,1)S(1)} %get-tuple-element.37.refs_1_, bf16[64,5120]{1,0:T(8,128)(2,1)S(1)} %collective-permute-done.7.refs_2_, ...), custom_call_target="tpu_custom_call" | custom-call | bytes 4194304 | tf_op jit(solution)/shard_map/gather/pallas_call | solution.py:376
  100.4 7.6 %collective-permute-done.5.refs_0_ = bf16[64,5120]{1,0:T(8,128)(2,1)S(1)} collective-permute-done((bf16[64,5120]{1,0:T(8,128)(2,1)S(1)}, bf16[64,5120]{1,0:T(8,128)(2,1)S(1)}, u32[]{:S(2)}, u32[]{:S(2)}) %collective-permute-start.5) | collective-permute-done | bytes 655392 | tf_op jit(solution)/shard_map/ppermute | solution.py:502
  108.0 1.2 %collective-permute-done.6.refs_1_ = bf16[64,5120]{1,0:T(8,128)(2,1)S(1)} collective-permute-done((bf16[64,5120]{1,0:T(8,128)(2,1)S(1)}, bf16[64,5120]{1,0:T(8,128)(2,1)S(1)}, u32[]{:S(2)}, u32[]{:S(2)}) %collective-permute-start.6) | collective-permute-done | bytes 655392 | tf_op jit(solution)/shard_map/ppermute | solution.py:503
  109.2 1.7 %collective-permute-start.10 = (bf16[64,5120]{1,0:T(8,128)(2,1)S(1)}, bf16[64,5120]{1,0:T(8,128)(2,1)S(1)}, u32[]{:S(2)}, u32[]{:S(2)}) collective-permute-start(bf16[64,5120]{1,0:T(8,128)(2,1)S(1)} %collective-permute-done.6.refs_1_), channel_id=1, source_target_pairs={{0,1},{1,0},{2,3},{3,2},{4,5},{5,4},{6,7},{7,6},{8,9},{9,8},{10,11... | collective-permute-start | bytes 1966088 | tf_op jit(solution)/shard_map/ppermute | solution.py:509
  110.9 0.0 collective-permute-start.9
  110.9 1.7 %gather.4.refs_2_ = bf16[512,5120]{1,0:T(8,128)(2,1)} custom-call(s32[2]{0:T(128)S(1)} %fusion.8.rows, bf16[64,5120]{1,0:T(8,128)(2,1)S(1)} %collective-permute-done.5.refs_0_, bf16[64,5120]{1,0:T(8,128)(2,1)S(1)} %collective-permute-done.6.refs_1_, bf16[512,5120]{1,0:T(8,128)(2,1)} %gather.3.refs_2_), custom_call_target="tpu_custom_call", output_to_operand_aliasing={{}: (3, {})} | custom-call | bytes 4194304 | tf_op jit(solution)/shard_map/gather/pallas_call | solution.py:376
  112.5 0.0 collective-permute-done.10.refs_1_
  112.6 0.9 collective-permute-done.9.refs_0_
  113.5 1.7 %gather.5 = bf16[512,5120]{1,0:T(8,128)(2,1)} custom-call(s32[2]{0:T(128)S(1)} %fusion.9.rows, bf16[64,5120]{1,0:T(8,128)(2,1)S(1)} %collective-permute-done.9.refs_0_, bf16[64,5120]{1,0:T(8,128)(2,1)S(1)} %collective-permute-done.10.refs_1_, bf16[512,5120]{1,0:T(8,128)(2,1)} %gather.4.refs_2_), custom_call_target="tpu_custom_call", output_to_operand_aliasing={{}: (3, {})} | custom-call | bytes 4194304 | tf_op jit(solution)/shard_map/gather/pallas_call | solution.py:376
  (30 shorter events, 0.1 us)
Async XLA Ops:
  0.6 7.3 %copy-start.14 = (bf16[1024,5120]{1,0:T(8,128)(2,1)S(1)}, bf16[1024,5120]{1,0:T(8,128)(2,1)}, u32[]{:S(2)}) copy-start(bf16[1024,5120]{1,0:T(8,128)(2,1)} %param.12) | copy-start | bytes 31457284
  6.4 3.2 %copy-start.13 = (s32[1,2,80,32]{2,3,1,0:T(8,128)S(1)}, s32[1,2,80,32]{2,3,1,0:T(8,128)}, u32[]{:S(2)}) copy-start(s32[1,2,80,32]{2,3,1,0:T(8,128)} %param.14) | copy-start | bytes 61444
  6.4 6.2 %collective-permute-start.2 = (f32[256,2560]{1,0:T(8,128)S(1)}, f32[256,2560]{1,0:T(8,128)S(1)}, u32[]{:S(2)}, u32[]{:S(2)}) collective-permute-start(f32[256,2560]{1,0:T(8,128)S(1)} %fusion), channel_id=1, source_target_pairs={{0,1},{1,0},{2,3},{3,2},{4,5},{5,4},{6,7},{7,6},{8,9},{9,8},{10,11... | collective-permute-start | bytes 7864328 | tf_op jit(solution)/shard_map/ppermute | solution.py:483
  9.5 11.7 %collective-permute-start = (f32[256,2560]{1,0:T(8,128)S(1)}, f32[256,2560]{1,0:T(8,128)S(1)}, u32[]{:S(2)}, u32[]{:S(2)}) collective-permute-start(f32[256,2560]{1,0:T(8,128)S(1)} %fusion.4), channel_id=1, source_target_pairs={{0,1},{1,0},{2,3},{3,2},{4,5},{5,4},{6,7},{7,6},{8,9},{9,8},{10,11... | collective-permute-start | bytes 7864328 | tf_op jit(solution)/shard_map/ppermute | solution.py:483
  9.6 6.9 %collective-permute-start.1 = (s32[2,32,128]{2,1,0:T(8,128)S(1)}, s32[2,32,128]{2,1,0:T(8,128)S(1)}, u32[]{:S(2)}, u32[]{:S(2)}) collective-permute-start(s32[2,32,128]{2,1,0:T(8,128)S(1)} %get-tuple-element.54), channel_id=1, source_target_pairs={{0,2},{2,0},{4,6},{6,4},{1,3},{3,1},{5,7},{7,5},{8,10},{10,8},{12,... | collective-permute-start | bytes 98312 | tf_op jit(solution)/shard_map/ppermute | solution.py:477
  13.6 3.0 %copy-start = (f32[1,128,5120]{2,1,0:T(8,128)S(1)}, f32[1,128,5120]{2,1,0:T(8,128)}, u32[]{:S(2)}) copy-start(f32[1,128,5120]{2,1,0:T(8,128)} %mom.3) | copy-start | bytes 7864324
  13.6 3.0 %copy-start.1 = (bf16[256,256]{1,0:T(8,128)(2,1)S(1)}, bf16[256,256]{1,0:T(8,128)(2,1)}, u32[]{:S(2)}) copy-start(bf16[256,256]{1,0:T(8,128)(2,1)} %constant.30.clone.rt) | copy-start | bytes 393220
  13.6 2.9 %copy-start.6 = (bf16[512,256]{1,0:T(8,128)(2,1)S(1)}, bf16[512,256]{1,0:T(8,128)(2,1)}, u32[]{:S(2)}) copy-start(bf16[512,256]{1,0:T(8,128)(2,1)} %constant.32.clone.lt) | copy-start | bytes 786436
  13.6 2.9 %copy-start.12 = (s32[2,8,128]{2,1,0:T(8,128)S(1)}, s32[2,8,128]{2,1,0:T(8,128)}, u32[]{:S(2)}) copy-start(s32[2,8,128]{2,1,0:T(8,128)} %constant.35.clone.tab) | copy-start | bytes 24580
  13.6 15.9 %collective-permute-start.3 = (s16[4,656,128]{2,1,0:T(8,128)(2,1)S(1)}, s16[4,656,128]{2,1,0:T(8,128)(2,1)S(1)}, u32[]{:S(2)}, u32[]{:S(2)}) collective-permute-start(s16[4,656,128]{2,1,0:T(8,128)(2,1)S(1)} %code.1), channel_id=1, source_target_pairs={{0,2},{2,0},{4,6},{6,4},{1,3},{3,1},{5,7},{7,5},{8,10},{10,8},{12,... | collective-permute-start | bytes 2015240 | tf_op jit(solution)/shard_map/ppermute | solution.py:486
  21.2 20.7 %copy-start.5 = (bf16[256,256]{1,0:T(8,128)(2,1)S(1)}, bf16[256,256]{1,0:T(8,128)(2,1)}, u32[]{:S(2)}) copy-start(bf16[256,256]{1,0:T(8,128)(2,1)} %constant.31.clone.irt.rt) | copy-start | bytes 393220
  21.2 20.7 %copy-start.9 = (bf16[256,128]{1,0:T(8,128)(2,1)S(1)}, bf16[256,128]{1,0:T(8,128)(2,1)}, u32[]{:S(2)}) copy-start(bf16[256,128]{1,0:T(8,128)(2,1)} %constant.34.clone.ilt.lt) | copy-start | bytes 196612
  26.5 1.1 copy-start.3
  27.6 32.0 %collective-permute-start.4 = (s16[4,656,128]{2,1,0:T(8,128)(2,1)}, s16[4,656,128]{2,1,0:T(8,128)(2,1)}, u32[]{:S(2)}, u32[]{:S(2)}) collective-permute-start(s16[4,656,128]{2,1,0:T(8,128)(2,1)} %get-tuple-element.32), channel_id=1, source_target_pairs={{0,2},{2,0},{4,6},{6,4},{1,3},{3,1},{5,7},{7,5},{8,10},{10,8},{12,... | collective-permute-start | bytes 2015240 | tf_op jit(solution)/shard_map/ppermute | solution.py:489
  29.5 0.8 copy-start.7
  30.4 24.5 %all-to-all-start = ((f32[64,16,128]{2,1,0:T(8,128)}), f32[64,16,128]{2,1,0:T(8,128)S(1)}, u32[]{:S(2)}, u32[]{:S(2)}) async-start(f32[64,16,128]{2,1,0:T(8,128)} %bitcast.6), calls=%async_computation | async-start | bytes 1048576 | tf_op jit(solution)/shard_map/all_to_all | solution.py:491
  41.9 44.6 %copy-start.2 = (bf16[128,5120]{1,0:T(8,128)(2,1)S(1)}, bf16[128,5120]{1,0:T(8,128)(2,1)}, u32[]{:S(2)}) copy-start(bf16[128,5120]{1,0:T(8,128)(2,1)} %par.1) | copy-start | bytes 3932164
  41.9 1.2 %copy-start.8 = (s16[4,656,128]{2,1,0:T(8,128)(2,1)S(1)}, s16[4,656,128]{2,1,0:T(8,128)(2,1)}, u32[]{:S(2)}) copy-start(s16[4,656,128]{2,1,0:T(8,128)(2,1)} %copy-done.7) | copy-start | bytes 2015236
  43.1 0.8 copy-start.10
  48.0 45.3 %copy-start.4 = (f32[128,2560]{1,0:T(8,128)S(1)}, f32[128,2560]{1,0:T(8,128)}, u32[]{:S(2)}) copy-start(f32[128,2560]{1,0:T(8,128)} %copy-done.3) | copy-start | bytes 3932164
  54.9 38.4 %copy-start.11 = (bf16[256,128]{1,0:T(8,128)(2,1)S(1)}, bf16[256,128]{1,0:T(8,128)(2,1)}, u32[]{:S(2)}) copy-start(bf16[256,128]{1,0:T(8,128)(2,1)} %constant.33.clone.lt) | copy-start | bytes 196612
  89.0 9.2 %collective-permute-start.7 = (bf16[64,5120]{1,0:T(8,128)(2,1)S(1)}, bf16[64,5120]{1,0:T(8,128)(2,1)S(1)}, u32[]{:S(2)}, u32[]{:S(2)}) collective-permute-start(bf16[64,5120]{1,0:T(8,128)(2,1)S(1)} %get-tuple-element.36.refs_0_), channel_id=1, source_target_pairs={{0,1},{1,0},{2,3},{3,2},{4,5},{5,4},{6,7},{7,6},{8,9},{9,8},{10,11... | collective-permute-start | bytes 1966088 | tf_op jit(solution)/shard_map/ppermute | solution.py:505
  92.2 6.1 %collective-permute-start.8 = (bf16[64,5120]{1,0:T(8,128)(2,1)S(1)}, bf16[64,5120]{1,0:T(8,128)(2,1)S(1)}, u32[]{:S(2)}, u32[]{:S(2)}) collective-permute-start(bf16[64,5120]{1,0:T(8,128)(2,1)S(1)} %get-tuple-element.37.refs_1_), channel_id=1, source_target_pairs={{0,1},{1,0},{2,3},{3,2},{4,5},{5,4},{6,7},{7,6},{8,9},{9,8},{10,11... | collective-permute-start | bytes 1966088 | tf_op jit(solution)/shard_map/ppermute | solution.py:505
  92.2 15.8 %collective-permute-start.5 = (bf16[64,5120]{1,0:T(8,128)(2,1)S(1)}, bf16[64,5120]{1,0:T(8,128)(2,1)S(1)}, u32[]{:S(2)}, u32[]{:S(2)}) collective-permute-start(bf16[64,5120]{1,0:T(8,128)(2,1)S(1)} %get-tuple-element.36.refs_0_), channel_id=1, source_target_pairs={{0,2},{2,0},{4,6},{6,4},{1,3},{3,1},{5,7},{7,5},{8,10},{10,8},{12,... | collective-permute-start | bytes 1966088 | tf_op jit(solution)/shard_map/ppermute | solution.py:502
  92.5 16.7 %collective-permute-start.6 = (bf16[64,5120]{1,0:T(8,128)(2,1)S(1)}, bf16[64,5120]{1,0:T(8,128)(2,1)S(1)}, u32[]{:S(2)}, u32[]{:S(2)}) collective-permute-start(bf16[64,5120]{1,0:T(8,128)(2,1)S(1)} %get-tuple-element.37.refs_1_), channel_id=1, source_target_pairs={{0,6},{2,4},{4,2},{6,0},{1,7},{3,5},{5,3},{7,1},{8,14},{10,12},{12... | collective-permute-start | bytes 1966088 | tf_op jit(solution)/shard_map/ppermute | solution.py:503
  109.2 3.4 %collective-permute-start.10 = (bf16[64,5120]{1,0:T(8,128)(2,1)S(1)}, bf16[64,5120]{1,0:T(8,128)(2,1)S(1)}, u32[]{:S(2)}, u32[]{:S(2)}) collective-permute-start(bf16[64,5120]{1,0:T(8,128)(2,1)S(1)} %collective-permute-done.6.refs_1_), channel_id=1, source_target_pairs={{0,1},{1,0},{2,3},{3,2},{4,5},{5,4},{6,7},{7,6},{8,9},{9,8},{10,11... | collective-permute-start | bytes 1966088 | tf_op jit(solution)/shard_map/ppermute | solution.py:509
  110.9 2.7 %collective-permute-start.9 = (bf16[64,5120]{1,0:T(8,128)(2,1)S(1)}, bf16[64,5120]{1,0:T(8,128)(2,1)S(1)}, u32[]{:S(2)}, u32[]{:S(2)}) collective-permute-start(bf16[64,5120]{1,0:T(8,128)(2,1)S(1)} %collective-permute-done.5.refs_0_), channel_id=1, source_target_pairs={{0,1},{1,0},{2,3},{3,2},{4,5},{5,4},{6,7},{7,6},{8,9},{9,8},{10,11... | collective-permute-start | bytes 1966088 | tf_op jit(solution)/shard_map/ppermute | solution.py:509

commit v5 on v4

--- a/solution.py
+++ b/solution.py
@@ -285,7 +285,7 @@
             hot[t, pl.ds(at, 16), :] = jnp.where(lanes_of(x, 80 + half) == here, 1.0, 0.0).astype(BF16)
         return 0
 
-    lax.fori_loop(0, got.shape[0] // 2, one, 0, unroll=8)
+    lax.fori_loop(0, got.shape[0] // 2, one, 0, unroll=4)
     same = (sub((128, 128)) >> 6) == (lane((128, 128)) >> 6)
     grids = []
     for t in range(3):

time: 116 us -> 114 us (0.983)
  Pallas kernels: 32.7 us -> 31 us
    pallas_call x1, Pallas kernels: 4.68 us -> 2.97 us  [owner(): pl.pallas_call(owner_kernel, out_shape=jax.ShapeDtypeStruct((UROWS, 128),...]
  transfers between devices with their start and end apart: 12 -> 12, of which waited for: 5 -> 5; matrix products, arithmetic and copies ran while one was open for 4% -> 4% of each run, Pallas kernels for 25% -> 23%
where the time goes in v5:
time: 114 us
  Pallas kernels  31 us (27%)
  blocking collectives  26.7 us (23%)
  starting transfers between devices  21.9 us (19%)
  waiting for transfers between devices  18.3 us (16%)
  matrix products  8.98 us (8%)
  local copies, waits for them, and re-layouts  5.62 us (5%)
    all_to_all x1, blocking collectives, body(): lax.all_to_all(jnp.broadcast_to(mine16, (32, UROWS, 128)), REP, 0, 0, til...  26.7 us
    all_to_all x1, starting transfers between devices, body(): lax.all_to_all(comp.reshape(64, 16, 128), REP + ('yl',), 0, 0, tiled=True)  11.5 us
    pallas_call x2, Pallas kernels, compress(): pl.pallas_call(functools.partial(compress_kernel, part, with_code), grid_...  9.94 us
    pallas_call x2, Pallas kernels, left(): pl.pallas_call(functools.partial(left_kernel, part), grid=(n,), in_specs=...  9.08 us
    dot_general x4, matrix products, term(): lax.dot_general(hidden, right, (((0,), (0,)), ((), ())), preferred_elemen...  8.98 us
    ppermute x1, waiting for transfers between devices, body(): far_low = lax.ppermute(low, ('yh', 'yl'), NEAR)  7.57 us
    all_to_all x1, waiting for transfers between devices, body(): lax.all_to_all(comp.reshape(64, 16, 128), REP + ('yl',), 0, 0, tiled=True)  6.84 us
    pallas_call x3, Pallas kernels, gather(): pl.pallas_call(functools.partial(gather_kernel, n), grid_spec=pltpu.Prefe...  5.47 us
  transfers between devices with their start and end apart: 12, of which 5 were waited for; matrix products, arithmetic and copies ran while one was open for 4% of the time, Pallas kernels for 23%

profile of v5, /device:TPU:1, one launch (start us, length us, event | category | flops | bytes accessed | tf_op | source)
XLA Modules:
  0.0 113.6 jit_solution(16123111439571216511)
XLA Ops:
  0.6 0.0 copy-start.14
  0.7 1.4 %constant_dynamic-slice_fusion.1 = (bf16[1024,128]{1,0:T(8,128)(2,1)S(1)}, bf16[1024,128]{1,0:T(8,128)(2,1)S(1)}, bf16[1024,128]{1,0:T(8,128)(2,1)S(1)}, bf16[1024,128]{1,0:T(8,128)(2,1)S(1)}) fusion(bf16[1024,512]{1,0:T(8,128)(2,1)} %param.11, s32[]{:T(128)S(6)} %select_n.14, s32[]{:T(128)S(6)} %select_n.13, s32[]{:T(128)S(6)} %select_n.12, s32[]{:T(128)S(6)} %select_n.15), kind=kLoop, calls=%fused_computation.12 | loop fusion | bytes 2097168 | tf_op jit(solution)/shard_map/dynamic_slice | solution.py:125
  2.1 4.3 %fusion = f32[256,2560]{1,0:T(8,128)S(1)} fusion(bf16[1024,5120]{1,0:T(8,128)(2,1)} %param.12, bf16[1024,128]{1,0:T(8,128)(2,1)S(1)} %get-tuple-element.52, bf16[1024,128]{1,0:T(8,128)(2,1)S(1)} %get-tuple-element.49), kind=kOutput, calls=%fused_computation | convolution fusion | flops 1343225856 | bytes 8388608 | tf_op jit(solution)/shard_map/dot_general | solution.py:120
  6.4 0.0 copy-start.13
  6.4 1.5 %collective-permute-start.2 = (f32[256,2560]{1,0:T(8,128)S(1)}, f32[256,2560]{1,0:T(8,128)S(1)}, u32[]{:S(2)}, u32[]{:S(2)}) collective-permute-start(f32[256,2560]{1,0:T(8,128)S(1)} %fusion), channel_id=1, source_target_pairs={{0,1},{1,0},{2,3},{3,2},{4,5},{5,4},{6,7},{7,6},{8,9},{9,8},{10,11... | collective-permute-start | bytes 7864328 | tf_op jit(solution)/shard_map/ppermute | solution.py:483
  7.9 1.6 %fusion.4 = f32[256,2560]{1,0:T(8,128)S(1)} fusion(bf16[1024,5120]{1,0:T(8,128)(2,1)S(1)} %copy-done.14, bf16[1024,128]{1,0:T(8,128)(2,1)S(1)} %get-tuple-element.52, bf16[1024,128]{1,0:T(8,128)(2,1)S(1)} %get-tuple-element.49), kind=kOutput, calls=%fused_computation.4 | convolution fusion | flops 1343225856 | bytes 8388608 | tf_op jit(solution)/shard_map/dot_general | solution.py:120
  9.5 0.1 collective-permute-start
  9.6 1.5 %collective-permute-start.1 = (s32[2,32,128]{2,1,0:T(8,128)S(1)}, s32[2,32,128]{2,1,0:T(8,128)S(1)}, u32[]{:S(2)}, u32[]{:S(2)}) collective-permute-start(s32[2,32,128]{2,1,0:T(8,128)S(1)} %get-tuple-element.54), channel_id=1, source_target_pairs={{0,2},{2,0},{4,6},{6,4},{1,3},{3,1},{5,7},{7,5},{8,10},{10,8},{12,... | collective-permute-start | bytes 98312 | tf_op jit(solution)/shard_map/ppermute | solution.py:477
  11.1 1.6 %fusion.2.own = f32[256,2560]{1,0:T(8,128)S(1)} fusion(bf16[1024,5120]{1,0:T(8,128)(2,1)S(1)} %copy-done.14, bf16[1024,128]{1,0:T(8,128)(2,1)S(1)} %get-tuple-element.50, bf16[1024,128]{1,0:T(8,128)(2,1)S(1)} %get-tuple-element.51), kind=kOutput, calls=%fused_computation.2 | convolution fusion | flops 1343225856 | bytes 8388608 | tf_op jit(solution)/shard_map/dot_general | solution.py:120
  12.7 0.9 code.1
  13.6 0.0 copy-start
  13.6 0.0 copy-start.1
  13.6 0.0 copy-start.6
  13.6 0.0 copy-start.12
  13.6 1.3 %collective-permute-start.3 = (s16[4,656,128]{2,1,0:T(8,128)(2,1)S(1)}, s16[4,656,128]{2,1,0:T(8,128)(2,1)S(1)}, u32[]{:S(2)}, u32[]{:S(2)}) collective-permute-start(s16[4,656,128]{2,1,0:T(8,128)(2,1)S(1)} %code.1), channel_id=1, source_target_pairs={{0,2},{2,0},{4,6},{6,4},{1,3},{3,1},{5,7},{7,5},{8,10},{10,8},{12,... | collective-permute-start | bytes 2015240 | tf_op jit(solution)/shard_map/ppermute | solution.py:486
  14.9 1.6 %fusion.6.own = f32[256,2560]{1,0:T(8,128)S(1)} fusion(bf16[1024,5120]{1,0:T(8,128)(2,1)S(1)} %copy-done.14, bf16[1024,128]{1,0:T(8,128)(2,1)S(1)} %get-tuple-element.50, bf16[1024,128]{1,0:T(8,128)(2,1)S(1)} %get-tuple-element.51), kind=kOutput, calls=%fused_computation.6 | convolution fusion | flops 1343225856 | bytes 8388608 | tf_op jit(solution)/shard_map/dot_general | solution.py:120
  16.4 0.1 pad_add_fusion.1.me
  16.6 4.7 %compress.2 = (f32[128,2560]{1,0:T(8,128)S(1)}, f32[2,16,2,16,128]{4,3,2,1,0:T(8,128)}) custom-call(s32[2]{0:T(128)S(1)} %pad_add_fusion.1.me, f32[256,2560]{1,0:T(8,128)S(1)} %fusion.2.own, f32[256,2560]{1,0:T(8,128)S(1)} %collective-permute-done.2.got, f32[1,128,5120]{2,1,0:T(8,128)S(1)} %copy-done, s32[2,2,32,128]{3,2,1,0:T(8,128)S(1)} %pad_add_fusion.picks, ...), custom_call_target="tpu_custom_call" | custom-call | flops 1000 | bytes 1000 | tf_op jit(solution)/shard_map/compress/pallas_call | solution.py:245
  21.2 5.3 %compress.3 = (s16[4,656,128]{2,1,0:T(8,128)(2,1)}, f32[128,2560]{1,0:T(8,128)S(1)}, f32[2,16,2,16,128]{4,3,2,1,0:T(8,128)}) custom-call(s32[2]{0:T(128)S(1)} %pad_add_fusion.1.me, f32[256,2560]{1,0:T(8,128)S(1)} %fusion.6.own, f32[256,2560]{1,0:T(8,128)S(1)} %collective-permute-done.got, ...), custom_call_target="tpu_custom_call", output_to_operand_aliasing={{2}: (8, {})} | custom-call | flops 1000 | bytes 1000 | tf_op jit(solution)/shard_map/compress/pallas_call | solution.py:245
  26.5 1.1 copy-done.3
  27.6 0.3 collective-permute-start.4
  27.8 1.7 %collective-permute-done.3.q = s16[4,656,128]{2,1,0:T(8,128)(2,1)S(1)} collective-permute-done((s16[4,656,128]{2,1,0:T(8,128)(2,1)S(1)}, s16[4,656,128]{2,1,0:T(8,128)(2,1)S(1)}, u32[]{:S(2)}, u32[]{:S(2)}) %collective-permute-start.3) | collective-permute-done | bytes 671776 | tf_op jit(solution)/shard_map/ppermute | solution.py:486
  29.5 0.8 copy-done.7
  30.4 11.5 %all-to-all-start = ((f32[64,16,128]{2,1,0:T(8,128)}), f32[64,16,128]{2,1,0:T(8,128)S(1)}, u32[]{:S(2)}, u32[]{:S(2)}) async-start(f32[64,16,128]{2,1,0:T(8,128)} %bitcast.6), calls=%async_computation | async-start | bytes 1048576 | tf_op jit(solution)/shard_map/all_to_all | solution.py:491
  41.9 0.0 copy-start.2
  41.9 0.0 copy-start.8
  41.9 1.2 %copy-done.8 = s16[4,656,128]{2,1,0:T(8,128)(2,1)S(1)} copy-done((s16[4,656,128]{2,1,0:T(8,128)(2,1)S(1)}, s16[4,656,128]{2,1,0:T(8,128)(2,1)}, u32[]{:S(2)}) %copy-start.8) | copy-done | bytes 671768
  43.1 0.8 copy-done.10
  43.9 4.1 %left.2.refs_0_ = f32[1,128,5120]{2,1,0:T(8,128)} custom-call(s16[4,656,128]{2,1,0:T(8,128)(2,1)S(1)} %copy-done.8, f32[128,2560]{1,0:T(8,128)S(1)} %get-tuple-element.30.pm, s32[2,2,32,128]{3,2,1,0:T(8,128)S(1)} %pad_add_fusion.picks, bf16[256,256]{1,0:T(8,128)(2,1)S(1)} %copy-done.1, bf16[256,128]{1,0:T(8,128)(2,1)S(1)} %copy-done.10, ...), custom_call_target="tpu_custom_call" | custom-call | flops 1000 | bytes 1000 | tf_op jit(solution)/shard_map/left/pallas_call | solution.py:446
  48.0 6.8 %all-to-all-done.got = f32[64,16,128]{2,1,0:T(8,128)S(1)} async-done(((f32[64,16,128]{2,1,0:T(8,128)}), f32[64,16,128]{2,1,0:T(8,128)S(1)}, u32[]{:S(2)}, u32[]{:S(2)}) %all-to-all-start) | async-done | bytes 524320 | tf_op jit(solution)/shard_map/all_to_all | solution.py:491
  54.9 3.0 %owner.1 = s16[176,128]{1,0:T(8,128)(2,1)S(1)} custom-call(f32[64,16,128]{2,1,0:T(8,128)S(1)} %all-to-all-done.got, bf16[256,256]{1,0:T(8,128)(2,1)S(1)} %copy-done.5, bf16[256,128]{1,0:T(8,128)(2,1)S(1)} %copy-done.9), custom_call_target="tpu_custom_call" | custom-call | tf_op jit(solution)/shard_map/owner/pallas_call | solution.py:308
  57.8 0.2 broadcast_in_dim.3
  58.0 26.7 %all_to_all.10.got0.got1 = s16[32,176,128]{2,1,0:T(8,128)(2,1)S(1)} all-to-all(s16[32,176,128]{2,1,0:T(8,128)(2,1)S(1)} %broadcast_in_dim.3), channel_id=1, replica_groups=mesh['x'=4,'z'=4,'yh'=2,'yl'=2,'c'=2] {'x','z','yh'}, dimensions={0} | all-to-all | bytes 2883584 | tf_op jit(solution)/shard_map/all_to_all | solution.py:496
  84.7 2.6 %finish.1 = (f32[128,5120]{1,0:T(8,128)}, bf16[64,5120]{1,0:T(8,128)(2,1)S(1)}, bf16[64,5120]{1,0:T(8,128)(2,1)S(1)}) custom-call(s16[32,176,128]{2,1,0:T(8,128)(2,1)S(1)} %all_to_all.10.got0.got1, s16[32,176,128]{2,1,0:T(8,128)(2,1)S(1)} %all_to_all.10.got0.got1, bf16[128,5120]{1,0:T(8,128)(2,1)S(1)} %copy-done.2), custom_call_target="tpu_custom_call" | custom-call | flops 1000 | bytes 1000 | tf_op jit(solution)/shard_map/finish/pallas_call | solution.py:345
  87.3 3.2 %collective-permute-start.7 = (bf16[64,5120]{1,0:T(8,128)(2,1)S(1)}, bf16[64,5120]{1,0:T(8,128)(2,1)S(1)}, u32[]{:S(2)}, u32[]{:S(2)}) collective-permute-start(bf16[64,5120]{1,0:T(8,128)(2,1)S(1)} %get-tuple-element.36.refs_0_), channel_id=1, source_target_pairs={{0,1},{1,0},{2,3},{3,2},{4,5},{5,4},{6,7},{7,6},{8,9},{9,8},{10,11... | collective-permute-start | bytes 1966088 | tf_op jit(solution)/shard_map/ppermute | solution.py:505
  90.5 0.3 collective-permute-start.5
  90.8 0.7 collective-permute-start.6
  91.5 0.1 pad_add_fusion.2.rows
  91.6 5.0 %left.3 = f32[1,128,5120]{2,1,0:T(8,128)} custom-call(s16[4,656,128]{2,1,0:T(8,128)(2,1)} %collective-permute-done.4.q, f32[128,2560]{1,0:T(8,128)S(1)} %copy-done.4, s32[2,2,32,128]{3,2,1,0:T(8,128)S(1)} %pad_add_fusion.picks, bf16[256,256]{1,0:T(8,128)(2,1)S(1)} %copy-done.1, bf16[256,128]{1,0:T(8,128)(2,1)S(1)} %copy-done.11, ...), custom_call_target="tpu_custom_call", output_to_operand_aliasing={{}: (7, {})} | custom-call | flops 1000 | bytes 1000 | tf_op jit(solution)/shard_map/left/pallas_call | solution.py:446
  96.6 2.2 %gather.3.refs_2_ = bf16[512,5120]{1,0:T(8,128)(2,1)} custom-call(s32[4]{0:T(128)S(1)} %pad_add_fusion.2.rows, bf16[64,5120]{1,0:T(8,128)(2,1)S(1)} %get-tuple-element.36.refs_0_, bf16[64,5120]{1,0:T(8,128)(2,1)S(1)} %get-tuple-element.37.refs_1_, bf16[64,5120]{1,0:T(8,128)(2,1)S(1)} %collective-permute-done.7.refs_2_, ...), custom_call_target="tpu_custom_call" | custom-call | bytes 4194304 | tf_op jit(solution)/shard_map/gather/pallas_call | solution.py:376
  98.7 7.6 %collective-permute-done.5.refs_0_ = bf16[64,5120]{1,0:T(8,128)(2,1)S(1)} collective-permute-done((bf16[64,5120]{1,0:T(8,128)(2,1)S(1)}, bf16[64,5120]{1,0:T(8,128)(2,1)S(1)}, u32[]{:S(2)}, u32[]{:S(2)}) %collective-permute-start.5) | collective-permute-done | bytes 655392 | tf_op jit(solution)/shard_map/ppermute | solution.py:502
  106.3 1.2 %collective-permute-done.6.refs_1_ = bf16[64,5120]{1,0:T(8,128)(2,1)S(1)} collective-permute-done((bf16[64,5120]{1,0:T(8,128)(2,1)S(1)}, bf16[64,5120]{1,0:T(8,128)(2,1)S(1)}, u32[]{:S(2)}, u32[]{:S(2)}) %collective-permute-start.6) | collective-permute-done | bytes 655392 | tf_op jit(solution)/shard_map/ppermute | solution.py:503
  107.5 1.7 %collective-permute-start.10 = (bf16[64,5120]{1,0:T(8,128)(2,1)S(1)}, bf16[64,5120]{1,0:T(8,128)(2,1)S(1)}, u32[]{:S(2)}, u32[]{:S(2)}) collective-permute-start(bf16[64,5120]{1,0:T(8,128)(2,1)S(1)} %collective-permute-done.6.refs_1_), channel_id=1, source_target_pairs={{0,1},{1,0},{2,3},{3,2},{4,5},{5,4},{6,7},{7,6},{8,9},{9,8},{10,11... | collective-permute-start | bytes 1966088 | tf_op jit(solution)/shard_map/ppermute | solution.py:509
  109.1 0.0 collective-permute-start.9
  109.2 1.7 %gather.4.refs_2_ = bf16[512,5120]{1,0:T(8,128)(2,1)} custom-call(s32[2]{0:T(128)S(1)} %fusion.8.rows, bf16[64,5120]{1,0:T(8,128)(2,1)S(1)} %collective-permute-done.5.refs_0_, bf16[64,5120]{1,0:T(8,128)(2,1)S(1)} %collective-permute-done.6.refs_1_, bf16[512,5120]{1,0:T(8,128)(2,1)} %gather.3.refs_2_), custom_call_target="tpu_custom_call", output_to_operand_aliasing={{}: (3, {})} | custom-call | bytes 4194304 | tf_op jit(solution)/shard_map/gather/pallas_call | solution.py:376
  110.8 0.0 collective-permute-done.10.refs_1_
  110.9 0.9 collective-permute-done.9.refs_0_
  111.8 1.7 %gather.5 = bf16[512,5120]{1,0:T(8,128)(2,1)} custom-call(s32[2]{0:T(128)S(1)} %fusion.9.rows, bf16[64,5120]{1,0:T(8,128)(2,1)S(1)} %collective-permute-done.9.refs_0_, bf16[64,5120]{1,0:T(8,128)(2,1)S(1)} %collective-permute-done.10.refs_1_, bf16[512,5120]{1,0:T(8,128)(2,1)} %gather.4.refs_2_), custom_call_target="tpu_custom_call", output_to_operand_aliasing={{}: (3, {})} | custom-call | bytes 4194304 | tf_op jit(solution)/shard_map/gather/pallas_call | solution.py:376
  (30 shorter events, 0.1 us)
Async XLA Ops:
  0.6 7.3 %copy-start.14 = (bf16[1024,5120]{1,0:T(8,128)(2,1)S(1)}, bf16[1024,5120]{1,0:T(8,128)(2,1)}, u32[]{:S(2)}) copy-start(bf16[1024,5120]{1,0:T(8,128)(2,1)} %param.12) | copy-start | bytes 31457284
  6.4 3.2 %copy-start.13 = (s32[1,2,80,32]{2,3,1,0:T(8,128)S(1)}, s32[1,2,80,32]{2,3,1,0:T(8,128)}, u32[]{:S(2)}) copy-start(s32[1,2,80,32]{2,3,1,0:T(8,128)} %param.14) | copy-start | bytes 61444
  6.4 6.2 %collective-permute-start.2 = (f32[256,2560]{1,0:T(8,128)S(1)}, f32[256,2560]{1,0:T(8,128)S(1)}, u32[]{:S(2)}, u32[]{:S(2)}) collective-permute-start(f32[256,2560]{1,0:T(8,128)S(1)} %fusion), channel_id=1, source_target_pairs={{0,1},{1,0},{2,3},{3,2},{4,5},{5,4},{6,7},{7,6},{8,9},{9,8},{10,11... | collective-permute-start | bytes 7864328 | tf_op jit(solution)/shard_map/ppermute | solution.py:483
  9.5 11.7 %collective-permute-start = (f32[256,2560]{1,0:T(8,128)S(1)}, f32[256,2560]{1,0:T(8,128)S(1)}, u32[]{:S(2)}, u32[]{:S(2)}) collective-permute-start(f32[256,2560]{1,0:T(8,128)S(1)} %fusion.4), channel_id=1, source_target_pairs={{0,1},{1,0},{2,3},{3,2},{4,5},{5,4},{6,7},{7,6},{8,9},{9,8},{10,11... | collective-permute-start | bytes 7864328 | tf_op jit(solution)/shard_map/ppermute | solution.py:483
  9.6 6.9 %collective-permute-start.1 = (s32[2,32,128]{2,1,0:T(8,128)S(1)}, s32[2,32,128]{2,1,0:T(8,128)S(1)}, u32[]{:S(2)}, u32[]{:S(2)}) collective-permute-start(s32[2,32,128]{2,1,0:T(8,128)S(1)} %get-tuple-element.54), channel_id=1, source_target_pairs={{0,2},{2,0},{4,6},{6,4},{1,3},{3,1},{5,7},{7,5},{8,10},{10,8},{12,... | collective-permute-start | bytes 98312 | tf_op jit(solution)/shard_map/ppermute | solution.py:477
  13.6 3.0 %copy-start = (f32[1,128,5120]{2,1,0:T(8,128)S(1)}, f32[1,128,5120]{2,1,0:T(8,128)}, u32[]{:S(2)}) copy-start(f32[1,128,5120]{2,1,0:T(8,128)} %mom.3) | copy-start | bytes 7864324
  13.6 3.0 %copy-start.1 = (bf16[256,256]{1,0:T(8,128)(2,1)S(1)}, bf16[256,256]{1,0:T(8,128)(2,1)}, u32[]{:S(2)}) copy-start(bf16[256,256]{1,0:T(8,128)(2,1)} %constant.30.clone.rt) | copy-start | bytes 393220
  13.6 2.9 %copy-start.6 = (bf16[512,256]{1,0:T(8,128)(2,1)S(1)}, bf16[512,256]{1,0:T(8,128)(2,1)}, u32[]{:S(2)}) copy-start(bf16[512,256]{1,0:T(8,128)(2,1)} %constant.32.clone.lt) | copy-start | bytes 786436
  13.6 2.9 %copy-start.12 = (s32[2,8,128]{2,1,0:T(8,128)S(1)}, s32[2,8,128]{2,1,0:T(8,128)}, u32[]{:S(2)}) copy-start(s32[2,8,128]{2,1,0:T(8,128)} %constant.35.clone.tab) | copy-start | bytes 24580
  13.6 15.9 %collective-permute-start.3 = (s16[4,656,128]{2,1,0:T(8,128)(2,1)S(1)}, s16[4,656,128]{2,1,0:T(8,128)(2,1)S(1)}, u32[]{:S(2)}, u32[]{:S(2)}) collective-permute-start(s16[4,656,128]{2,1,0:T(8,128)(2,1)S(1)} %code.1), channel_id=1, source_target_pairs={{0,2},{2,0},{4,6},{6,4},{1,3},{3,1},{5,7},{7,5},{8,10},{10,8},{12,... | collective-permute-start | bytes 2015240 | tf_op jit(solution)/shard_map/ppermute | solution.py:486
  21.2 20.7 %copy-start.5 = (bf16[256,256]{1,0:T(8,128)(2,1)S(1)}, bf16[256,256]{1,0:T(8,128)(2,1)}, u32[]{:S(2)}) copy-start(bf16[256,256]{1,0:T(8,128)(2,1)} %constant.31.clone.irt.rt) | copy-start | bytes 393220
  21.2 20.7 %copy-start.9 = (bf16[256,128]{1,0:T(8,128)(2,1)S(1)}, bf16[256,128]{1,0:T(8,128)(2,1)}, u32[]{:S(2)}) copy-start(bf16[256,128]{1,0:T(8,128)(2,1)} %constant.34.clone.ilt.lt) | copy-start | bytes 196612
  26.5 1.1 copy-start.3
  27.6 30.3 %collective-permute-start.4 = (s16[4,656,128]{2,1,0:T(8,128)(2,1)}, s16[4,656,128]{2,1,0:T(8,128)(2,1)}, u32[]{:S(2)}, u32[]{:S(2)}) collective-permute-start(s16[4,656,128]{2,1,0:T(8,128)(2,1)} %get-tuple-element.32), channel_id=1, source_target_pairs={{0,2},{2,0},{4,6},{6,4},{1,3},{3,1},{5,7},{7,5},{8,10},{10,8},{12,... | collective-permute-start | bytes 2015240 | tf_op jit(solution)/shard_map/ppermute | solution.py:489
  29.5 0.8 copy-start.7
  30.4 24.5 %all-to-all-start = ((f32[64,16,128]{2,1,0:T(8,128)}), f32[64,16,128]{2,1,0:T(8,128)S(1)}, u32[]{:S(2)}, u32[]{:S(2)}) async-start(f32[64,16,128]{2,1,0:T(8,128)} %bitcast.6), calls=%async_computation | async-start | bytes 1048576 | tf_op jit(solution)/shard_map/all_to_all | solution.py:491
  41.9 42.9 %copy-start.2 = (bf16[128,5120]{1,0:T(8,128)(2,1)S(1)}, bf16[128,5120]{1,0:T(8,128)(2,1)}, u32[]{:S(2)}) copy-start(bf16[128,5120]{1,0:T(8,128)(2,1)} %par.1) | copy-start | bytes 3932164
  41.9 1.2 %copy-start.8 = (s16[4,656,128]{2,1,0:T(8,128)(2,1)S(1)}, s16[4,656,128]{2,1,0:T(8,128)(2,1)}, u32[]{:S(2)}) copy-start(s16[4,656,128]{2,1,0:T(8,128)(2,1)} %copy-done.7) | copy-start | bytes 2015236
  43.1 0.8 copy-start.10
  48.0 43.5 %copy-start.4 = (f32[128,2560]{1,0:T(8,128)S(1)}, f32[128,2560]{1,0:T(8,128)}, u32[]{:S(2)}) copy-start(f32[128,2560]{1,0:T(8,128)} %copy-done.3) | copy-start | bytes 3932164
  54.9 36.7 %copy-start.11 = (bf16[256,128]{1,0:T(8,128)(2,1)S(1)}, bf16[256,128]{1,0:T(8,128)(2,1)}, u32[]{:S(2)}) copy-start(bf16[256,128]{1,0:T(8,128)(2,1)} %constant.33.clone.lt) | copy-start | bytes 196612
  87.3 9.2 %collective-permute-start.7 = (bf16[64,5120]{1,0:T(8,128)(2,1)S(1)}, bf16[64,5120]{1,0:T(8,128)(2,1)S(1)}, u32[]{:S(2)}, u32[]{:S(2)}) collective-permute-start(bf16[64,5120]{1,0:T(8,128)(2,1)S(1)} %get-tuple-element.36.refs_0_), channel_id=1, source_target_pairs={{0,1},{1,0},{2,3},{3,2},{4,5},{5,4},{6,7},{7,6},{8,9},{9,8},{10,11... | collective-permute-start | bytes 1966088 | tf_op jit(solution)/shard_map/ppermute | solution.py:505
  90.5 6.1 %collective-permute-start.8 = (bf16[64,5120]{1,0:T(8,128)(2,1)S(1)}, bf16[64,5120]{1,0:T(8,128)(2,1)S(1)}, u32[]{:S(2)}, u32[]{:S(2)}) collective-permute-start(bf16[64,5120]{1,0:T(8,128)(2,1)S(1)} %get-tuple-element.37.refs_1_), channel_id=1, source_target_pairs={{0,1},{1,0},{2,3},{3,2},{4,5},{5,4},{6,7},{7,6},{8,9},{9,8},{10,11... | collective-permute-start | bytes 1966088 | tf_op jit(solution)/shard_map/ppermute | solution.py:505
  90.5 15.8 %collective-permute-start.5 = (bf16[64,5120]{1,0:T(8,128)(2,1)S(1)}, bf16[64,5120]{1,0:T(8,128)(2,1)S(1)}, u32[]{:S(2)}, u32[]{:S(2)}) collective-permute-start(bf16[64,5120]{1,0:T(8,128)(2,1)S(1)} %get-tuple-element.36.refs_0_), channel_id=1, source_target_pairs={{0,2},{2,0},{4,6},{6,4},{1,3},{3,1},{5,7},{7,5},{8,10},{10,8},{12,... | collective-permute-start | bytes 1966088 | tf_op jit(solution)/shard_map/ppermute | solution.py:502
  90.8 16.7 %collective-permute-start.6 = (bf16[64,5120]{1,0:T(8,128)(2,1)S(1)}, bf16[64,5120]{1,0:T(8,128)(2,1)S(1)}, u32[]{:S(2)}, u32[]{:S(2)}) collective-permute-start(bf16[64,5120]{1,0:T(8,128)(2,1)S(1)} %get-tuple-element.37.refs_1_), channel_id=1, source_target_pairs={{0,6},{2,4},{4,2},{6,0},{1,7},{3,5},{5,3},{7,1},{8,14},{10,12},{12... | collective-permute-start | bytes 1966088 | tf_op jit(solution)/shard_map/ppermute | solution.py:503
  107.5 3.4 %collective-permute-start.10 = (bf16[64,5120]{1,0:T(8,128)(2,1)S(1)}, bf16[64,5120]{1,0:T(8,128)(2,1)S(1)}, u32[]{:S(2)}, u32[]{:S(2)}) collective-permute-start(bf16[64,5120]{1,0:T(8,128)(2,1)S(1)} %collective-permute-done.6.refs_1_), channel_id=1, source_target_pairs={{0,1},{1,0},{2,3},{3,2},{4,5},{5,4},{6,7},{7,6},{8,9},{9,8},{10,11... | collective-permute-start | bytes 1966088 | tf_op jit(solution)/shard_map/ppermute | solution.py:509
  109.1 2.7 %collective-permute-start.9 = (bf16[64,5120]{1,0:T(8,128)(2,1)S(1)}, bf16[64,5120]{1,0:T(8,128)(2,1)S(1)}, u32[]{:S(2)}, u32[]{:S(2)}) collective-permute-start(bf16[64,5120]{1,0:T(8,128)(2,1)S(1)} %collective-permute-done.5.refs_0_), channel_id=1, source_target_pairs={{0,1},{1,0},{2,3},{3,2},{4,5},{5,4},{6,7},{7,6},{8,9},{9,8},{10,11... | collective-permute-start | bytes 1966088 | tf_op jit(solution)/shard_map/ppermute | solution.py:509

commit v6 on v5

--- a/solution.py
+++ b/solution.py
@@ -17,6 +17,7 @@
 PAIRS = 8
 PER = PAIRS // PARTS
 GW = 640
+FINISH = 4
 LEFT = 2
 QROWS = 656
 UROWS = 176
@@ -330,7 +331,7 @@
 def finish_kernel(got0, got1, par, update, low, high):
     for a, (got, new) in enumerate(((got0, low), (got1, high))):
         rows = slice(64 * a, 64 * a + 64)
-        for pair in range(LEFT):
+        for pair in range(FINISH):
             for t, u in enumerate(decode(got, pair)):
                 cols = slice(GW * pair + 128 * t, GW * pair + 128 * t + 128)
                 update[rows, cols] = u
@@ -338,9 +339,9 @@
 
 
 def finish(got, par):
-    n = PAIRS // LEFT
-    col = lambda r: pl.BlockSpec((r, LEFT * GW), lambda i: (0, i))
-    blocks = lambda a: pl.BlockSpec((2 * LEFT, UROWS, 128), lambda i: (n * a + i, 0, 0))
+    n = PAIRS // FINISH
+    col = lambda r: pl.BlockSpec((r, FINISH * GW), lambda i: (0, i))
+    blocks = lambda a: pl.BlockSpec((2 * FINISH, UROWS, 128), lambda i: (n * a + i, 0, 0))
     half = jax.ShapeDtypeStruct((64, 5120), BF16)
     return pl.pallas_call(
         finish_kernel,

time: 114 us -> 113 us (level)
  transfers between devices with their start and end apart: 12 -> 12, of which waited for: 5 -> 5; matrix products, arithmetic and copies ran while one was open for 4% -> 4% of each run, Pallas kernels for 23% -> 24%
where the time goes in v6:
time: 113 us
  Pallas kernels  30.5 us (27%)
  blocking collectives  26.7 us (24%)
  starting transfers between devices  21.9 us (19%)
  waiting for transfers between devices  18.3 us (16%)
  matrix products  8.98 us (8%)
  local copies, waits for them, and re-layouts  5.62 us (5%)
    all_to_all x1, blocking collectives, body(): lax.all_to_all(jnp.broadcast_to(mine16, (32, UROWS, 128)), REP, 0, 0, til...  26.7 us
    all_to_all x1, starting transfers between devices, body(): lax.all_to_all(comp.reshape(64, 16, 128), REP + ('yl',), 0, 0, tiled=True)  11.5 us
    pallas_call x2, Pallas kernels, compress(): pl.pallas_call(functools.partial(compress_kernel, part, with_code), grid_...  9.94 us
    pallas_call x2, Pallas kernels, left(): pl.pallas_call(functools.partial(left_kernel, part), grid=(n,), in_specs=...  9.08 us
    dot_general x4, matrix products, term(): lax.dot_general(hidden, right, (((0,), (0,)), ((), ())), preferred_elemen...  8.98 us
    ppermute x1, waiting for transfers between devices, body(): far_low = lax.ppermute(low, ('yh', 'yl'), NEAR)  7.57 us
    all_to_all x1, waiting for transfers between devices, body(): lax.all_to_all(comp.reshape(64, 16, 128), REP + ('yl',), 0, 0, tiled=True)  6.84 us
    pallas_call x3, Pallas kernels, gather(): pl.pallas_call(functools.partial(gather_kernel, n), grid_spec=pltpu.Prefe...  5.47 us
  transfers between devices with their start and end apart: 12, of which 5 were waited for; matrix products, arithmetic and copies ran while one was open for 4% of the time, Pallas kernels for 24%

profile of v6, /device:TPU:1, one launch (start us, length us, event | category | flops | bytes accessed | tf_op | source)
XLA Modules:
  0.0 113.2 jit_solution(8447324350485793625)
XLA Ops:
  0.6 0.0 copy-start.14
  0.7 1.4 %constant_dynamic-slice_fusion.1 = (bf16[1024,128]{1,0:T(8,128)(2,1)S(1)}, bf16[1024,128]{1,0:T(8,128)(2,1)S(1)}, bf16[1024,128]{1,0:T(8,128)(2,1)S(1)}, bf16[1024,128]{1,0:T(8,128)(2,1)S(1)}) fusion(bf16[1024,512]{1,0:T(8,128)(2,1)} %param.11, s32[]{:T(128)S(6)} %select_n.14, s32[]{:T(128)S(6)} %select_n.13, s32[]{:T(128)S(6)} %select_n.12, s32[]{:T(128)S(6)} %select_n.15), kind=kLoop, calls=%fused_computation.12 | loop fusion | bytes 2097168 | tf_op jit(solution)/shard_map/dynamic_slice | solution.py:126
  2.1 4.3 %fusion = f32[256,2560]{1,0:T(8,128)S(1)} fusion(bf16[1024,5120]{1,0:T(8,128)(2,1)} %param.12, bf16[1024,128]{1,0:T(8,128)(2,1)S(1)} %get-tuple-element.52, bf16[1024,128]{1,0:T(8,128)(2,1)S(1)} %get-tuple-element.49), kind=kOutput, calls=%fused_computation | convolution fusion | flops 1343225856 | bytes 8388608 | tf_op jit(solution)/shard_map/dot_general | solution.py:121
  6.4 0.0 copy-start.13
  6.4 1.5 %collective-permute-start.2 = (f32[256,2560]{1,0:T(8,128)S(1)}, f32[256,2560]{1,0:T(8,128)S(1)}, u32[]{:S(2)}, u32[]{:S(2)}) collective-permute-start(f32[256,2560]{1,0:T(8,128)S(1)} %fusion), channel_id=1, source_target_pairs={{0,1},{1,0},{2,3},{3,2},{4,5},{5,4},{6,7},{7,6},{8,9},{9,8},{10,11... | collective-permute-start | bytes 7864328 | tf_op jit(solution)/shard_map/ppermute | solution.py:484
  7.9 1.6 %fusion.4 = f32[256,2560]{1,0:T(8,128)S(1)} fusion(bf16[1024,5120]{1,0:T(8,128)(2,1)S(1)} %copy-done.14, bf16[1024,128]{1,0:T(8,128)(2,1)S(1)} %get-tuple-element.52, bf16[1024,128]{1,0:T(8,128)(2,1)S(1)} %get-tuple-element.49), kind=kOutput, calls=%fused_computation.4 | convolution fusion | flops 1343225856 | bytes 8388608 | tf_op jit(solution)/shard_map/dot_general | solution.py:121
  9.5 0.1 collective-permute-start
  9.6 1.5 %collective-permute-start.1 = (s32[2,32,128]{2,1,0:T(8,128)S(1)}, s32[2,32,128]{2,1,0:T(8,128)S(1)}, u32[]{:S(2)}, u32[]{:S(2)}) collective-permute-start(s32[2,32,128]{2,1,0:T(8,128)S(1)} %get-tuple-element.54), channel_id=1, source_target_pairs={{0,2},{2,0},{4,6},{6,4},{1,3},{3,1},{5,7},{7,5},{8,10},{10,8},{12,... | collective-permute-start | bytes 98312 | tf_op jit(solution)/shard_map/ppermute | solution.py:478
  11.1 1.6 %fusion.2.own = f32[256,2560]{1,0:T(8,128)S(1)} fusion(bf16[1024,5120]{1,0:T(8,128)(2,1)S(1)} %copy-done.14, bf16[1024,128]{1,0:T(8,128)(2,1)S(1)} %get-tuple-element.50, bf16[1024,128]{1,0:T(8,128)(2,1)S(1)} %get-tuple-element.51), kind=kOutput, calls=%fused_computation.2 | convolution fusion | flops 1343225856 | bytes 8388608 | tf_op jit(solution)/shard_map/dot_general | solution.py:121
  12.7 0.9 code.1
  13.6 0.0 copy-start
  13.6 0.0 copy-start.1
  13.6 0.0 copy-start.6
  13.6 0.0 copy-start.12
  13.6 1.3 %collective-permute-start.3 = (s16[4,656,128]{2,1,0:T(8,128)(2,1)S(1)}, s16[4,656,128]{2,1,0:T(8,128)(2,1)S(1)}, u32[]{:S(2)}, u32[]{:S(2)}) collective-permute-start(s16[4,656,128]{2,1,0:T(8,128)(2,1)S(1)} %code.1), channel_id=1, source_target_pairs={{0,2},{2,0},{4,6},{6,4},{1,3},{3,1},{5,7},{7,5},{8,10},{10,8},{12,... | collective-permute-start | bytes 2015240 | tf_op jit(solution)/shard_map/ppermute | solution.py:487
  14.9 1.6 %fusion.6.own = f32[256,2560]{1,0:T(8,128)S(1)} fusion(bf16[1024,5120]{1,0:T(8,128)(2,1)S(1)} %copy-done.14, bf16[1024,128]{1,0:T(8,128)(2,1)S(1)} %get-tuple-element.50, bf16[1024,128]{1,0:T(8,128)(2,1)S(1)} %get-tuple-element.51), kind=kOutput, calls=%fused_computation.6 | convolution fusion | flops 1343225856 | bytes 8388608 | tf_op jit(solution)/shard_map/dot_general | solution.py:121
  16.4 0.1 pad_add_fusion.1.me
  16.6 4.7 %compress.2 = (f32[128,2560]{1,0:T(8,128)S(1)}, f32[2,16,2,16,128]{4,3,2,1,0:T(8,128)}) custom-call(s32[2]{0:T(128)S(1)} %pad_add_fusion.1.me, f32[256,2560]{1,0:T(8,128)S(1)} %fusion.2.own, f32[256,2560]{1,0:T(8,128)S(1)} %collective-permute-done.2.got, f32[1,128,5120]{2,1,0:T(8,128)S(1)} %copy-done, s32[2,2,32,128]{3,2,1,0:T(8,128)S(1)} %pad_add_fusion.picks, ...), custom_call_target="tpu_custom_call" | custom-call | flops 1000 | bytes 1000 | tf_op jit(solution)/shard_map/compress/pallas_call | solution.py:246
  21.2 5.3 %compress.3 = (s16[4,656,128]{2,1,0:T(8,128)(2,1)}, f32[128,2560]{1,0:T(8,128)S(1)}, f32[2,16,2,16,128]{4,3,2,1,0:T(8,128)}) custom-call(s32[2]{0:T(128)S(1)} %pad_add_fusion.1.me, f32[256,2560]{1,0:T(8,128)S(1)} %fusion.6.own, f32[256,2560]{1,0:T(8,128)S(1)} %collective-permute-done.got, ...), custom_call_target="tpu_custom_call", output_to_operand_aliasing={{2}: (8, {})} | custom-call | flops 1000 | bytes 1000 | tf_op jit(solution)/shard_map/compress/pallas_call | solution.py:246
  26.5 1.1 copy-done.3
  27.6 0.3 collective-permute-start.4
  27.8 1.7 %collective-permute-done.3.q = s16[4,656,128]{2,1,0:T(8,128)(2,1)S(1)} collective-permute-done((s16[4,656,128]{2,1,0:T(8,128)(2,1)S(1)}, s16[4,656,128]{2,1,0:T(8,128)(2,1)S(1)}, u32[]{:S(2)}, u32[]{:S(2)}) %collective-permute-start.3) | collective-permute-done | bytes 671776 | tf_op jit(solution)/shard_map/ppermute | solution.py:487
  29.5 0.8 copy-done.7
  30.4 11.5 %all-to-all-start = ((f32[64,16,128]{2,1,0:T(8,128)}), f32[64,16,128]{2,1,0:T(8,128)S(1)}, u32[]{:S(2)}, u32[]{:S(2)}) async-start(f32[64,16,128]{2,1,0:T(8,128)} %bitcast.6), calls=%async_computation | async-start | bytes 1048576 | tf_op jit(solution)/shard_map/all_to_all | solution.py:492
  41.9 0.0 copy-start.2
  41.9 0.0 copy-start.8
  41.9 1.2 %copy-done.8 = s16[4,656,128]{2,1,0:T(8,128)(2,1)S(1)} copy-done((s16[4,656,128]{2,1,0:T(8,128)(2,1)S(1)}, s16[4,656,128]{2,1,0:T(8,128)(2,1)}, u32[]{:S(2)}) %copy-start.8) | copy-done | bytes 671768
  43.1 0.8 copy-done.10
  43.9 4.1 %left.2.refs_0_ = f32[1,128,5120]{2,1,0:T(8,128)} custom-call(s16[4,656,128]{2,1,0:T(8,128)(2,1)S(1)} %copy-done.8, f32[128,2560]{1,0:T(8,128)S(1)} %get-tuple-element.30.pm, s32[2,2,32,128]{3,2,1,0:T(8,128)S(1)} %pad_add_fusion.picks, bf16[256,256]{1,0:T(8,128)(2,1)S(1)} %copy-done.1, bf16[256,128]{1,0:T(8,128)(2,1)S(1)} %copy-done.10, ...), custom_call_target="tpu_custom_call" | custom-call | flops 1000 | bytes 1000 | tf_op jit(solution)/shard_map/left/pallas_call | solution.py:447
  48.0 6.8 %all-to-all-done.got = f32[64,16,128]{2,1,0:T(8,128)S(1)} async-done(((f32[64,16,128]{2,1,0:T(8,128)}), f32[64,16,128]{2,1,0:T(8,128)S(1)}, u32[]{:S(2)}, u32[]{:S(2)}) %all-to-all-start) | async-done | bytes 524320 | tf_op jit(solution)/shard_map/all_to_all | solution.py:492
  54.9 3.0 %owner.1 = s16[176,128]{1,0:T(8,128)(2,1)S(1)} custom-call(f32[64,16,128]{2,1,0:T(8,128)S(1)} %all-to-all-done.got, bf16[256,256]{1,0:T(8,128)(2,1)S(1)} %copy-done.5, bf16[256,128]{1,0:T(8,128)(2,1)S(1)} %copy-done.9), custom_call_target="tpu_custom_call" | custom-call | tf_op jit(solution)/shard_map/owner/pallas_call | solution.py:309
  57.8 0.2 broadcast_in_dim.3
  58.0 26.7 %all_to_all.10.got0.got1 = s16[32,176,128]{2,1,0:T(8,128)(2,1)S(1)} all-to-all(s16[32,176,128]{2,1,0:T(8,128)(2,1)S(1)} %broadcast_in_dim.3), channel_id=1, replica_groups=mesh['x'=4,'z'=4,'yh'=2,'yl'=2,'c'=2] {'x','z','yh'}, dimensions={0} | all-to-all | bytes 2883584 | tf_op jit(solution)/shard_map/all_to_all | solution.py:497
  84.7 2.2 %finish.1 = (f32[128,5120]{1,0:T(8,128)}, bf16[64,5120]{1,0:T(8,128)(2,1)S(1)}, bf16[64,5120]{1,0:T(8,128)(2,1)S(1)}) custom-call(s16[32,176,128]{2,1,0:T(8,128)(2,1)S(1)} %all_to_all.10.got0.got1, s16[32,176,128]{2,1,0:T(8,128)(2,1)S(1)} %all_to_all.10.got0.got1, bf16[128,5120]{1,0:T(8,128)(2,1)S(1)} %copy-done.2), custom_call_target="tpu_custom_call" | custom-call | flops 1000 | bytes 1000 | tf_op jit(solution)/shard_map/finish/pallas_call | solution.py:346
  86.9 3.2 %collective-permute-start.7 = (bf16[64,5120]{1,0:T(8,128)(2,1)S(1)}, bf16[64,5120]{1,0:T(8,128)(2,1)S(1)}, u32[]{:S(2)}, u32[]{:S(2)}) collective-permute-start(bf16[64,5120]{1,0:T(8,128)(2,1)S(1)} %get-tuple-element.36.refs_0_), channel_id=1, source_target_pairs={{0,1},{1,0},{2,3},{3,2},{4,5},{5,4},{6,7},{7,6},{8,9},{9,8},{10,11... | collective-permute-start | bytes 1966088 | tf_op jit(solution)/shard_map/ppermute | solution.py:506
  90.1 0.3 collective-permute-start.5
  90.4 0.7 collective-permute-start.6
  91.0 0.1 pad_add_fusion.2.rows
  91.1 5.0 %left.3 = f32[1,128,5120]{2,1,0:T(8,128)} custom-call(s16[4,656,128]{2,1,0:T(8,128)(2,1)} %collective-permute-done.4.q, f32[128,2560]{1,0:T(8,128)S(1)} %copy-done.4, s32[2,2,32,128]{3,2,1,0:T(8,128)S(1)} %pad_add_fusion.picks, bf16[256,256]{1,0:T(8,128)(2,1)S(1)} %copy-done.1, bf16[256,128]{1,0:T(8,128)(2,1)S(1)} %copy-done.11, ...), custom_call_target="tpu_custom_call", output_to_operand_aliasing={{}: (7, {})} | custom-call | flops 1000 | bytes 1000 | tf_op jit(solution)/shard_map/left/pallas_call | solution.py:447
  96.1 2.2 %gather.3.refs_2_ = bf16[512,5120]{1,0:T(8,128)(2,1)} custom-call(s32[4]{0:T(128)S(1)} %pad_add_fusion.2.rows, bf16[64,5120]{1,0:T(8,128)(2,1)S(1)} %get-tuple-element.36.refs_0_, bf16[64,5120]{1,0:T(8,128)(2,1)S(1)} %get-tuple-element.37.refs_1_, bf16[64,5120]{1,0:T(8,128)(2,1)S(1)} %collective-permute-done.7.refs_2_, ...), custom_call_target="tpu_custom_call" | custom-call | bytes 4194304 | tf_op jit(solution)/shard_map/gather/pallas_call | solution.py:377
  98.3 7.6 %collective-permute-done.5.refs_0_ = bf16[64,5120]{1,0:T(8,128)(2,1)S(1)} collective-permute-done((bf16[64,5120]{1,0:T(8,128)(2,1)S(1)}, bf16[64,5120]{1,0:T(8,128)(2,1)S(1)}, u32[]{:S(2)}, u32[]{:S(2)}) %collective-permute-start.5) | collective-permute-done | bytes 655392 | tf_op jit(solution)/shard_map/ppermute | solution.py:503
  105.9 1.2 %collective-permute-done.6.refs_1_ = bf16[64,5120]{1,0:T(8,128)(2,1)S(1)} collective-permute-done((bf16[64,5120]{1,0:T(8,128)(2,1)S(1)}, bf16[64,5120]{1,0:T(8,128)(2,1)S(1)}, u32[]{:S(2)}, u32[]{:S(2)}) %collective-permute-start.6) | collective-permute-done | bytes 655392 | tf_op jit(solution)/shard_map/ppermute | solution.py:504
  107.0 1.7 %collective-permute-start.10 = (bf16[64,5120]{1,0:T(8,128)(2,1)S(1)}, bf16[64,5120]{1,0:T(8,128)(2,1)S(1)}, u32[]{:S(2)}, u32[]{:S(2)}) collective-permute-start(bf16[64,5120]{1,0:T(8,128)(2,1)S(1)} %collective-permute-done.6.refs_1_), channel_id=1, source_target_pairs={{0,1},{1,0},{2,3},{3,2},{4,5},{5,4},{6,7},{7,6},{8,9},{9,8},{10,11... | collective-permute-start | bytes 1966088 | tf_op jit(solution)/shard_map/ppermute | solution.py:510
  108.7 0.0 collective-permute-start.9
  108.7 1.7 %gather.4.refs_2_ = bf16[512,5120]{1,0:T(8,128)(2,1)} custom-call(s32[2]{0:T(128)S(1)} %fusion.8.rows, bf16[64,5120]{1,0:T(8,128)(2,1)S(1)} %collective-permute-done.5.refs_0_, bf16[64,5120]{1,0:T(8,128)(2,1)S(1)} %collective-permute-done.6.refs_1_, bf16[512,5120]{1,0:T(8,128)(2,1)} %gather.3.refs_2_), custom_call_target="tpu_custom_call", output_to_operand_aliasing={{}: (3, {})} | custom-call | bytes 4194304 | tf_op jit(solution)/shard_map/gather/pallas_call | solution.py:377
  110.4 0.0 collective-permute-done.10.refs_1_
  110.4 0.9 collective-permute-done.9.refs_0_
  111.4 1.7 %gather.5 = bf16[512,5120]{1,0:T(8,128)(2,1)} custom-call(s32[2]{0:T(128)S(1)} %fusion.9.rows, bf16[64,5120]{1,0:T(8,128)(2,1)S(1)} %collective-permute-done.9.refs_0_, bf16[64,5120]{1,0:T(8,128)(2,1)S(1)} %collective-permute-done.10.refs_1_, bf16[512,5120]{1,0:T(8,128)(2,1)} %gather.4.refs_2_), custom_call_target="tpu_custom_call", output_to_operand_aliasing={{}: (3, {})} | custom-call | bytes 4194304 | tf_op jit(solution)/shard_map/gather/pallas_call | solution.py:377
  (30 shorter events, 0.1 us)
Async XLA Ops:
  0.6 7.3 %copy-start.14 = (bf16[1024,5120]{1,0:T(8,128)(2,1)S(1)}, bf16[1024,5120]{1,0:T(8,128)(2,1)}, u32[]{:S(2)}) copy-start(bf16[1024,5120]{1,0:T(8,128)(2,1)} %param.12) | copy-start | bytes 31457284
  6.4 3.2 %copy-start.13 = (s32[1,2,80,32]{2,3,1,0:T(8,128)S(1)}, s32[1,2,80,32]{2,3,1,0:T(8,128)}, u32[]{:S(2)}) copy-start(s32[1,2,80,32]{2,3,1,0:T(8,128)} %param.14) | copy-start | bytes 61444
  6.4 6.2 %collective-permute-start.2 = (f32[256,2560]{1,0:T(8,128)S(1)}, f32[256,2560]{1,0:T(8,128)S(1)}, u32[]{:S(2)}, u32[]{:S(2)}) collective-permute-start(f32[256,2560]{1,0:T(8,128)S(1)} %fusion), channel_id=1, source_target_pairs={{0,1},{1,0},{2,3},{3,2},{4,5},{5,4},{6,7},{7,6},{8,9},{9,8},{10,11... | collective-permute-start | bytes 7864328 | tf_op jit(solution)/shard_map/ppermute | solution.py:484
  9.5 11.7 %collective-permute-start = (f32[256,2560]{1,0:T(8,128)S(1)}, f32[256,2560]{1,0:T(8,128)S(1)}, u32[]{:S(2)}, u32[]{:S(2)}) collective-permute-start(f32[256,2560]{1,0:T(8,128)S(1)} %fusion.4), channel_id=1, source_target_pairs={{0,1},{1,0},{2,3},{3,2},{4,5},{5,4},{6,7},{7,6},{8,9},{9,8},{10,11... | collective-permute-start | bytes 7864328 | tf_op jit(solution)/shard_map/ppermute | solution.py:484
  9.6 6.9 %collective-permute-start.1 = (s32[2,32,128]{2,1,0:T(8,128)S(1)}, s32[2,32,128]{2,1,0:T(8,128)S(1)}, u32[]{:S(2)}, u32[]{:S(2)}) collective-permute-start(s32[2,32,128]{2,1,0:T(8,128)S(1)} %get-tuple-element.54), channel_id=1, source_target_pairs={{0,2},{2,0},{4,6},{6,4},{1,3},{3,1},{5,7},{7,5},{8,10},{10,8},{12,... | collective-permute-start | bytes 98312 | tf_op jit(solution)/shard_map/ppermute | solution.py:478
  13.6 3.0 %copy-start = (f32[1,128,5120]{2,1,0:T(8,128)S(1)}, f32[1,128,5120]{2,1,0:T(8,128)}, u32[]{:S(2)}) copy-start(f32[1,128,5120]{2,1,0:T(8,128)} %mom.3) | copy-start | bytes 7864324
  13.6 3.0 %copy-start.1 = (bf16[256,256]{1,0:T(8,128)(2,1)S(1)}, bf16[256,256]{1,0:T(8,128)(2,1)}, u32[]{:S(2)}) copy-start(bf16[256,256]{1,0:T(8,128)(2,1)} %constant.30.clone.rt) | copy-start | bytes 393220
  13.6 2.9 %copy-start.6 = (bf16[512,256]{1,0:T(8,128)(2,1)S(1)}, bf16[512,256]{1,0:T(8,128)(2,1)}, u32[]{:S(2)}) copy-start(bf16[512,256]{1,0:T(8,128)(2,1)} %constant.32.clone.lt) | copy-start | bytes 786436
  13.6 2.9 %copy-start.12 = (s32[2,8,128]{2,1,0:T(8,128)S(1)}, s32[2,8,128]{2,1,0:T(8,128)}, u32[]{:S(2)}) copy-start(s32[2,8,128]{2,1,0:T(8,128)} %constant.35.clone.tab) | copy-start | bytes 24580
  13.6 15.9 %collective-permute-start.3 = (s16[4,656,128]{2,1,0:T(8,128)(2,1)S(1)}, s16[4,656,128]{2,1,0:T(8,128)(2,1)S(1)}, u32[]{:S(2)}, u32[]{:S(2)}) collective-permute-start(s16[4,656,128]{2,1,0:T(8,128)(2,1)S(1)} %code.1), channel_id=1, source_target_pairs={{0,2},{2,0},{4,6},{6,4},{1,3},{3,1},{5,7},{7,5},{8,10},{10,8},{12,... | collective-permute-start | bytes 2015240 | tf_op jit(solution)/shard_map/ppermute | solution.py:487
  21.2 20.7 %copy-start.5 = (bf16[256,256]{1,0:T(8,128)(2,1)S(1)}, bf16[256,256]{1,0:T(8,128)(2,1)}, u32[]{:S(2)}) copy-start(bf16[256,256]{1,0:T(8,128)(2,1)} %constant.31.clone.irt.rt) | copy-start | bytes 393220
  21.2 20.7 %copy-start.9 = (bf16[256,128]{1,0:T(8,128)(2,1)S(1)}, bf16[256,128]{1,0:T(8,128)(2,1)}, u32[]{:S(2)}) copy-start(bf16[256,128]{1,0:T(8,128)(2,1)} %constant.34.clone.ilt.lt) | copy-start | bytes 196612
  26.5 1.1 copy-start.3
  27.6 30.3 %collective-permute-start.4 = (s16[4,656,128]{2,1,0:T(8,128)(2,1)}, s16[4,656,128]{2,1,0:T(8,128)(2,1)}, u32[]{:S(2)}, u32[]{:S(2)}) collective-permute-start(s16[4,656,128]{2,1,0:T(8,128)(2,1)} %get-tuple-element.32), channel_id=1, source_target_pairs={{0,2},{2,0},{4,6},{6,4},{1,3},{3,1},{5,7},{7,5},{8,10},{10,8},{12,... | collective-permute-start | bytes 2015240 | tf_op jit(solution)/shard_map/ppermute | solution.py:490
  29.5 0.8 copy-start.7
  30.4 24.5 %all-to-all-start = ((f32[64,16,128]{2,1,0:T(8,128)}), f32[64,16,128]{2,1,0:T(8,128)S(1)}, u32[]{:S(2)}, u32[]{:S(2)}) async-start(f32[64,16,128]{2,1,0:T(8,128)} %bitcast.6), calls=%async_computation | async-start | bytes 1048576 | tf_op jit(solution)/shard_map/all_to_all | solution.py:492
  41.9 42.9 %copy-start.2 = (bf16[128,5120]{1,0:T(8,128)(2,1)S(1)}, bf16[128,5120]{1,0:T(8,128)(2,1)}, u32[]{:S(2)}) copy-start(bf16[128,5120]{1,0:T(8,128)(2,1)} %par.1) | copy-start | bytes 3932164
  41.9 1.2 %copy-start.8 = (s16[4,656,128]{2,1,0:T(8,128)(2,1)S(1)}, s16[4,656,128]{2,1,0:T(8,128)(2,1)}, u32[]{:S(2)}) copy-start(s16[4,656,128]{2,1,0:T(8,128)(2,1)} %copy-done.7) | copy-start | bytes 2015236
  43.1 0.8 copy-start.10
  48.0 43.1 %copy-start.4 = (f32[128,2560]{1,0:T(8,128)S(1)}, f32[128,2560]{1,0:T(8,128)}, u32[]{:S(2)}) copy-start(f32[128,2560]{1,0:T(8,128)} %copy-done.3) | copy-start | bytes 3932164
  54.9 36.3 %copy-start.11 = (bf16[256,128]{1,0:T(8,128)(2,1)S(1)}, bf16[256,128]{1,0:T(8,128)(2,1)}, u32[]{:S(2)}) copy-start(bf16[256,128]{1,0:T(8,128)(2,1)} %constant.33.clone.lt) | copy-start | bytes 196612
  86.9 9.2 %collective-permute-start.7 = (bf16[64,5120]{1,0:T(8,128)(2,1)S(1)}, bf16[64,5120]{1,0:T(8,128)(2,1)S(1)}, u32[]{:S(2)}, u32[]{:S(2)}) collective-permute-start(bf16[64,5120]{1,0:T(8,128)(2,1)S(1)} %get-tuple-element.36.refs_0_), channel_id=1, source_target_pairs={{0,1},{1,0},{2,3},{3,2},{4,5},{5,4},{6,7},{7,6},{8,9},{9,8},{10,11... | collective-permute-start | bytes 1966088 | tf_op jit(solution)/shard_map/ppermute | solution.py:506
  90.1 6.1 %collective-permute-start.8 = (bf16[64,5120]{1,0:T(8,128)(2,1)S(1)}, bf16[64,5120]{1,0:T(8,128)(2,1)S(1)}, u32[]{:S(2)}, u32[]{:S(2)}) collective-permute-start(bf16[64,5120]{1,0:T(8,128)(2,1)S(1)} %get-tuple-element.37.refs_1_), channel_id=1, source_target_pairs={{0,1},{1,0},{2,3},{3,2},{4,5},{5,4},{6,7},{7,6},{8,9},{9,8},{10,11... | collective-permute-start | bytes 1966088 | tf_op jit(solution)/shard_map/ppermute | solution.py:506
  90.1 15.8 %collective-permute-start.5 = (bf16[64,5120]{1,0:T(8,128)(2,1)S(1)}, bf16[64,5120]{1,0:T(8,128)(2,1)S(1)}, u32[]{:S(2)}, u32[]{:S(2)}) collective-permute-start(bf16[64,5120]{1,0:T(8,128)(2,1)S(1)} %get-tuple-element.36.refs_0_), channel_id=1, source_target_pairs={{0,2},{2,0},{4,6},{6,4},{1,3},{3,1},{5,7},{7,5},{8,10},{10,8},{12,... | collective-permute-start | bytes 1966088 | tf_op jit(solution)/shard_map/ppermute | solution.py:503
  90.4 16.7 %collective-permute-start.6 = (bf16[64,5120]{1,0:T(8,128)(2,1)S(1)}, bf16[64,5120]{1,0:T(8,128)(2,1)S(1)}, u32[]{:S(2)}, u32[]{:S(2)}) collective-permute-start(bf16[64,5120]{1,0:T(8,128)(2,1)S(1)} %get-tuple-element.37.refs_1_), channel_id=1, source_target_pairs={{0,6},{2,4},{4,2},{6,0},{1,7},{3,5},{5,3},{7,1},{8,14},{10,12},{12... | collective-permute-start | bytes 1966088 | tf_op jit(solution)/shard_map/ppermute | solution.py:504
  107.0 3.4 %collective-permute-start.10 = (bf16[64,5120]{1,0:T(8,128)(2,1)S(1)}, bf16[64,5120]{1,0:T(8,128)(2,1)S(1)}, u32[]{:S(2)}, u32[]{:S(2)}) collective-permute-start(bf16[64,5120]{1,0:T(8,128)(2,1)S(1)} %collective-permute-done.6.refs_1_), channel_id=1, source_target_pairs={{0,1},{1,0},{2,3},{3,2},{4,5},{5,4},{6,7},{7,6},{8,9},{9,8},{10,11... | collective-permute-start | bytes 1966088 | tf_op jit(solution)/shard_map/ppermute | solution.py:510
  108.7 2.7 %collective-permute-start.9 = (bf16[64,5120]{1,0:T(8,128)(2,1)S(1)}, bf16[64,5120]{1,0:T(8,128)(2,1)S(1)}, u32[]{:S(2)}, u32[]{:S(2)}) collective-permute-start(bf16[64,5120]{1,0:T(8,128)(2,1)S(1)} %collective-permute-done.5.refs_0_), channel_id=1, source_target_pairs={{0,1},{1,0},{2,3},{3,2},{4,5},{5,4},{6,7},{7,6},{8,9},{9,8},{10,11... | collective-permute-start | bytes 1966088 | tf_op jit(solution)/shard_map/ppermute | solution.py:510
